TPU v7x, 256 devices: a whole 4x4x8 slice. The times are simulated.
256 devices in a mesh: sub: 256 (over y, z, x, core).
Axes of the slice: x: 4, y: 4, z: 8, core: 2. Of those that a mesh axis runs over, the one named last changes fastest.
Arguments:
- jumps: float32 [256, 1536, 128], P('sub'), may hold values from -6 to 6
- schur: bfloat16 [256, 1536, 1536], P('sub'), as said below
- coupling: float32 [256, 24, 1536], P('sub'), may hold values from -0.4375 to 0.4375
- coarse_inverse: float32 [768, 768], replicated, as said below
- scaling: float32 [256, 1536], P('sub'), as said below
- glued: int32 [256, 6], P('sub'), may hold values from 0 to 1, as said below
- matching: int32 [256, 6, 256], P('sub'), may hold values from 0 to 255, as said below
- corners: int32 [256, 24], P('sub'), may hold values from 0 to 767, all different within a row
Outputs:
- multipliers: float32 [256, 1536, 128], P('sub')
- residual: float32 [256, 1536, 128], P('sub')
Inputs may be any that keep to these rules, and one draw needn't show every extreme that they name: Subdomain s sits at x = s % 4, y = (s // 4) % 4, z = s // 16; 1 where a face is glued to its neighbour in the grid, 0 where it is not or where the grid has no neighbour; both sides of a face agree. `matching`: each row is a permutation of 0 to 255; the row of face 2d + 1 of the upper neighbour is the inverse of the row of face 2d. `corners`: each row names 24 different coarse dofs, and every coarse dof is named by some row. `schur`: each block is symmetric positive definite. `coarse_inverse`: symmetric positive definite. `scaling`: positive, and equal at the two dofs of every glued match.
All inputs are finite; a program needn't handle non-finite values.
Results may differ from a plain program's by a relative error of at most 0.013.
Values sent between devices are 32-bit elements; how exact they have to be, the bound alone decides.
No kernel may reach another device: no remote copies, remote signals or barrier semaphores. Data moves between devices by JAX's collectives and lax.ppermute only.
A program may use at most 128 MiB of HBM per device.

v0:
```python
import jax
import jax.numpy as jnp
from jax import lax
from jax.sharding import PartitionSpec as P

ITERS = 5
GX = 4
GY = 4


def passed_along(block, axis, distance):
    devices = range(lax.axis_size(axis))
    route = [(i - distance, i) for i in devices if i - distance in devices]
    return lax.ppermute(block, axis, route)


def shards(jumps, schur, coupling, coarse_inverse, scaling, glued, matching, corners):
    highest = lax.Precision.HIGHEST
    face_count = matching.shape[1]
    face_dofs = matching.shape[2]
    load_count = jumps.shape[2]
    coarse_count = coarse_inverse.shape[0]
    schur_block = schur[0]
    couple = coupling[0]
    weights = scaling[0][:, None]
    face_links = matching[0]
    corner_ids = corners[0]
    corner_count = corner_ids.shape[0]
    glue_mask = jnp.repeat(glued[0].astype(jnp.float32), face_dofs)[:, None]
    face_sign = jnp.repeat(jnp.array([1.0, -1.0, 1.0, -1.0, 1.0, -1.0], jnp.float32), face_dofs)[
        :, None
    ]
    strides = (1, GX, GX * GY)
    sinv_rows = coarse_inverse[corner_ids]

    def neighbour(face_rows, offset):
        return passed_along(face_rows, "sub", offset)

    def assemble(values):
        blocks = values.reshape(face_count, face_dofs, load_count)
        partner_rows = []
        for direction in range(3):
            from_upper = neighbour(blocks[2 * direction + 1], -strides[direction])
            from_lower = neighbour(blocks[2 * direction], strides[direction])
            partner_rows.append(from_upper[face_links[2 * direction]])
            partner_rows.append(from_lower[face_links[2 * direction + 1]])
        return glue_mask * (values + jnp.concatenate(partner_rows, 0))

    selector = (
        lax.broadcasted_iota(jnp.int32, (coarse_count, corner_count), 0) == corner_ids[None, :]
    ).astype(jnp.float32)

    def energy_sum(left, right):
        return lax.psum(0.5 * jnp.sum(left * right, axis=0), "sub")

    gap = assemble(face_sign * jumps[0])
    multipliers = jnp.zeros_like(gap)
    residual = gap
    precond = weights * residual
    energy_now = energy_sum(residual, precond)
    direction = precond
    for iteration in range(ITERS):
        signed = face_sign * direction
        local_part = jnp.dot(
            schur_block, signed.astype(jnp.bfloat16), preferred_element_type=jnp.float32
        )
        corner_terms = jnp.dot(
            couple, signed, precision=highest, preferred_element_type=jnp.float32
        )
        partial_sum = jnp.dot(
            selector, corner_terms, precision=highest, preferred_element_type=jnp.float32
        )
        summed = lax.psum(partial_sum, "sub")
        nearby = jnp.dot(sinv_rows, summed, precision=highest, preferred_element_type=jnp.float32)
        lifted = lax.dot_general(
            couple,
            nearby,
            (((0,), (0,)), ((), ())),
            precision=highest,
            preferred_element_type=jnp.float32,
        )
        signed, local_image = (signed, local_part + lifted)
        product = assemble(face_sign * local_image)
        curvature_sum = lax.psum(0.5 * jnp.sum(direction * product, axis=0), "sub")
        step_size = energy_now / curvature_sum
        multipliers = multipliers + step_size * direction
        residual = residual - step_size * product
        if iteration + 1 < ITERS:
            precond = weights * residual
            energy_next = energy_sum(residual, precond)
            direction = precond + energy_next / energy_now * direction
            energy_now = energy_next
    return (multipliers[None], residual[None])


def solution(mesh):
    return jax.shard_map(
        shards,
        mesh=mesh,
        in_specs=(
            P("sub", None, None),
            P("sub", None, None),
            P("sub", None, None),
            P(),
            P("sub", None),
            P("sub", None),
            P("sub", None, None),
            P("sub", None),
        ),
        out_specs=(P("sub", None, None), P("sub", None, None)),
        check_vma=False,
    )
```

profile of v0, /device:TPU:24, one launch (start us, length us, event | category | flops | bytes accessed | tf_op | source)
XLA Modules:
  0.0 2319.4 jit_solution(13778186618183654097)
XLA Ops:
  10.7 5.2 collective-permute-start.5
  15.8 5.1 collective-permute-start.4
  21.0 6.8 collective-permute-start.2
  29.8 7.9 collective-permute-start
  57.2 3.4 fusion.31
  60.7 6.1 fusion.8
  69.8 245.4 %all-reduce.7.cloned.1.call-done = f32[768,128]{1,0:T(8,128)} async-done(((f32[768,128]{1,0:T(8,128)}), f32[768,128]{1,0:T(8,128)}) %all-reduce.7.cloned.1.call-update) | async-done | bytes 393232 | tf_op jit(solution)/shard_map/psum | solution.py:73
  328.4 6.4 collective-permute-start.10
  334.8 3.8 collective-permute-start.9
  338.6 6.6 collective-permute-start.8
  347.1 7.9 collective-permute-start.6
  384.4 71.4 %all-reduce = (f32[128]{0:T(128)S(1)}, f32[128]{0:T(128)S(1)}) all-reduce(f32[128]{0:T(128)S(1)} %get-tuple-element.64, f32[128]{0:T(128)S(1)} %get-tuple-element.63), channel_id=1, replica_groups=mesh['sub'=256] {'sub'}, use_global_device_ids=true, to_apply=%region_1.0 | all-reduce | flops 256 | bytes 2048 | tf_op jit(solution)/shard_map/psum | solution.py:54
  458.3 74.9 %psum.108 = f32[128]{0:T(128)S(1)} all-reduce(f32[128]{0:T(128)S(1)} %broadcast_multiply_fusion.7), channel_id=1, replica_groups=mesh['sub'=256] {'sub'}, use_global_device_ids=true, to_apply=%region_6.0 | all-reduce | flops 128 | bytes 1024 | tf_op jit(solution)/shard_map/psum | solution.py:54
  537.2 4.9 fusion.6
  542.1 238.6 %all-reduce.9.cloned.1.call-done = f32[768,128]{1,0:T(8,128)} async-done(((f32[768,128]{1,0:T(8,128)}), f32[768,128]{1,0:T(8,128)}) %all-reduce.9.cloned.1.call-update) | async-done | bytes 393232 | tf_op jit(solution)/shard_map/psum | solution.py:73
  788.1 6.4 collective-permute-start.16
  794.5 3.8 collective-permute-start.15
  798.3 6.6 collective-permute-start.14
  807.5 7.8 collective-permute-start.12
  845.6 71.4 %psum.110 = f32[128]{0:T(128)S(1)} all-reduce(f32[128]{0:T(128)S(1)} %broadcast_multiply_fusion.6), channel_id=1, replica_groups=mesh['sub'=256] {'sub'}, use_global_device_ids=true, to_apply=%region_9.0 | all-reduce | flops 128 | bytes 1024 | tf_op jit(solution)/shard_map/psum | solution.py:84
  917.6 2.7 fusion.28
  920.4 74.7 %psum.111 = f32[128]{0:T(128)S(1)} all-reduce(f32[128]{0:T(128)S(1)} %broadcast_multiply_fusion.5), channel_id=1, replica_groups=mesh['sub'=256] {'sub'}, use_global_device_ids=true, to_apply=%region_11.0 | all-reduce | flops 128 | bytes 1024 | tf_op jit(solution)/shard_map/psum | solution.py:54
  999.8 5.2 fusion.4
  1005.0 238.4 %all-reduce.11.cloned.1.call-done = f32[768,128]{1,0:T(8,128)} async-done(((f32[768,128]{1,0:T(8,128)}), f32[768,128]{1,0:T(8,128)}) %all-reduce.11.cloned.1.call-update) | async-done | bytes 393232 | tf_op jit(solution)/shard_map/psum | solution.py:73
  1250.9 6.4 collective-permute-start.22
  1257.3 3.8 collective-permute-start.21
  1261.1 6.6 collective-permute-start.20
  1270.3 8.1 collective-permute-start.18
  1308.8 71.4 %psum.113 = f32[128]{0:T(128)S(1)} all-reduce(f32[128]{0:T(128)S(1)} %broadcast_multiply_fusion.4), channel_id=1, replica_groups=mesh['sub'=256] {'sub'}, use_global_device_ids=true, to_apply=%region_14.0 | all-reduce | flops 128 | bytes 1024 | tf_op jit(solution)/shard_map/psum | solution.py:84
  1380.8 2.7 fusion.29
  1383.5 74.7 %psum.114 = f32[128]{0:T(128)S(1)} all-reduce(f32[128]{0:T(128)S(1)} %broadcast_multiply_fusion.3), channel_id=1, replica_groups=mesh['sub'=256] {'sub'}, use_global_device_ids=true, to_apply=%region_16.0 | all-reduce | flops 128 | bytes 1024 | tf_op jit(solution)/shard_map/psum | solution.py:54
  1463.3 5.1 fusion.2
  1468.4 238.4 %all-reduce.13.cloned.1.call-done = f32[768,128]{1,0:T(8,128)} async-done(((f32[768,128]{1,0:T(8,128)}), f32[768,128]{1,0:T(8,128)}) %all-reduce.13.cloned.1.call-update) | async-done | bytes 393232 | tf_op jit(solution)/shard_map/psum | solution.py:73
  1714.2 6.4 collective-permute-start.28
  1720.7 3.8 collective-permute-start.27
  1724.4 6.6 collective-permute-start.26
  1733.6 7.8 collective-permute-start.24
  1772.0 71.4 %psum.116 = f32[128]{0:T(128)S(1)} all-reduce(f32[128]{0:T(128)S(1)} %broadcast_multiply_fusion.2), channel_id=1, replica_groups=mesh['sub'=256] {'sub'}, use_global_device_ids=true, to_apply=%region_19.0 | all-reduce | flops 128 | bytes 1024 | tf_op jit(solution)/shard_map/psum | solution.py:84
  1844.0 2.7 fusion.30
  1846.7 75.0 %psum.117 = f32[128]{0:T(128)S(1)} all-reduce(f32[128]{0:T(128)S(1)} %broadcast_multiply_fusion.1), channel_id=1, replica_groups=mesh['sub'=256] {'sub'}, use_global_device_ids=true, to_apply=%region_21.0 | all-reduce | flops 128 | bytes 1024 | tf_op jit(solution)/shard_map/psum | solution.py:54
  1926.7 5.1 fusion
  1931.8 238.4 %all-reduce.15.cloned.1.call-done = f32[768,128]{1,0:T(8,128)} async-done(((f32[768,128]{1,0:T(8,128)}), f32[768,128]{1,0:T(8,128)}) %all-reduce.15.cloned.1.call-update) | async-done | bytes 393232 | tf_op jit(solution)/shard_map/psum | solution.py:73
  2177.7 6.4 collective-permute-start.34
  2184.1 3.8 collective-permute-start.33
  2187.9 6.6 collective-permute-start.32
  2196.4 7.9 collective-permute-start.30
  2232.3 71.4 %psum.119 = f32[128]{0:T(128)S(1)} all-reduce(f32[128]{0:T(128)S(1)} %broadcast_multiply_fusion), channel_id=1, replica_groups=mesh['sub'=256] {'sub'}, use_global_device_ids=true, to_apply=%region_24.0 | all-reduce | flops 128 | bytes 1024 | tf_op jit(solution)/shard_map/psum | solution.py:84
  2303.7 4.2 subtract_bitcast_fusion
  (351 shorter events, 257.9 us)
Async XLA Ops:
  7.2 308.0 %all-reduce.7.cloned.1.call-start = ((), (), s32[]{:S(2)}) async-start(), calls=%async_computation | async-start | bytes 786432 | tf_op jit(solution)/shard_map/psum | solution.py:73
  10.7 38.0 %collective-permute-start.5 = (f32[256,128]{0,1:T(8,128)}, f32[256,128]{0,1:T(8,128)}, u32[]{:S(2)}, u32[]{:S(2)}) collective-permute-start(f32[256,128]{0,1:T(8,128)} %get-tuple-element.49), channel_id=1, source_target_pairs={{0,16},{1,17},{2,18},{3,19},{4,20},{5,21},{6,22},{7,23},{8,24},{9,... | collective-permute-start | bytes 393224 | tf_op jit(solution)/shard_map/ppermute | solution.py:14
  15.8 35.2 %collective-permute-start.4 = (f32[256,128]{0,1:T(8,128)}, f32[256,128]{0,1:T(8,128)}, u32[]{:S(2)}, u32[]{:S(2)}) collective-permute-start(f32[256,128]{0,1:T(8,128)} %get-tuple-element.50), channel_id=1, source_target_pairs={{16,0},{17,1},{18,2},{19,3},{20,4},{21,5},{22,6},{23,7},{24,8},{25... | collective-permute-start | bytes 393224 | tf_op jit(solution)/shard_map/ppermute | solution.py:14
  21.0 17.5 collective-permute-start.2
  27.8 15.1 collective-permute-start.1
  29.8 15.7 collective-permute-start
  38.5 14.9 collective-permute-start.3
  67.9 712.7 %all-reduce.9.cloned.1.call-start = ((), (), s32[]{:S(2)}) async-start(), calls=%async_computation.1 | async-start | bytes 786432 | tf_op jit(solution)/shard_map/psum | solution.py:73
  69.8 245.5 %copy-start.19 = (f32[1536,128]{0,1:T(8,128)}, f32[1536,128]{0,1:T(8,128)S(1)}, u32[]{:S(2)}) copy-start(f32[1536,128]{0,1:T(8,128)S(1)} %constant_dynamic-update-slice_fusion.4) | copy-start | bytes 2359300
  318.5 54.8 %copy-start.7 = (f32[1536,128]{0,1:T(8,128)}, f32[1536,128]{0,1:T(8,128)S(1)}, u32[]{:S(2)}) copy-start(f32[1536,128]{0,1:T(8,128)S(1)} %fusion.15) | copy-start | bytes 2359300
  319.5 27.7 %collective-permute-start.11 = (f32[256,128]{0,1:T(8,128)}, f32[256,128]{0,1:T(8,128)}, u32[]{:S(2)}, u32[]{:S(2)}) collective-permute-start(f32[256,128]{0,1:T(8,128)} %get-tuple-element.43), channel_id=1, source_target_pairs={{0,16},{1,17},{2,18},{3,19},{4,20},{5,21},{6,22},{7,23},{8,24},{9,... | collective-permute-start | bytes 393224 | tf_op jit(solution)/shard_map/ppermute | solution.py:14
  328.4 34.6 %collective-permute-start.10 = (f32[256,128]{0,1:T(8,128)}, f32[256,128]{0,1:T(8,128)}, u32[]{:S(2)}, u32[]{:S(2)}) collective-permute-start(f32[256,128]{0,1:T(8,128)} %get-tuple-element.44), channel_id=1, source_target_pairs={{16,0},{17,1},{18,2},{19,3},{20,4},{21,5},{22,6},{23,7},{24,8},{25... | collective-permute-start | bytes 393224 | tf_op jit(solution)/shard_map/ppermute | solution.py:14
  334.8 32.1 %collective-permute-start.9 = (f32[256,128]{0,1:T(8,128)}, f32[256,128]{0,1:T(8,128)}, u32[]{:S(2)}, u32[]{:S(2)}) collective-permute-start(f32[256,128]{0,1:T(8,128)} %get-tuple-element.45), channel_id=1, source_target_pairs={{0,4},{1,5},{2,6},{3,7},{4,8},{5,9},{6,10},{7,11},{8,12},{9,13},{1... | collective-permute-start | bytes 393224 | tf_op jit(solution)/shard_map/ppermute | solution.py:14
  338.6 32.4 %collective-permute-start.8 = (f32[256,128]{0,1:T(8,128)}, f32[256,128]{0,1:T(8,128)}, u32[]{:S(2)}, u32[]{:S(2)}) collective-permute-start(f32[256,128]{0,1:T(8,128)} %get-tuple-element.46), channel_id=1, source_target_pairs={{4,0},{5,1},{6,2},{7,3},{8,4},{9,5},{10,6},{11,7},{12,8},{13,9},{1... | collective-permute-start | bytes 393224 | tf_op jit(solution)/shard_map/ppermute | solution.py:14
  345.2 29.8 %collective-permute-start.7 = (f32[256,128]{0,1:T(8,128)}, f32[256,128]{0,1:T(8,128)}, u32[]{:S(2)}, u32[]{:S(2)}) collective-permute-start(f32[256,128]{0,1:T(8,128)} %get-tuple-element.47), channel_id=1, source_target_pairs={{0,1},{1,2},{2,3},{3,4},{4,5},{5,6},{6,7},{7,8},{8,9},{9,10},{10,1... | collective-permute-start | bytes 393224 | tf_op jit(solution)/shard_map/ppermute | solution.py:14
  347.1 29.7 %collective-permute-start.6 = (f32[256,128]{0,1:T(8,128)}, f32[256,128]{0,1:T(8,128)}, u32[]{:S(2)}, u32[]{:S(2)}) collective-permute-start(f32[256,128]{0,1:T(8,128)} %get-tuple-element.48), channel_id=1, source_target_pairs={{1,0},{2,1},{3,2},{4,3},{5,4},{6,5},{7,6},{8,7},{9,8},{10,9},{11,1... | collective-permute-start | bytes 393224 | tf_op jit(solution)/shard_map/ppermute | solution.py:14
  384.4 148.8 %copy-start.6 = (f32[1536,128]{0,1:T(8,128)}, f32[1536,128]{0,1:T(8,128)S(1)}, u32[]{:S(2)}) copy-start(f32[1536,128]{0,1:T(8,128)S(1)} %get-tuple-element.18) | copy-start | bytes 2359300
  537.1 706.2 %all-reduce.11.cloned.1.call-start = ((), (), s32[]{:S(2)}) async-start(), calls=%async_computation.2 | async-start | bytes 786432 | tf_op jit(solution)/shard_map/psum | solution.py:73
  785.7 21.2 collective-permute-start.17
  788.1 31.3 %collective-permute-start.16 = (f32[256,128]{0,1:T(8,128)}, f32[256,128]{0,1:T(8,128)}, u32[]{:S(2)}, u32[]{:S(2)}) collective-permute-start(f32[256,128]{0,1:T(8,128)} %get-tuple-element.38), channel_id=1, source_target_pairs={{16,0},{17,1},{18,2},{19,3},{20,4},{21,5},{22,6},{23,7},{24,8},{25... | collective-permute-start | bytes 393224 | tf_op jit(solution)/shard_map/ppermute | solution.py:14
  794.5 28.9 %collective-permute-start.15 = (f32[256,128]{0,1:T(8,128)}, f32[256,128]{0,1:T(8,128)}, u32[]{:S(2)}, u32[]{:S(2)}) collective-permute-start(f32[256,128]{0,1:T(8,128)} %get-tuple-element.39), channel_id=1, source_target_pairs={{0,4},{1,5},{2,6},{3,7},{4,8},{5,9},{6,10},{7,11},{8,12},{9,13},{1... | collective-permute-start | bytes 393224 | tf_op jit(solution)/shard_map/ppermute | solution.py:14
  798.3 29.1 %collective-permute-start.14 = (f32[256,128]{0,1:T(8,128)}, f32[256,128]{0,1:T(8,128)}, u32[]{:S(2)}, u32[]{:S(2)}) collective-permute-start(f32[256,128]{0,1:T(8,128)} %get-tuple-element.40), channel_id=1, source_target_pairs={{4,0},{5,1},{6,2},{7,3},{8,4},{9,5},{10,6},{11,7},{12,8},{13,9},{1... | collective-permute-start | bytes 393224 | tf_op jit(solution)/shard_map/ppermute | solution.py:14
  804.9 26.5 %collective-permute-start.13 = (f32[256,128]{0,1:T(8,128)}, f32[256,128]{0,1:T(8,128)}, u32[]{:S(2)}, u32[]{:S(2)}) collective-permute-start(f32[256,128]{0,1:T(8,128)} %get-tuple-element.41), channel_id=1, source_target_pairs={{0,1},{1,2},{2,3},{3,4},{4,5},{5,6},{6,7},{7,8},{8,9},{9,10},{10,1... | collective-permute-start | bytes 393224 | tf_op jit(solution)/shard_map/ppermute | solution.py:14
  807.5 27.9 %collective-permute-start.12 = (f32[256,128]{0,1:T(8,128)}, f32[256,128]{0,1:T(8,128)}, u32[]{:S(2)}, u32[]{:S(2)}) collective-permute-start(f32[256,128]{0,1:T(8,128)} %get-tuple-element.42), channel_id=1, source_target_pairs={{1,0},{2,1},{3,2},{4,3},{5,4},{6,5},{7,6},{8,7},{9,8},{10,9},{11,1... | collective-permute-start | bytes 393224 | tf_op jit(solution)/shard_map/ppermute | solution.py:14
  917.6 78.1 %copy-start.27 = (f32[128]{0:T(128)}, f32[128]{0:T(128)S(1)}, u32[]{:S(2)}) copy-start(f32[128]{0:T(128)S(1)} %div.29) | copy-start | bytes 1540
  999.7 707.0 %all-reduce.13.cloned.1.call-start = ((), (), s32[]{:S(2)}) async-start(), calls=%async_computation.3 | async-start | bytes 786432 | tf_op jit(solution)/shard_map/psum | solution.py:73
  1248.4 21.2 collective-permute-start.23
  1250.9 31.5 %collective-permute-start.22 = (f32[256,128]{0,1:T(8,128)}, f32[256,128]{0,1:T(8,128)}, u32[]{:S(2)}, u32[]{:S(2)}) collective-permute-start(f32[256,128]{0,1:T(8,128)} %get-tuple-element.32), channel_id=1, source_target_pairs={{16,0},{17,1},{18,2},{19,3},{20,4},{21,5},{22,6},{23,7},{24,8},{25... | collective-permute-start | bytes 393224 | tf_op jit(solution)/shard_map/ppermute | solution.py:14
  1257.3 29.1 %collective-permute-start.21 = (f32[256,128]{0,1:T(8,128)}, f32[256,128]{0,1:T(8,128)}, u32[]{:S(2)}, u32[]{:S(2)}) collective-permute-start(f32[256,128]{0,1:T(8,128)} %get-tuple-element.33), channel_id=1, source_target_pairs={{0,4},{1,5},{2,6},{3,7},{4,8},{5,9},{6,10},{7,11},{8,12},{9,13},{1... | collective-permute-start | bytes 393224 | tf_op jit(solution)/shard_map/ppermute | solution.py:14
  1261.1 29.3 %collective-permute-start.20 = (f32[256,128]{0,1:T(8,128)}, f32[256,128]{0,1:T(8,128)}, u32[]{:S(2)}, u32[]{:S(2)}) collective-permute-start(f32[256,128]{0,1:T(8,128)} %get-tuple-element.34), channel_id=1, source_target_pairs={{4,0},{5,1},{6,2},{7,3},{8,4},{9,5},{10,6},{11,7},{12,8},{13,9},{1... | collective-permute-start | bytes 393224 | tf_op jit(solution)/shard_map/ppermute | solution.py:14
  1267.7 26.7 %collective-permute-start.19 = (f32[256,128]{0,1:T(8,128)}, f32[256,128]{0,1:T(8,128)}, u32[]{:S(2)}, u32[]{:S(2)}) collective-permute-start(f32[256,128]{0,1:T(8,128)} %get-tuple-element.35), channel_id=1, source_target_pairs={{0,1},{1,2},{2,3},{3,4},{4,5},{5,6},{6,7},{7,8},{8,9},{9,10},{10,1... | collective-permute-start | bytes 393224 | tf_op jit(solution)/shard_map/ppermute | solution.py:14
  1270.3 28.1 %collective-permute-start.18 = (f32[256,128]{0,1:T(8,128)}, f32[256,128]{0,1:T(8,128)}, u32[]{:S(2)}, u32[]{:S(2)}) collective-permute-start(f32[256,128]{0,1:T(8,128)} %get-tuple-element.36), channel_id=1, source_target_pairs={{1,0},{2,1},{3,2},{4,3},{5,4},{6,5},{7,6},{8,7},{9,8},{10,9},{11,1... | collective-permute-start | bytes 393224 | tf_op jit(solution)/shard_map/ppermute | solution.py:14
  1380.8 78.1 %copy-start.29 = (f32[128]{0:T(128)}, f32[128]{0:T(128)S(1)}, u32[]{:S(2)}) copy-start(f32[128]{0:T(128)S(1)} %div.31) | copy-start | bytes 1540
  1463.2 707.0 %all-reduce.15.cloned.1.call-start = ((), (), s32[]{:S(2)}) async-start(), calls=%async_computation.4 | async-start | bytes 786432 | tf_op jit(solution)/shard_map/psum | solution.py:73
  1711.8 21.2 collective-permute-start.29
  1714.2 31.2 %collective-permute-start.28 = (f32[256,128]{0,1:T(8,128)}, f32[256,128]{0,1:T(8,128)}, u32[]{:S(2)}, u32[]{:S(2)}) collective-permute-start(f32[256,128]{0,1:T(8,128)} %get-tuple-element.26), channel_id=1, source_target_pairs={{16,0},{17,1},{18,2},{19,3},{20,4},{21,5},{22,6},{23,7},{24,8},{25... | collective-permute-start | bytes 393224 | tf_op jit(solution)/shard_map/ppermute | solution.py:14
  1720.7 28.8 %collective-permute-start.27 = (f32[256,128]{0,1:T(8,128)}, f32[256,128]{0,1:T(8,128)}, u32[]{:S(2)}, u32[]{:S(2)}) collective-permute-start(f32[256,128]{0,1:T(8,128)} %get-tuple-element.27), channel_id=1, source_target_pairs={{0,4},{1,5},{2,6},{3,7},{4,8},{5,9},{6,10},{7,11},{8,12},{9,13},{1... | collective-permute-start | bytes 393224 | tf_op jit(solution)/shard_map/ppermute | solution.py:14
  1724.4 29.1 %collective-permute-start.26 = (f32[256,128]{0,1:T(8,128)}, f32[256,128]{0,1:T(8,128)}, u32[]{:S(2)}, u32[]{:S(2)}) collective-permute-start(f32[256,128]{0,1:T(8,128)} %get-tuple-element.28), channel_id=1, source_target_pairs={{4,0},{5,1},{6,2},{7,3},{8,4},{9,5},{10,6},{11,7},{12,8},{13,9},{1... | collective-permute-start | bytes 393224 | tf_op jit(solution)/shard_map/ppermute | solution.py:14
  1731.1 26.5 %collective-permute-start.25 = (f32[256,128]{0,1:T(8,128)}, f32[256,128]{0,1:T(8,128)}, u32[]{:S(2)}, u32[]{:S(2)}) collective-permute-start(f32[256,128]{0,1:T(8,128)} %get-tuple-element.29), channel_id=1, source_target_pairs={{0,1},{1,2},{2,3},{3,4},{4,5},{5,6},{6,7},{7,8},{8,9},{9,10},{10,1... | collective-permute-start | bytes 393224 | tf_op jit(solution)/shard_map/ppermute | solution.py:14
  1733.6 27.9 %collective-permute-start.24 = (f32[256,128]{0,1:T(8,128)}, f32[256,128]{0,1:T(8,128)}, u32[]{:S(2)}, u32[]{:S(2)}) collective-permute-start(f32[256,128]{0,1:T(8,128)} %get-tuple-element.30), channel_id=1, source_target_pairs={{1,0},{2,1},{3,2},{4,3},{5,4},{6,5},{7,6},{8,7},{9,8},{10,9},{11,1... | collective-permute-start | bytes 393224 | tf_op jit(solution)/shard_map/ppermute | solution.py:14
  2175.2 21.2 collective-permute-start.35
  2177.7 29.1 %collective-permute-start.34 = (f32[256,128]{0,1:T(8,128)}, f32[256,128]{0,1:T(8,128)}, u32[]{:S(2)}, u32[]{:S(2)}) collective-permute-start(f32[256,128]{0,1:T(8,128)} %get-tuple-element.20), channel_id=1, source_target_pairs={{16,0},{17,1},{18,2},{19,3},{20,4},{21,5},{22,6},{23,7},{24,8},{25... | collective-permute-start | bytes 393224 | tf_op jit(solution)/shard_map/ppermute | solution.py:14
  2184.1 26.7 %collective-permute-start.33 = (f32[256,128]{0,1:T(8,128)}, f32[256,128]{0,1:T(8,128)}, u32[]{:S(2)}, u32[]{:S(2)}) collective-permute-start(f32[256,128]{0,1:T(8,128)} %get-tuple-element.21), channel_id=1, source_target_pairs={{0,4},{1,5},{2,6},{3,7},{4,8},{5,9},{6,10},{7,11},{8,12},{9,13},{1... | collective-permute-start | bytes 393224 | tf_op jit(solution)/shard_map/ppermute | solution.py:14
  2187.9 26.9 %collective-permute-start.32 = (f32[256,128]{0,1:T(8,128)}, f32[256,128]{0,1:T(8,128)}, u32[]{:S(2)}, u32[]{:S(2)}) collective-permute-start(f32[256,128]{0,1:T(8,128)} %get-tuple-element.22), channel_id=1, source_target_pairs={{4,0},{5,1},{6,2},{7,3},{8,4},{9,5},{10,6},{11,7},{12,8},{13,9},{1... | collective-permute-start | bytes 393224 | tf_op jit(solution)/shard_map/ppermute | solution.py:14
  2194.5 24.3 %collective-permute-start.31 = (f32[256,128]{0,1:T(8,128)}, f32[256,128]{0,1:T(8,128)}, u32[]{:S(2)}, u32[]{:S(2)}) collective-permute-start(f32[256,128]{0,1:T(8,128)} %get-tuple-element.23), channel_id=1, source_target_pairs={{0,1},{1,2},{2,3},{3,4},{4,5},{5,6},{6,7},{7,8},{8,9},{9,10},{10,1... | collective-permute-start | bytes 393224 | tf_op jit(solution)/shard_map/ppermute | solution.py:14
  2196.4 26.4 %collective-permute-start.30 = (f32[256,128]{0,1:T(8,128)}, f32[256,128]{0,1:T(8,128)}, u32[]{:S(2)}, u32[]{:S(2)}) collective-permute-start(f32[256,128]{0,1:T(8,128)} %get-tuple-element.24), channel_id=1, source_target_pairs={{1,0},{2,1},{3,2},{4,3},{5,4},{6,5},{7,6},{8,7},{9,8},{10,9},{11,1... | collective-permute-start | bytes 393224 | tf_op jit(solution)/shard_map/ppermute | solution.py:14
  2213.1 90.6 %copy-start.28 = (f32[128]{0:T(128)S(1)}, f32[128]{0:T(128)}, u32[]{:S(2)}) copy-start(f32[128]{0:T(128)} %copy-done.27) | copy-start | bytes 1540
  2213.1 90.6 %copy-start.30 = (f32[128]{0:T(128)S(1)}, f32[128]{0:T(128)}, u32[]{:S(2)}) copy-start(f32[128]{0:T(128)} %copy-done.29) | copy-start | bytes 1540
  (28 other events, 244.3 us)
Sparse Core Ops, SparseCore 0:
  68.0 247.1 all-reduce.6
  537.3 243.3 all-reduce.8
  999.9 243.4 all-reduce.10
  1463.3 243.3 all-reduce.12
  1926.8 243.3 all-reduce.14
where the time goes:
time: 2340 us; the launch traced here: 2320 us
  waiting for transfers between devices  1200 us (51%)
  blocking collectives  656 us (28%)
  local copies, waits for them, and re-layouts  187 us (8%)
  starting transfers between devices  174 us (7%)
  matrix products  54.7 us (2%)
  other arithmetic  32.8 us (1%)
    psum x5, waiting for transfers between devices, shards(): summed = lax.psum(partial_sum, 'sub')  1200 us
    psum x5, blocking collectives, energy_sum(): return lax.psum(0.5 * jnp.sum(left * right, axis=0), 'sub')  371 us
    psum x4, blocking collectives, shards(): curvature_sum = lax.psum(0.5 * jnp.sum(direction * product, axis=0), 'sub')  285 us
    ppermute x36, starting transfers between devices, passed_along(): return lax.ppermute(block, axis, route)  174 us
    gather x36, local copies, waits for them, and re-layouts, assemble(): partner_rows.append(from_lower[face_links[2 * direction + 1]])  47.6 us
  transfers between devices with their start and end apart: 41, of which 5 were waited for; matrix products, arithmetic and copies ran while one was open for 6% of the time, Pallas kernels for 0%

commit v1 on v0

v1 whole, which is shorter than its diff:
```python
import functools

import jax
import jax.numpy as jnp
import numpy as np
from jax import lax
from jax.experimental import pallas as pl
from jax.experimental.pallas import tpu as pltpu
from jax.sharding import PartitionSpec as P

ITERS = 5
STRIDES = (1, 4, 16)
GRID = (4, 4, 16)
NSUB = 256
FACES = 6
FD = 256
DOFS = FACES * FD
LOADS = 128
CORNERS = 24
COARSE = 768
NEAR = 256
DOTS = 8
PACKED = FD + 2 * CORNERS + 8
PLACES = np.arange(NSUB).reshape(4, 8, 8)
PLANES = PLACES.transpose(1, 0, 2).reshape(8, 32).tolist()
LINES = PLACES.transpose(0, 2, 1).reshape(32, 8).tolist()
PLANE = 32
LINE = 8
ROWS = COARSE // PLANE
f32 = jnp.float32
bf16 = jnp.bfloat16


def route(direction, sign):
    stride, extent = STRIDES[direction], GRID[direction]
    pairs = []
    for i in range(NSUB):
        place = i // stride % extent
        if 0 <= place + sign < extent:
            pairs.append((i, i + sign * stride))
    return pairs


UP = [route(d, 1) for d in range(3)]
DOWN = [route(d, -1) for d in range(3)]


def swap_faces(blocks):
    received = []
    for d in range(3):
        received.append(lax.ppermute(blocks[2 * d + 1], "sub", DOWN[d]))
        received.append(lax.ppermute(blocks[2 * d], "sub", UP[d]))
    return received


def call(kernel, outs, inputs, smem=(), scratch=(), flops=0):
    shapes = [jax.ShapeDtypeStruct(s, t) for s, t in outs]
    size = sum(int(np.prod(s)) * jnp.dtype(t).itemsize for s, t in outs)
    size += sum(x.size * x.dtype.itemsize for x in inputs)
    return pl.pallas_call(
        kernel,
        out_shape=shapes,
        in_specs=[
            pl.BlockSpec(memory_space=pltpu.SMEM if i in smem else pltpu.VMEM)
            for i in range(len(inputs))
        ],
        out_specs=[pl.BlockSpec(memory_space=pltpu.VMEM)] * len(outs),
        scratch_shapes=list(scratch),
        compiler_params=pltpu.CompilerParams(vmem_limit_bytes=40 * 2**20),
        cost_estimate=pl.CostEstimate(flops=flops, bytes_accessed=size, transcendentals=0),
    )(*inputs)


def mm(a, b):
    return lax.dot_general(a, b, (((1,), (0,)), ((), ())), preferred_element_type=f32)


def mm_t(a, b):
    return lax.dot_general(a, b, (((1,), (1,)), ((), ())), preferred_element_type=f32)


def split(values):
    high = values.astype(bf16)
    return high, (values - high.astype(f32)).astype(bf16)


def split3(values):
    high = values.astype(bf16)
    rest = values - high.astype(f32)
    middle = rest.astype(bf16)
    return high, middle, (rest - middle.astype(f32)).astype(bf16)


def face(f):
    return slice(f * FD, (f + 1) * FD)


def order_of(links_ref, f):
    place = lax.broadcasted_iota(jnp.int32, (FD, FD), 0)
    return jnp.where(place == links_ref[f : f + 1, :], 1.0, 0.0).astype(bf16)


def reorder(order, values):
    high, middle, low = split3(values)
    both = mm(order, jnp.concatenate([high, middle], 1))
    return both[:, :LOADS] + both[:, LOADS:] + mm(order, low)


def pack_kernel(jumps, coupling, links, ids, couple, *packs):
    for f in range(FACES):
        part = coupling[:, face(f)]
        jump = jumps[face(f), :]
        if f % 2:
            order = order_of(links, f)
            jump = -reorder(order, jump)
            high, middle, low = split3(part)
            part = -(mm_t(high, order) + mm_t(middle, order) + mm_t(low, order))
        couple[:, face(f)] = part
        packs[f][:FD, :] = jump
        packs[f][FD : FD + CORNERS, :] = part[:, :LOADS]
        packs[f][FD + CORNERS : FD + 2 * CORNERS, :] = part[:, LOADS:]
        packs[f][FD + 2 * CORNERS :, :] = ids[...]


def arrange_kernel(schur, links, weights, schur_out, weights_out, half):
    for f in range(FACES):
        if f % 2:
            order = order_of(links, f)
            half[face(f), :] = (-mm(order, schur[face(f), :])).astype(bf16)
            weights_out[face(f), :] = reorder(order, weights[face(f), :])
        else:
            half[face(f), :] = schur[face(f), :]
            weights_out[face(f), :] = weights[face(f), :]
    for f in range(FACES):
        if f % 2:
            order = order_of(links, f)
            schur_out[:, face(f)] = (-mm_t(half[:, face(f)], order)).astype(bf16)
        else:
            schur_out[:, face(f)] = half[:, face(f)]


def lift_kernel(*refs):
    glued, couple = refs[:2]
    packs = refs[2 : 2 + FACES]
    high, low, rows = refs[2 + FACES :]
    for f in range(FACES):
        mask = glued[0, f].astype(f32)
        rows[...] = jnp.zeros_like(rows)
        rows[:CORNERS, :] = couple[:, face(f)] * mask
        start = CORNERS * (f + 1)
        rows[start : start + CORNERS, :LOADS] = packs[f][FD : FD + CORNERS, :] * mask
        rows[start : start + CORNERS, LOADS:] = packs[f][FD + CORNERS : FD + 2 * CORNERS, :] * mask
        both = split(rows[...].T)
        high[face(f), :] = both[0]
        low[face(f), :] = both[1]


def open_precond(weights, couple, ids, residual, precond, rounded, spread, state):
    terms = jnp.zeros((2 * CORNERS, 2 * LOADS), f32)
    energy = jnp.zeros((1, LOADS), f32)
    couple_high, couple_low = split(couple[...])
    stacked = jnp.concatenate([couple_high.astype(f32), couple_low.astype(f32)], 0).astype(bf16)
    for f in range(FACES):
        now = weights[face(f), :] * residual[face(f), :]
        precond[face(f), :] = now
        energy += jnp.sum(now * residual[face(f), :], 0, keepdims=True)
        high, low = split(now)
        rounded[face(f), :] = high
        terms += mm(stacked[:, face(f)], jnp.concatenate([high, low], 1))
    terms = terms[:, :LOADS] + terms[:, LOADS:]
    terms = terms[:CORNERS] + terms[CORNERS:]
    spread[...] = jnp.zeros_like(spread)
    for j in range(CORNERS):
        spread[pl.ds(ids[0, j], 1), :] = terms[j : j + 1]
    state[0:1, :] = 0.5 * energy


def begin_kernel(*refs):
    glued, ids, couple, weights = refs[:4]
    sent = refs[4 : 4 + FACES]
    got = refs[4 + FACES : 4 + 2 * FACES]
    residual, precond, rounded, spread, state = refs[4 + 2 * FACES :]
    state[...] = jnp.zeros_like(state)
    for f in range(FACES):
        mask = glued[0, f].astype(f32)
        residual[face(f), :] = mask * (sent[f][:FD, :] + got[f][:FD, :])
    open_precond(weights, couple, ids, residual, precond, rounded, spread, state)


def local_kernel(schur, rounded, precond, state, *refs):
    faces, dots = refs[:FACES], refs[FACES]
    bend = jnp.zeros((1, LOADS), f32)
    for f in range(FACES):
        now = mm(schur[face(f), :], rounded[...])
        faces[f][...] = now
        bend += jnp.sum(now * precond[face(f), :], 0, keepdims=True)
    dots[...] = state[...]
    dots[1:2, :] = bend


def fold_plane_kernel(parts, dots, out):
    total = jnp.sum(parts[...], 0)
    for i in range(LINE):
        out[i, :ROWS, :] = total
        out[i, ROWS:, :] = dots[...]


def fold_line_kernel(parts, out):
    total = jnp.sum(parts[...], 0)
    for i in range(PLANE):
        out[i] = total


def advance_kernel(first, last, *refs):
    glued, ids, near_ids, whole, inverse_high, inverse_low, lift_high, lift_low = refs[:8]
    refs = refs[8:]
    local, got, refs = refs[:FACES], refs[FACES : 2 * FACES], refs[2 * FACES :]
    weights, precond, residual, history = refs[:4]
    refs = refs[4:]
    if not first:
        multipliers, direction, image = refs[:3]
        refs = refs[3:]
    if last:
        links, multipliers_out, residual_out, solved, near = refs
    else:
        couple, multipliers_out, residual_out, direction_out, image_out = refs[:5]
        history_out, precond_out, rounded, spread, state, solved, near = refs[5:]

    coarse = whole[:, :ROWS, :].reshape(COARSE, LOADS)
    sums = jnp.sum(whole[:, ROWS:, :], 0)
    coarse_high, coarse_low = split(coarse)
    both = mm(inverse_high[...], jnp.concatenate([coarse_high, coarse_low], 1))
    solution_rows = both[:, :LOADS] + both[:, LOADS:] + mm(inverse_low[...], coarse_high)
    solved[...] = solution_rows
    near[...] = jnp.zeros_like(near)
    for j in range(CORNERS * (FACES + 1)):
        near[pl.ds(j, 1), :] = solved[pl.ds(near_ids[0, j], 1), :]
    near_high, near_low = split(near[...])
    near_both = jnp.concatenate([near_high, near_low], 1)

    energy = sums[0:1]
    curvature = sums[1:2] + jnp.sum(coarse * solution_rows, 0, keepdims=True)
    if not first:
        ratio = energy / history[0:1, :]
        curvature = curvature + ratio * (2.0 * sums[2:3] + ratio * history[1:2, :])
    step = energy / curvature
    if not last:
        history_out[0:1, :] = energy
        history_out[1:2, :] = curvature
        state[...] = jnp.zeros_like(state)
    cross = jnp.zeros((1, LOADS), f32)
    for f in range(FACES):
        mask = glued[0, f].astype(f32)
        lift = mm(lift_high[face(f), :], near_both)
        lift = lift[:, :LOADS] + lift[:, LOADS:] + mm(lift_low[face(f), :], near_high)
        now = mask * (local[f][...] + got[f][...]) + lift
        way = precond[face(f), :]
        if not first:
            now = now + ratio * image[face(f), :]
            way = way + ratio * direction[face(f), :]
        move = step * way
        if not first:
            move = multipliers[face(f), :] + move
        rest = residual[face(f), :] - step * now
        if last:
            if f % 2:
                place = lax.broadcasted_iota(jnp.int32, (FD, FD), 0)
                order = jnp.where(place == links[f : f + 1, :], 1.0, 0.0).T.astype(bf16)
                move = reorder(order, move)
                rest = reorder(order, rest)
            multipliers_out[face(f), :] = move
            residual_out[face(f), :] = rest
        else:
            multipliers_out[face(f), :] = move
            residual_out[face(f), :] = rest
            direction_out[face(f), :] = way
            image_out[face(f), :] = now
            cross += jnp.sum(weights[face(f), :] * rest * now, 0, keepdims=True)
    if not last:
        open_precond(weights, couple, ids, residual_out, precond_out, rounded, spread, state)
        state[2:3, :] = 0.5 * cross


def shards(jumps, schur, coupling, coarse_inverse, scaling, glued, matching, corners):
    links = matching[0]
    field = ((DOFS, LOADS), f32)
    small = ((DOTS, LOADS), f32)
    open_outs = [field, ((DOFS, LOADS), bf16), ((COARSE, LOADS), f32), small]

    ids_row = jnp.pad(corners.astype(f32), ((0, 7), (0, LOADS - CORNERS)))
    couple, *sent = call(
        pack_kernel,
        [((CORNERS, DOFS), f32)] + [((PACKED, LOADS), f32)] * FACES,
        [jumps[0], coupling[0], links, ids_row],
    )
    got = swap_faces(sent)
    schur_block, weights = call(
        arrange_kernel,
        [((DOFS, DOFS), bf16), field],
        [schur[0], links, jnp.broadcast_to(scaling[0][:, None], (DOFS, LOADS))],
        scratch=[pltpu.VMEM((DOFS, DOFS), bf16)],
        flops=4 * DOFS * DOFS * FD,
    )
    residual, precond, rounded, spread, state = call(
        begin_kernel, [field] + open_outs, [glued, corners, couple, weights, *sent, *got], smem=(0, 1)
    )
    lift_high, lift_low = call(
        lift_kernel,
        [((DOFS, NEAR), bf16)] * 2,
        [glued, couple, *got],
        smem=(0,),
        scratch=[pltpu.VMEM((NEAR, FD), f32)],
    )
    near_ids = jnp.concatenate(
        [corners] + [g[FD + 2 * CORNERS :][:1, :CORNERS].astype(jnp.int32) for g in got], 1
    )
    kept = lax.reduce_precision(coarse_inverse, 8, 7)
    inverse_high, inverse_low = kept.astype(bf16), (coarse_inverse - kept).astype(bf16)

    multipliers = direction = image = history = None
    for iteration in range(ITERS):
        first, last = iteration == 0, iteration + 1 == ITERS
        parts = lax.all_to_all(
            spread.reshape(PLANE, ROWS, LOADS), "sub", 0, 0, axis_index_groups=PLANES
        )
        *local, dots = call(
            local_kernel,
            [((FD, LOADS), f32)] * FACES + [small],
            [schur_block, rounded, precond, state],
            flops=2 * DOFS * DOFS * LOADS,
        )
        received = swap_faces(local)
        (lines,) = call(fold_plane_kernel, [((LINE, ROWS + DOTS, LOADS), f32)], [parts, dots])
        lines = lax.all_to_all(lines, "sub", 0, 0, axis_index_groups=LINES)
        (whole,) = call(fold_line_kernel, [((PLANE, ROWS + DOTS, LOADS), f32)], [lines])
        whole = lax.all_to_all(whole, "sub", 0, 0, axis_index_groups=PLANES)
        inputs = [glued, corners, near_ids, whole, inverse_high, inverse_low, lift_high, lift_low]
        inputs += [*local, *received, weights, precond, residual]
        inputs += [state if first else history]
        if not first:
            inputs += [multipliers, direction, image]
        inputs += [links if last else couple]
        outs = [field, field]
        if not last:
            outs += [field, field, small] + open_outs
        results = call(
            functools.partial(advance_kernel, first, last),
            outs,
            inputs,
            smem=(0, 1, 2),
            scratch=[pltpu.VMEM((COARSE, LOADS), f32), pltpu.VMEM((NEAR, LOADS), f32)],
        )
        multipliers, residual = results[:2]
        if not last:
            direction, image, history, precond, rounded, spread, state = results[2:]
    return (multipliers[None], residual[None])


def solution(mesh):
    return jax.shard_map(
        shards,
        mesh=mesh,
        in_specs=(
            P("sub", None, None),
            P("sub", None, None),
            P("sub", None, None),
            P(),
            P("sub", None),
            P("sub", None),
            P("sub", None, None),
            P("sub", None),
        ),
        out_specs=(P("sub", None, None), P("sub", None, None)),
        check_vma=False,
    )
```

time: 2340 us -> 513 us (0.22)
  waiting for transfers between devices: 1200 us -> 33.3 us
  blocking collectives: 656 us -> 60.3 us
  matrix products: 54.7 us -> 0 us
  Pallas kernels: 0 us -> 37 us
  other arithmetic: 32.8 us -> 6.95 us
    psum x5 -> x0, waiting for transfers between devices: 1200 us -> none  [shards(): summed = lax.psum(partial_sum, 'sub')]
    psum x9 -> x0, blocking collectives: 656 us -> none  [the longest x5 371 us: energy_sum(): return lax.psum(0.5 * jnp.sum(left * right, axis=0), 'sub')]
    unnamed x108 -> x415, local copies, waits for them, and re-layouts: 46.7 us -> 170 us
    gather x73 -> x0, local copies, waits for them, and re-layouts: 93.8 us -> none  [the longest x36 47.6 us: assemble(): partner_rows.append(from_lower[face_links[2 * direction + 1]])]
    all_to_all x0 -> x11, starting transfers between devices: none -> 82.7 us  [the longest x5 39.3 us: shards(): lax.all_to_all(spread.reshape(PLANE, ROWS, LOADS), 'sub', 0, 0, axis_inde...]
    ppermute x36, starting transfers between devices: 174 us -> 113 us  [the longest x18 58.2 us: swap_faces(): received.append(lax.ppermute(blocks[2 * d], 'sub', UP[d]))]
    all_to_all x0 -> x4, blocking collectives: none -> 60.3 us  [shards(): lines = lax.all_to_all(lines, 'sub', 0, 0, axis_index_groups=LINES)]
    dot_general x25 -> x0, matrix products: 54.7 us -> none  [the longest x5 26.4 us: shards(): jnp.dot(schur_block, signed.astype(jnp.bfloat16), preferred_element_type=...]
  transfers between devices with their start and end apart: 41 -> 47, of which waited for: 5 -> 11; matrix products, arithmetic and copies ran while one was open for 6% -> 1% of each run, Pallas kernels for 0% -> 2%
where the time goes in v1:
time: 513 us; the launch traced here: 505 us
  starting transfers between devices  196 us (38%)
  local copies, waits for them, and re-layouts  170 us (33%)
  blocking collectives  60.3 us (12%)
  Pallas kernels  37 us (7%)
  waiting for transfers between devices  33.3 us (6%)
  other arithmetic  6.95 us (1%)
    unnamed x415, local copies, waits for them, and re-layouts  170 us
    all_to_all x4, blocking collectives, shards(): lines = lax.all_to_all(lines, 'sub', 0, 0, axis_index_groups=LINES)  60.3 us
    ppermute x18, starting transfers between devices, swap_faces(): received.append(lax.ppermute(blocks[2 * d], 'sub', UP[d]))  58.2 us
    ppermute x18, starting transfers between devices, swap_faces(): received.append(lax.ppermute(blocks[2 * d + 1], 'sub', DOWN[d]))  54.7 us
    all_to_all x5, starting transfers between devices, shards(): lax.all_to_all(spread.reshape(PLANE, ROWS, LOADS), 'sub', 0, 0, axis_inde...  39.3 us
    all_to_all x5, starting transfers between devices, shards(): whole = lax.all_to_all(whole, 'sub', 0, 0, axis_index_groups=PLANES)  38.6 us
    pallas_call x24, Pallas kernels, call(): pl.pallas_call(kernel, out_shape=shapes, in_specs=[pl.BlockSpec(memory_sp...  37 us
    ppermute x18, waiting for transfers between devices, swap_faces(): received.append(lax.ppermute(blocks[2 * d], 'sub', UP[d]))  19.2 us
  transfers between devices with their start and end apart: 47, of which 11 were waited for; matrix products, arithmetic and copies ran while one was open for 1% of the time, Pallas kernels for 2%

profile of v1, /device:TPU:24, one launch (start us, length us, event | category | flops | bytes accessed | tf_op | source)
XLA Modules:
  0.0 505.3 jit_solution(11666741811239854472)
XLA Ops:
  6.5 3.0 collective-permute-start.1
  10.8 6.1 %collective-permute-start.3 = (f32[312,128]{1,0:T(8,128)S(1)}, f32[312,128]{1,0:T(8,128)S(1)}, u32[]{:S(2)}, u32[]{:S(2)}) collective-permute-start(f32[312,128]{1,0:T(8,128)S(1)} %get-tuple-element.94.refs_6_), channel_id=1, source_target_pairs={{0,4},{1,5},{2,6},{3,7},{4,8},{5,9},{6,10},{7,11},{8,12},{9,13},{1... | collective-permute-start | bytes 479240 | tf_op jit(solution)/shard_map/ppermute | solution.py:52
  16.9 8.4 %collective-permute-start.4 = (f32[312,128]{1,0:T(8,128)S(1)}, f32[312,128]{1,0:T(8,128)S(1)}, u32[]{:S(2)}, u32[]{:S(2)}) collective-permute-start(f32[312,128]{1,0:T(8,128)S(1)} %get-tuple-element.95.refs_9_), channel_id=1, source_target_pairs={{16,0},{17,1},{18,2},{19,3},{20,4},{21,5},{22,6},{23,7},{24,8},{25... | collective-permute-start | bytes 479240 | tf_op jit(solution)/shard_map/ppermute | solution.py:51
  28.2 2.3 copy-done.206
  34.5 5.9 %collective-permute-done.5.refs_15_.refs_7_ = f32[312,128]{1,0:T(8,128)S(1)} collective-permute-done((f32[312,128]{1,0:T(8,128)}, f32[312,128]{1,0:T(8,128)S(1)}, u32[]{:S(2)}, u32[]{:S(2)}) %collective-permute-start.5) | collective-permute-done | bytes 159776 | tf_op jit(solution)/shard_map/ppermute | solution.py:52
  46.6 5.1 %all-to-all-start = ((f32[32,24,128]{2,1,0:T(8,128)}), f32[32,24,128]{2,1,0:T(8,128)}, u32[]{:S(2)}, u32[]{:S(2)}) async-start(f32[32,24,128]{2,1,0:T(8,128)} %bitcast.3), calls=%async_computation | async-start | bytes 786432 | tf_op jit(solution)/shard_map/all_to_all | solution.py:323
  56.9 2.2 shard_map.98
  59.7 2.8 collective-permute-start.7
  63.8 5.6 %collective-permute-start.9 = (f32[256,128]{1,0:T(8,128)}, f32[256,128]{1,0:T(8,128)}, u32[]{:S(2)}, u32[]{:S(2)}) collective-permute-start(f32[256,128]{1,0:T(8,128)} %get-tuple-element.109.refs_10_), channel_id=1, source_target_pairs={{0,4},{1,5},{2,6},{3,7},{4,8},{5,9},{6,10},{7,11},{8,12},{9,13},{1... | collective-permute-start | bytes 393224 | tf_op jit(solution)/shard_map/ppermute | solution.py:52
  70.6 3.0 collective-permute-start.11
  75.4 4.9 all-to-all-start.1
  81.6 8.6 %all-to-all-done.1.parts = f32[8,32,128]{2,1,0:T(8,128)} async-done(((f32[8,32,128]{2,1,0:T(8,128)}), f32[8,32,128]{2,1,0:T(8,128)}, u32[]{:S(2)}, u32[]{:S(2)}) %all-to-all-start.1) | async-done | bytes 131104 | tf_op jit(solution)/shard_map/all_to_all | solution.py:334
  92.0 9.1 %all-to-all-start.2 = ((f32[32,32,128]{2,1,0:T(8,128)}), f32[32,32,128]{2,1,0:T(8,128)}, u32[]{:S(2)}, u32[]{:S(2)}) async-start(f32[32,32,128]{2,1,0:T(8,128)} %copy-done.34), calls=%async_computation.2 | async-start | bytes 1048576 | tf_op jit(solution)/shard_map/all_to_all | solution.py:336
  102.5 2.9 collective-permute-start.10
  119.4 3.4 shard_map.102
  129.4 7.4 %all-to-all-start.3 = ((f32[32,24,128]{2,1,0:T(8,128)}), f32[32,24,128]{2,1,0:T(8,128)S(1)}, u32[]{:S(2)}, u32[]{:S(2)}) async-start(f32[32,24,128]{2,1,0:T(8,128)} %bitcast.17), calls=%async_computation.3 | async-start | bytes 786432 | tf_op jit(solution)/shard_map/all_to_all | solution.py:323
  136.8 2.3 copy-done.2
  146.6 13.4 %all_to_all.75.parts = f32[8,32,128]{2,1,0:T(8,128)S(1)} all-to-all(f32[8,32,128]{2,1,0:T(8,128)S(1)} %shard_map.104), channel_id=1, replica_groups={{0,8,16,24,32,40,48,56},{1,9,17,25,33,41,49,57},{2,10,18,26,34,42,50,58..., dimensions={0} | all-to-all | bytes 262144 | tf_op jit(solution)/shard_map/all_to_all | solution.py:334
  160.9 7.4 %all-to-all-start.5 = ((f32[32,32,128]{2,1,0:T(8,128)}), f32[32,32,128]{2,1,0:T(8,128)}, u32[]{:S(2)}, u32[]{:S(2)}) async-start(f32[32,32,128]{2,1,0:T(8,128)} %shard_map.105), calls=%async_computation.5 | async-start | bytes 1048576 | tf_op jit(solution)/shard_map/all_to_all | solution.py:336
  168.3 2.2 collective-permute-start.13
  171.8 4.9 collective-permute-start.15
  180.0 6.9 %collective-permute-start.16 = (f32[256,128]{1,0:T(8,128)}, f32[256,128]{1,0:T(8,128)S(1)}, u32[]{:S(2)}, u32[]{:S(2)}) collective-permute-start(f32[256,128]{1,0:T(8,128)} %copy-done.120), channel_id=1, source_target_pairs={{16,0},{17,1},{18,2},{19,3},{20,4},{21,5},{22,6},{23,7},{24,8},{25... | collective-permute-start | bytes 393224 | tf_op jit(solution)/shard_map/ppermute | solution.py:51
  187.6 4.3 collective-permute-done.17.refs_19_
  210.0 3.3 shard_map.106
  220.5 8.9 %all-to-all-start.6 = ((f32[32,24,128]{2,1,0:T(8,128)}), f32[32,24,128]{2,1,0:T(8,128)S(1)}, u32[]{:S(2)}, u32[]{:S(2)}) async-start(f32[32,24,128]{2,1,0:T(8,128)} %bitcast.15), calls=%async_computation.6 | async-start | bytes 786432 | tf_op jit(solution)/shard_map/all_to_all | solution.py:323
  229.4 2.3 copy-done.3
  239.8 15.6 %all_to_all.76.parts = f32[8,32,128]{2,1,0:T(8,128)S(1)} all-to-all(f32[8,32,128]{2,1,0:T(8,128)S(1)} %shard_map.108), channel_id=1, replica_groups={{0,8,16,24,32,40,48,56},{1,9,17,25,33,41,49,57},{2,10,18,26,34,42,50,58..., dimensions={0} | all-to-all | bytes 262144 | tf_op jit(solution)/shard_map/all_to_all | solution.py:334
  256.3 7.4 %all-to-all-start.8 = ((f32[32,32,128]{2,1,0:T(8,128)}), f32[32,32,128]{2,1,0:T(8,128)}, u32[]{:S(2)}, u32[]{:S(2)}) async-start(f32[32,32,128]{2,1,0:T(8,128)} %shard_map.109), calls=%async_computation.8 | async-start | bytes 1048576 | tf_op jit(solution)/shard_map/all_to_all | solution.py:336
  267.1 4.9 collective-permute-start.21
  275.2 6.9 %collective-permute-start.22 = (f32[256,128]{1,0:T(8,128)}, f32[256,128]{1,0:T(8,128)S(1)}, u32[]{:S(2)}, u32[]{:S(2)}) collective-permute-start(f32[256,128]{1,0:T(8,128)} %copy-done.128), channel_id=1, source_target_pairs={{16,0},{17,1},{18,2},{19,3},{20,4},{21,5},{22,6},{23,7},{24,8},{25... | collective-permute-start | bytes 393224 | tf_op jit(solution)/shard_map/ppermute | solution.py:51
  282.9 4.3 collective-permute-done.23.refs_19_
  305.2 3.3 shard_map.110
  315.7 8.9 %all-to-all-start.9 = ((f32[32,24,128]{2,1,0:T(8,128)}), f32[32,24,128]{2,1,0:T(8,128)S(1)}, u32[]{:S(2)}, u32[]{:S(2)}) async-start(f32[32,24,128]{2,1,0:T(8,128)} %bitcast.16), calls=%async_computation.9 | async-start | bytes 786432 | tf_op jit(solution)/shard_map/all_to_all | solution.py:323
  324.6 2.3 copy-done.4
  335.1 15.6 %all_to_all.77.parts = f32[8,32,128]{2,1,0:T(8,128)S(1)} all-to-all(f32[8,32,128]{2,1,0:T(8,128)S(1)} %shard_map.112), channel_id=1, replica_groups={{0,8,16,24,32,40,48,56},{1,9,17,25,33,41,49,57},{2,10,18,26,34,42,50,58..., dimensions={0} | all-to-all | bytes 262144 | tf_op jit(solution)/shard_map/all_to_all | solution.py:334
  351.5 7.4 %all-to-all-start.11 = ((f32[32,32,128]{2,1,0:T(8,128)}), f32[32,32,128]{2,1,0:T(8,128)}, u32[]{:S(2)}, u32[]{:S(2)}) async-start(f32[32,32,128]{2,1,0:T(8,128)} %shard_map.113), calls=%async_computation.11 | async-start | bytes 1048576 | tf_op jit(solution)/shard_map/all_to_all | solution.py:336
  362.3 4.9 collective-permute-start.27
  371.1 7.1 %collective-permute-start.28 = (f32[256,128]{1,0:T(8,128)}, f32[256,128]{1,0:T(8,128)S(1)}, u32[]{:S(2)}, u32[]{:S(2)}) collective-permute-start(f32[256,128]{1,0:T(8,128)} %copy-done.104), channel_id=1, source_target_pairs={{16,0},{17,1},{18,2},{19,3},{20,4},{21,5},{22,6},{23,7},{24,8},{25... | collective-permute-start | bytes 393224 | tf_op jit(solution)/shard_map/ppermute | solution.py:51
  380.2 2.2 collective-permute-done.29.refs_19_
  403.8 3.3 shard_map.114
  413.5 9.0 %all-to-all-start.12 = ((f32[32,24,128]{2,1,0:T(8,128)}), f32[32,24,128]{2,1,0:T(8,128)}, u32[]{:S(2)}, u32[]{:S(2)}) async-start(f32[32,24,128]{2,1,0:T(8,128)} %bitcast.14), calls=%async_computation.12 | async-start | bytes 786432 | tf_op jit(solution)/shard_map/all_to_all | solution.py:323
  422.5 2.3 copy-done.5
  431.8 15.8 %all_to_all.78.parts = f32[8,32,128]{2,1,0:T(8,128)S(1)} all-to-all(f32[8,32,128]{2,1,0:T(8,128)S(1)} %shard_map.116), channel_id=1, replica_groups={{0,8,16,24,32,40,48,56},{1,9,17,25,33,41,49,57},{2,10,18,26,34,42,50,58..., dimensions={0} | all-to-all | bytes 262144 | tf_op jit(solution)/shard_map/all_to_all | solution.py:334
  448.5 7.2 %all-to-all-start.14 = ((f32[32,32,128]{2,1,0:T(8,128)}), f32[32,32,128]{2,1,0:T(8,128)}, u32[]{:S(2)}, u32[]{:S(2)}) async-start(f32[32,32,128]{2,1,0:T(8,128)} %copy-done.33), calls=%async_computation.14 | async-start | bytes 1048576 | tf_op jit(solution)/shard_map/all_to_all | solution.py:336
  459.0 4.9 collective-permute-start.33
  467.8 6.9 %collective-permute-start.34 = (f32[256,128]{1,0:T(8,128)}, f32[256,128]{1,0:T(8,128)S(1)}, u32[]{:S(2)}, u32[]{:S(2)}) collective-permute-start(f32[256,128]{1,0:T(8,128)} %copy-done.112), channel_id=1, source_target_pairs={{16,0},{17,1},{18,2},{19,3},{20,4},{21,5},{22,6},{23,7},{24,8},{25... | collective-permute-start | bytes 393224 | tf_op jit(solution)/shard_map/ppermute | solution.py:51
  476.7 2.4 collective-permute-done.35.refs_19_
  501.0 4.3 shard_map.118
  (501 shorter events, 219.8 us)
Async XLA Ops:
  5.2 20.8 %collective-permute-start = (f32[312,128]{1,0:T(8,128)S(1)}, f32[312,128]{1,0:T(8,128)S(1)}, u32[]{:S(2)}, u32[]{:S(2)}) collective-permute-start(f32[312,128]{1,0:T(8,128)S(1)} %get-tuple-element.91.refs_5_), channel_id=1, source_target_pairs={{1,0},{2,1},{3,2},{5,4},{6,5},{7,6},{9,8},{10,9},{11,10},{13,12},{... | collective-permute-start | bytes 479240 | tf_op jit(solution)/shard_map/ppermute | solution.py:51
  6.5 28.0 %collective-permute-start.1 = (f32[312,128]{1,0:T(8,128)S(1)}, f32[312,128]{1,0:T(8,128)S(1)}, u32[]{:S(2)}, u32[]{:S(2)}) collective-permute-start(f32[312,128]{1,0:T(8,128)S(1)} %get-tuple-element.92.refs_4_), channel_id=1, source_target_pairs={{0,1},{1,2},{2,3},{4,5},{5,6},{6,7},{8,9},{9,10},{10,11},{12,13},{... | collective-permute-start | bytes 479240 | tf_op jit(solution)/shard_map/ppermute | solution.py:52
  9.5 24.9 %collective-permute-start.2 = (f32[312,128]{1,0:T(8,128)S(1)}, f32[312,128]{1,0:T(8,128)S(1)}, u32[]{:S(2)}, u32[]{:S(2)}) collective-permute-start(f32[312,128]{1,0:T(8,128)S(1)} %get-tuple-element.93.refs_7_), channel_id=1, source_target_pairs={{4,0},{5,1},{6,2},{7,3},{8,4},{9,5},{10,6},{11,7},{12,8},{13,9},{1... | collective-permute-start | bytes 479240 | tf_op jit(solution)/shard_map/ppermute | solution.py:51
  10.8 23.7 %collective-permute-start.3 = (f32[312,128]{1,0:T(8,128)S(1)}, f32[312,128]{1,0:T(8,128)S(1)}, u32[]{:S(2)}, u32[]{:S(2)}) collective-permute-start(f32[312,128]{1,0:T(8,128)S(1)} %get-tuple-element.94.refs_6_), channel_id=1, source_target_pairs={{0,4},{1,5},{2,6},{3,7},{4,8},{5,9},{6,10},{7,11},{8,12},{9,13},{1... | collective-permute-start | bytes 479240 | tf_op jit(solution)/shard_map/ppermute | solution.py:52
  16.9 17.6 %collective-permute-start.4 = (f32[312,128]{1,0:T(8,128)S(1)}, f32[312,128]{1,0:T(8,128)S(1)}, u32[]{:S(2)}, u32[]{:S(2)}) collective-permute-start(f32[312,128]{1,0:T(8,128)S(1)} %get-tuple-element.95.refs_9_), channel_id=1, source_target_pairs={{16,0},{17,1},{18,2},{19,3},{20,4},{21,5},{22,6},{23,7},{24,8},{25... | collective-permute-start | bytes 479240 | tf_op jit(solution)/shard_map/ppermute | solution.py:51
  26.0 14.4 %collective-permute-start.5 = (f32[312,128]{1,0:T(8,128)}, f32[312,128]{1,0:T(8,128)S(1)}, u32[]{:S(2)}, u32[]{:S(2)}) collective-permute-start(f32[312,128]{1,0:T(8,128)} %get-tuple-element.96.refs_8_), channel_id=1, source_target_pairs={{0,16},{1,17},{2,18},{3,19},{4,20},{5,21},{6,22},{7,23},{8,24},{9,... | collective-permute-start | bytes 479240 | tf_op jit(solution)/shard_map/ppermute | solution.py:52
  46.6 27.1 %all-to-all-start = ((f32[32,24,128]{2,1,0:T(8,128)}), f32[32,24,128]{2,1,0:T(8,128)}, u32[]{:S(2)}, u32[]{:S(2)}) async-start(f32[32,24,128]{2,1,0:T(8,128)} %bitcast.3), calls=%async_computation | async-start | bytes 786432 | tf_op jit(solution)/shard_map/all_to_all | solution.py:323
  53.8 60.1 %copy-start.6 = (bf16[768,768]{1,0:T(8,128)(2,1)}, bf16[768,768]{1,0:T(8,128)(2,1)S(1)}, u32[]{:S(2)}) copy-start(bf16[768,768]{1,0:T(8,128)(2,1)S(1)} %get-tuple-element.180.refs_5_) | copy-start | bytes 3538948
  59.7 42.8 %collective-permute-start.7 = (f32[256,128]{1,0:T(8,128)}, f32[256,128]{1,0:T(8,128)}, u32[]{:S(2)}, u32[]{:S(2)}) collective-permute-start(f32[256,128]{1,0:T(8,128)} %get-tuple-element.107.refs_8_), channel_id=1, source_target_pairs={{0,1},{1,2},{2,3},{4,5},{5,6},{6,7},{8,9},{9,10},{10,11},{12,13},{... | collective-permute-start | bytes 393224 | tf_op jit(solution)/shard_map/ppermute | solution.py:52
  62.5 51.0 %collective-permute-start.6 = (f32[256,128]{1,0:T(8,128)}, f32[256,128]{1,0:T(8,128)}, u32[]{:S(2)}, u32[]{:S(2)}) collective-permute-start(f32[256,128]{1,0:T(8,128)} %get-tuple-element.108.refs_9_), channel_id=1, source_target_pairs={{1,0},{2,1},{3,2},{5,4},{6,5},{7,6},{9,8},{10,9},{11,10},{13,12},{... | collective-permute-start | bytes 393224 | tf_op jit(solution)/shard_map/ppermute | solution.py:51
  63.8 49.7 %collective-permute-start.9 = (f32[256,128]{1,0:T(8,128)}, f32[256,128]{1,0:T(8,128)}, u32[]{:S(2)}, u32[]{:S(2)}) collective-permute-start(f32[256,128]{1,0:T(8,128)} %get-tuple-element.109.refs_10_), channel_id=1, source_target_pairs={{0,4},{1,5},{2,6},{3,7},{4,8},{5,9},{6,10},{7,11},{8,12},{9,13},{1... | collective-permute-start | bytes 393224 | tf_op jit(solution)/shard_map/ppermute | solution.py:52
  69.4 44.1 %collective-permute-start.8 = (f32[256,128]{1,0:T(8,128)}, f32[256,128]{1,0:T(8,128)}, u32[]{:S(2)}, u32[]{:S(2)}) collective-permute-start(f32[256,128]{1,0:T(8,128)} %get-tuple-element.110.refs_11_), channel_id=1, source_target_pairs={{4,0},{5,1},{6,2},{7,3},{8,4},{9,5},{10,6},{11,7},{12,8},{13,9},{1... | collective-permute-start | bytes 393224 | tf_op jit(solution)/shard_map/ppermute | solution.py:51
  70.6 42.9 %collective-permute-start.11 = (f32[256,128]{1,0:T(8,128)}, f32[256,128]{1,0:T(8,128)}, u32[]{:S(2)}, u32[]{:S(2)}) collective-permute-start(f32[256,128]{1,0:T(8,128)} %get-tuple-element.111.refs_12_), channel_id=1, source_target_pairs={{0,16},{1,17},{2,18},{3,19},{4,20},{5,21},{6,22},{7,23},{8,24},{9,... | collective-permute-start | bytes 393224 | tf_op jit(solution)/shard_map/ppermute | solution.py:52
  75.4 14.8 %all-to-all-start.1 = ((f32[8,32,128]{2,1,0:T(8,128)}), f32[8,32,128]{2,1,0:T(8,128)}, u32[]{:S(2)}, u32[]{:S(2)}) async-start(f32[8,32,128]{2,1,0:T(8,128)} %copy-done.80), calls=%async_computation.1 | async-start | bytes 262144 | tf_op jit(solution)/shard_map/all_to_all | solution.py:334
  92.0 22.0 %all-to-all-start.2 = ((f32[32,32,128]{2,1,0:T(8,128)}), f32[32,32,128]{2,1,0:T(8,128)}, u32[]{:S(2)}, u32[]{:S(2)}) async-start(f32[32,32,128]{2,1,0:T(8,128)} %copy-done.34), calls=%async_computation.2 | async-start | bytes 1048576 | tf_op jit(solution)/shard_map/all_to_all | solution.py:336
  102.5 11.5 %collective-permute-start.10 = (f32[256,128]{1,0:T(8,128)}, f32[256,128]{1,0:T(8,128)}, u32[]{:S(2)}, u32[]{:S(2)}) collective-permute-start(f32[256,128]{1,0:T(8,128)} %copy-done.96), channel_id=1, source_target_pairs={{16,0},{17,1},{18,2},{19,3},{20,4},{21,5},{22,6},{23,7},{24,8},{25... | collective-permute-start | bytes 393224 | tf_op jit(solution)/shard_map/ppermute | solution.py:51
  129.4 16.4 %all-to-all-start.3 = ((f32[32,24,128]{2,1,0:T(8,128)}), f32[32,24,128]{2,1,0:T(8,128)S(1)}, u32[]{:S(2)}, u32[]{:S(2)}) async-start(f32[32,24,128]{2,1,0:T(8,128)} %bitcast.17), calls=%async_computation.3 | async-start | bytes 786432 | tf_op jit(solution)/shard_map/all_to_all | solution.py:323
  160.9 33.3 %all-to-all-start.5 = ((f32[32,32,128]{2,1,0:T(8,128)}), f32[32,32,128]{2,1,0:T(8,128)}, u32[]{:S(2)}, u32[]{:S(2)}) async-start(f32[32,32,128]{2,1,0:T(8,128)} %shard_map.105), calls=%async_computation.5 | async-start | bytes 1048576 | tf_op jit(solution)/shard_map/all_to_all | solution.py:336
  168.3 11.7 %collective-permute-start.13 = (f32[256,128]{1,0:T(8,128)S(1)}, f32[256,128]{1,0:T(8,128)S(1)}, u32[]{:S(2)}, u32[]{:S(2)}) collective-permute-start(f32[256,128]{1,0:T(8,128)S(1)} %get-tuple-element.119.refs_8_), channel_id=1, source_target_pairs={{0,1},{1,2},{2,3},{4,5},{5,6},{6,7},{8,9},{9,10},{10,11},{12,13},{... | collective-permute-start | bytes 393224 | tf_op jit(solution)/shard_map/ppermute | solution.py:52
  170.5 16.4 %collective-permute-start.12 = (f32[256,128]{1,0:T(8,128)S(1)}, f32[256,128]{1,0:T(8,128)S(1)}, u32[]{:S(2)}, u32[]{:S(2)}) collective-permute-start(f32[256,128]{1,0:T(8,128)S(1)} %get-tuple-element.120.refs_9_), channel_id=1, source_target_pairs={{1,0},{2,1},{3,2},{5,4},{6,5},{7,6},{9,8},{10,9},{11,10},{13,12},{... | collective-permute-start | bytes 393224 | tf_op jit(solution)/shard_map/ppermute | solution.py:51
  171.8 15.1 %collective-permute-start.15 = (f32[256,128]{1,0:T(8,128)}, f32[256,128]{1,0:T(8,128)S(1)}, u32[]{:S(2)}, u32[]{:S(2)}) collective-permute-start(f32[256,128]{1,0:T(8,128)} %copy-done.114), channel_id=1, source_target_pairs={{0,4},{1,5},{2,6},{3,7},{4,8},{5,9},{6,10},{7,11},{8,12},{9,13},{1... | collective-permute-start | bytes 393224 | tf_op jit(solution)/shard_map/ppermute | solution.py:52
  176.8 10.2 %collective-permute-start.14 = (f32[256,128]{1,0:T(8,128)}, f32[256,128]{1,0:T(8,128)S(1)}, u32[]{:S(2)}, u32[]{:S(2)}) collective-permute-start(f32[256,128]{1,0:T(8,128)} %copy-done.116), channel_id=1, source_target_pairs={{4,0},{5,1},{6,2},{7,3},{8,4},{9,5},{10,6},{11,7},{12,8},{13,9},{1... | collective-permute-start | bytes 393224 | tf_op jit(solution)/shard_map/ppermute | solution.py:51
  178.1 13.9 %collective-permute-start.17 = (f32[256,128]{1,0:T(8,128)}, f32[256,128]{1,0:T(8,128)S(1)}, u32[]{:S(2)}, u32[]{:S(2)}) collective-permute-start(f32[256,128]{1,0:T(8,128)} %copy-done.118), channel_id=1, source_target_pairs={{0,16},{1,17},{2,18},{3,19},{4,20},{5,21},{6,22},{7,23},{8,24},{9,... | collective-permute-start | bytes 393224 | tf_op jit(solution)/shard_map/ppermute | solution.py:52
  180.0 13.5 %collective-permute-start.16 = (f32[256,128]{1,0:T(8,128)}, f32[256,128]{1,0:T(8,128)S(1)}, u32[]{:S(2)}, u32[]{:S(2)}) collective-permute-start(f32[256,128]{1,0:T(8,128)} %copy-done.120), channel_id=1, source_target_pairs={{16,0},{17,1},{18,2},{19,3},{20,4},{21,5},{22,6},{23,7},{24,8},{25... | collective-permute-start | bytes 393224 | tf_op jit(solution)/shard_map/ppermute | solution.py:51
  220.5 18.7 %all-to-all-start.6 = ((f32[32,24,128]{2,1,0:T(8,128)}), f32[32,24,128]{2,1,0:T(8,128)S(1)}, u32[]{:S(2)}, u32[]{:S(2)}) async-start(f32[32,24,128]{2,1,0:T(8,128)} %bitcast.15), calls=%async_computation.6 | async-start | bytes 786432 | tf_op jit(solution)/shard_map/all_to_all | solution.py:323
  256.3 33.1 %all-to-all-start.8 = ((f32[32,32,128]{2,1,0:T(8,128)}), f32[32,32,128]{2,1,0:T(8,128)}, u32[]{:S(2)}, u32[]{:S(2)}) async-start(f32[32,32,128]{2,1,0:T(8,128)} %shard_map.109), calls=%async_computation.8 | async-start | bytes 1048576 | tf_op jit(solution)/shard_map/all_to_all | solution.py:336
  263.7 11.5 %collective-permute-start.19 = (f32[256,128]{1,0:T(8,128)S(1)}, f32[256,128]{1,0:T(8,128)S(1)}, u32[]{:S(2)}, u32[]{:S(2)}) collective-permute-start(f32[256,128]{1,0:T(8,128)S(1)} %get-tuple-element.135.refs_8_), channel_id=1, source_target_pairs={{0,1},{1,2},{2,3},{4,5},{5,6},{6,7},{8,9},{9,10},{10,11},{12,13},{... | collective-permute-start | bytes 393224 | tf_op jit(solution)/shard_map/ppermute | solution.py:52
  265.8 16.4 %collective-permute-start.18 = (f32[256,128]{1,0:T(8,128)S(1)}, f32[256,128]{1,0:T(8,128)S(1)}, u32[]{:S(2)}, u32[]{:S(2)}) collective-permute-start(f32[256,128]{1,0:T(8,128)S(1)} %get-tuple-element.136.refs_9_), channel_id=1, source_target_pairs={{1,0},{2,1},{3,2},{5,4},{6,5},{7,6},{9,8},{10,9},{11,10},{13,12},{... | collective-permute-start | bytes 393224 | tf_op jit(solution)/shard_map/ppermute | solution.py:51
  267.1 15.1 %collective-permute-start.21 = (f32[256,128]{1,0:T(8,128)}, f32[256,128]{1,0:T(8,128)S(1)}, u32[]{:S(2)}, u32[]{:S(2)}) collective-permute-start(f32[256,128]{1,0:T(8,128)} %copy-done.122), channel_id=1, source_target_pairs={{0,4},{1,5},{2,6},{3,7},{4,8},{5,9},{6,10},{7,11},{8,12},{9,13},{1... | collective-permute-start | bytes 393224 | tf_op jit(solution)/shard_map/ppermute | solution.py:52
  272.0 10.2 %collective-permute-start.20 = (f32[256,128]{1,0:T(8,128)}, f32[256,128]{1,0:T(8,128)S(1)}, u32[]{:S(2)}, u32[]{:S(2)}) collective-permute-start(f32[256,128]{1,0:T(8,128)} %copy-done.124), channel_id=1, source_target_pairs={{4,0},{5,1},{6,2},{7,3},{8,4},{9,5},{10,6},{11,7},{12,8},{13,9},{1... | collective-permute-start | bytes 393224 | tf_op jit(solution)/shard_map/ppermute | solution.py:51
  273.3 13.9 %collective-permute-start.23 = (f32[256,128]{1,0:T(8,128)}, f32[256,128]{1,0:T(8,128)S(1)}, u32[]{:S(2)}, u32[]{:S(2)}) collective-permute-start(f32[256,128]{1,0:T(8,128)} %copy-done.126), channel_id=1, source_target_pairs={{0,16},{1,17},{2,18},{3,19},{4,20},{5,21},{6,22},{7,23},{8,24},{9,... | collective-permute-start | bytes 393224 | tf_op jit(solution)/shard_map/ppermute | solution.py:52
  275.2 13.5 %collective-permute-start.22 = (f32[256,128]{1,0:T(8,128)}, f32[256,128]{1,0:T(8,128)S(1)}, u32[]{:S(2)}, u32[]{:S(2)}) collective-permute-start(f32[256,128]{1,0:T(8,128)} %copy-done.128), channel_id=1, source_target_pairs={{16,0},{17,1},{18,2},{19,3},{20,4},{21,5},{22,6},{23,7},{24,8},{25... | collective-permute-start | bytes 393224 | tf_op jit(solution)/shard_map/ppermute | solution.py:51
  315.7 18.7 %all-to-all-start.9 = ((f32[32,24,128]{2,1,0:T(8,128)}), f32[32,24,128]{2,1,0:T(8,128)S(1)}, u32[]{:S(2)}, u32[]{:S(2)}) async-start(f32[32,24,128]{2,1,0:T(8,128)} %bitcast.16), calls=%async_computation.9 | async-start | bytes 786432 | tf_op jit(solution)/shard_map/all_to_all | solution.py:323
  351.5 33.8 %all-to-all-start.11 = ((f32[32,32,128]{2,1,0:T(8,128)}), f32[32,32,128]{2,1,0:T(8,128)}, u32[]{:S(2)}, u32[]{:S(2)}) async-start(f32[32,32,128]{2,1,0:T(8,128)} %shard_map.113), calls=%async_computation.11 | async-start | bytes 1048576 | tf_op jit(solution)/shard_map/all_to_all | solution.py:336
  359.0 11.5 %collective-permute-start.25 = (f32[256,128]{1,0:T(8,128)S(1)}, f32[256,128]{1,0:T(8,128)S(1)}, u32[]{:S(2)}, u32[]{:S(2)}) collective-permute-start(f32[256,128]{1,0:T(8,128)S(1)} %get-tuple-element.151.refs_8_), channel_id=1, source_target_pairs={{0,1},{1,2},{2,3},{4,5},{5,6},{6,7},{8,9},{9,10},{10,11},{12,13},{... | collective-permute-start | bytes 393224 | tf_op jit(solution)/shard_map/ppermute | solution.py:52
  361.0 17.2 %collective-permute-start.24 = (f32[256,128]{1,0:T(8,128)S(1)}, f32[256,128]{1,0:T(8,128)S(1)}, u32[]{:S(2)}, u32[]{:S(2)}) collective-permute-start(f32[256,128]{1,0:T(8,128)S(1)} %get-tuple-element.152.refs_9_), channel_id=1, source_target_pairs={{1,0},{2,1},{3,2},{5,4},{6,5},{7,6},{9,8},{10,9},{11,10},{13,12},{... | collective-permute-start | bytes 393224 | tf_op jit(solution)/shard_map/ppermute | solution.py:51
  362.3 16.6 %collective-permute-start.27 = (f32[256,128]{1,0:T(8,128)}, f32[256,128]{1,0:T(8,128)S(1)}, u32[]{:S(2)}, u32[]{:S(2)}) collective-permute-start(f32[256,128]{1,0:T(8,128)} %copy-done.98), channel_id=1, source_target_pairs={{0,4},{1,5},{2,6},{3,7},{4,8},{5,9},{6,10},{7,11},{8,12},{9,13},{1... | collective-permute-start | bytes 393224 | tf_op jit(solution)/shard_map/ppermute | solution.py:52
  367.2 12.4 %collective-permute-start.26 = (f32[256,128]{1,0:T(8,128)}, f32[256,128]{1,0:T(8,128)S(1)}, u32[]{:S(2)}, u32[]{:S(2)}) collective-permute-start(f32[256,128]{1,0:T(8,128)} %copy-done.100), channel_id=1, source_target_pairs={{4,0},{5,1},{6,2},{7,3},{8,4},{9,5},{10,6},{11,7},{12,8},{13,9},{1... | collective-permute-start | bytes 393224 | tf_op jit(solution)/shard_map/ppermute | solution.py:51
  368.5 13.9 %collective-permute-start.29 = (f32[256,128]{1,0:T(8,128)}, f32[256,128]{1,0:T(8,128)S(1)}, u32[]{:S(2)}, u32[]{:S(2)}) collective-permute-start(f32[256,128]{1,0:T(8,128)} %copy-done.102), channel_id=1, source_target_pairs={{0,16},{1,17},{2,18},{3,19},{4,20},{5,21},{6,22},{7,23},{8,24},{9,... | collective-permute-start | bytes 393224 | tf_op jit(solution)/shard_map/ppermute | solution.py:52
  371.1 13.5 %collective-permute-start.28 = (f32[256,128]{1,0:T(8,128)}, f32[256,128]{1,0:T(8,128)S(1)}, u32[]{:S(2)}, u32[]{:S(2)}) collective-permute-start(f32[256,128]{1,0:T(8,128)} %copy-done.104), channel_id=1, source_target_pairs={{16,0},{17,1},{18,2},{19,3},{20,4},{21,5},{22,6},{23,7},{24,8},{25... | collective-permute-start | bytes 393224 | tf_op jit(solution)/shard_map/ppermute | solution.py:51
  413.5 17.1 %all-to-all-start.12 = ((f32[32,24,128]{2,1,0:T(8,128)}), f32[32,24,128]{2,1,0:T(8,128)}, u32[]{:S(2)}, u32[]{:S(2)}) async-start(f32[32,24,128]{2,1,0:T(8,128)} %bitcast.14), calls=%async_computation.12 | async-start | bytes 786432 | tf_op jit(solution)/shard_map/all_to_all | solution.py:323
  448.5 33.5 %all-to-all-start.14 = ((f32[32,32,128]{2,1,0:T(8,128)}), f32[32,32,128]{2,1,0:T(8,128)}, u32[]{:S(2)}, u32[]{:S(2)}) async-start(f32[32,32,128]{2,1,0:T(8,128)} %copy-done.33), calls=%async_computation.14 | async-start | bytes 1048576 | tf_op jit(solution)/shard_map/all_to_all | solution.py:336
  455.7 11.5 %collective-permute-start.31 = (f32[256,128]{1,0:T(8,128)S(1)}, f32[256,128]{1,0:T(8,128)S(1)}, u32[]{:S(2)}, u32[]{:S(2)}) collective-permute-start(f32[256,128]{1,0:T(8,128)S(1)} %get-tuple-element.167.refs_8_), channel_id=1, source_target_pairs={{0,1},{1,2},{2,3},{4,5},{5,6},{6,7},{8,9},{9,10},{10,11},{12,13},{... | collective-permute-start | bytes 393224 | tf_op jit(solution)/shard_map/ppermute | solution.py:52
  457.7 17.0 %collective-permute-start.30 = (f32[256,128]{1,0:T(8,128)S(1)}, f32[256,128]{1,0:T(8,128)S(1)}, u32[]{:S(2)}, u32[]{:S(2)}) collective-permute-start(f32[256,128]{1,0:T(8,128)S(1)} %get-tuple-element.168.refs_9_), channel_id=1, source_target_pairs={{1,0},{2,1},{3,2},{5,4},{6,5},{7,6},{9,8},{10,9},{11,10},{13,12},{... | collective-permute-start | bytes 393224 | tf_op jit(solution)/shard_map/ppermute | solution.py:51
  459.0 16.4 %collective-permute-start.33 = (f32[256,128]{1,0:T(8,128)}, f32[256,128]{1,0:T(8,128)S(1)}, u32[]{:S(2)}, u32[]{:S(2)}) collective-permute-start(f32[256,128]{1,0:T(8,128)} %copy-done.106), channel_id=1, source_target_pairs={{0,4},{1,5},{2,6},{3,7},{4,8},{5,9},{6,10},{7,11},{8,12},{9,13},{1... | collective-permute-start | bytes 393224 | tf_op jit(solution)/shard_map/ppermute | solution.py:52
  463.9 12.1 %collective-permute-start.32 = (f32[256,128]{1,0:T(8,128)}, f32[256,128]{1,0:T(8,128)S(1)}, u32[]{:S(2)}, u32[]{:S(2)}) collective-permute-start(f32[256,128]{1,0:T(8,128)} %copy-done.108), channel_id=1, source_target_pairs={{4,0},{5,1},{6,2},{7,3},{8,4},{9,5},{10,6},{11,7},{12,8},{13,9},{1... | collective-permute-start | bytes 393224 | tf_op jit(solution)/shard_map/ppermute | solution.py:51
  465.2 13.9 %collective-permute-start.35 = (f32[256,128]{1,0:T(8,128)}, f32[256,128]{1,0:T(8,128)S(1)}, u32[]{:S(2)}, u32[]{:S(2)}) collective-permute-start(f32[256,128]{1,0:T(8,128)} %copy-done.110), channel_id=1, source_target_pairs={{0,16},{1,17},{2,18},{3,19},{4,20},{5,21},{6,22},{7,23},{8,24},{9,... | collective-permute-start | bytes 393224 | tf_op jit(solution)/shard_map/ppermute | solution.py:52
  467.8 13.5 %collective-permute-start.34 = (f32[256,128]{1,0:T(8,128)}, f32[256,128]{1,0:T(8,128)S(1)}, u32[]{:S(2)}, u32[]{:S(2)}) collective-permute-start(f32[256,128]{1,0:T(8,128)} %copy-done.112), channel_id=1, source_target_pairs={{16,0},{17,1},{18,2},{19,3},{20,4},{21,5},{22,6},{23,7},{24,8},{25... | collective-permute-start | bytes 393224 | tf_op jit(solution)/shard_map/ppermute | solution.py:51
  (206 other events, 560.6 us)

commit v2 on v1

--- a/solution.py
+++ b/solution.py
@@ -20,6 +20,8 @@
 COARSE = 768
 NEAR = 256
 DOTS = 8
+EARLY = (0, 1, 2)
+LATE = (3, 4, 5)
 PACKED = FD + 2 * CORNERS + 8
 PLACES = np.arange(NSUB).reshape(4, 8, 8)
 PLANES = PLACES.transpose(1, 0, 2).reshape(8, 32).tolist()
@@ -45,15 +47,11 @@
 DOWN = [route(d, -1) for d in range(3)]
 
 
-def swap_faces(blocks):
-    received = []
-    for d in range(3):
-        received.append(lax.ppermute(blocks[2 * d + 1], "sub", DOWN[d]))
-        received.append(lax.ppermute(blocks[2 * d], "sub", UP[d]))
-    return received
-
-
-def call(kernel, outs, inputs, smem=(), scratch=(), flops=0):
+def swap_face(blocks, f):
+    return lax.ppermute(blocks[f ^ 1], "sub", UP[f // 2] if f % 2 else DOWN[f // 2])
+
+
+def call(kernel, outs, inputs, smem=(), anywhere=(), alias={}, scratch=(), flops=0, grant=8):
     shapes = [jax.ShapeDtypeStruct(s, t) for s, t in outs]
     size = sum(int(np.prod(s)) * jnp.dtype(t).itemsize for s, t in outs)
     size += sum(x.size * x.dtype.itemsize for x in inputs)
@@ -61,12 +59,18 @@
         kernel,
         out_shape=shapes,
         in_specs=[
-            pl.BlockSpec(memory_space=pltpu.SMEM if i in smem else pltpu.VMEM)
+            pl.BlockSpec(
+                memory_space=pltpu.SMEM if i in smem else pl.ANY if i in anywhere else pltpu.VMEM
+            )
             for i in range(len(inputs))
         ],
-        out_specs=[pl.BlockSpec(memory_space=pltpu.VMEM)] * len(outs),
+        out_specs=[
+            pl.BlockSpec(memory_space=pl.ANY if i in alias.values() else pltpu.VMEM)
+            for i in range(len(outs))
+        ],
+        input_output_aliases=alias,
         scratch_shapes=list(scratch),
-        compiler_params=pltpu.CompilerParams(vmem_limit_bytes=40 * 2**20),
+        compiler_params=pltpu.CompilerParams(vmem_limit_bytes=grant * 2**20),
         cost_estimate=pl.CostEstimate(flops=flops, bytes_accessed=size, transcendentals=0),
     )(*inputs)
 
@@ -198,14 +202,16 @@
     dots[1:2, :] = bend
 
 
-def fold_plane_kernel(parts, dots, out):
+def fold_plane_kernel(parts, dots, *refs):
+    out = refs[-1]
     total = jnp.sum(parts[...], 0)
     for i in range(LINE):
         out[i, :ROWS, :] = total
         out[i, ROWS:, :] = dots[...]
 
 
-def fold_line_kernel(parts, out):
+def fold_line_kernel(parts, *refs):
+    out = refs[len(refs) // 2]
     total = jnp.sum(parts[...], 0)
     for i in range(PLANE):
         out[i] = total
@@ -293,13 +299,14 @@
         [((CORNERS, DOFS), f32)] + [((PACKED, LOADS), f32)] * FACES,
         [jumps[0], coupling[0], links, ids_row],
     )
-    got = swap_faces(sent)
+    got = [swap_face(sent, f) for f in range(FACES)]
     schur_block, weights = call(
         arrange_kernel,
         [((DOFS, DOFS), bf16), field],
         [schur[0], links, jnp.broadcast_to(scaling[0][:, None], (DOFS, LOADS))],
         scratch=[pltpu.VMEM((DOFS, DOFS), bf16)],
         flops=4 * DOFS * DOFS * FD,
+        grant=16,
     )
     residual, precond, rounded, spread, state = call(
         begin_kernel, [field] + open_outs, [glued, corners, couple, weights, *sent, *got], smem=(0, 1)
@@ -329,11 +336,30 @@
             [schur_block, rounded, precond, state],
             flops=2 * DOFS * DOFS * LOADS,
         )
-        received = swap_faces(local)
-        (lines,) = call(fold_plane_kernel, [((LINE, ROWS + DOTS, LOADS), f32)], [parts, dots])
+        received = [None] * FACES
+        for f in EARLY:
+            received[f] = swap_face(local, f)
+        early = [received[f] for f in EARLY]
+        (lines,) = call(
+            fold_plane_kernel,
+            [((LINE, ROWS + DOTS, LOADS), f32)],
+            [parts, dots, *early],
+            anywhere=range(2, 2 + len(early)),
+        )
         lines = lax.all_to_all(lines, "sub", 0, 0, axis_index_groups=LINES)
-        (whole,) = call(fold_line_kernel, [((PLANE, ROWS + DOTS, LOADS), f32)], [lines])
+        held = [f ^ 1 for f in LATE]
+        whole, *kept = call(
+            fold_line_kernel,
+            [((PLANE, ROWS + DOTS, LOADS), f32)] + [((FD, LOADS), f32)] * len(held),
+            [lines, *[local[f] for f in held]],
+            anywhere=range(1, 1 + len(held)),
+            alias={1 + i: 1 + i for i in range(len(held))},
+        )
+        for f, block in zip(held, kept):
+            local[f] = block
         whole = lax.all_to_all(whole, "sub", 0, 0, axis_index_groups=PLANES)
+        for f in LATE:
+            received[f] = swap_face(local, f)
         inputs = [glued, corners, near_ids, whole, inverse_high, inverse_low, lift_high, lift_low]
         inputs += [*local, *received, weights, precond, residual]
         inputs += [state if first else history]

time: 513 us -> 595 us (1.16)
  local copies, waits for them, and re-layouts: 170 us -> 228 us
  waiting for transfers between devices: 33.3 us -> 67.3 us
    unnamed x415 -> x549, local copies, waits for them, and re-layouts: 170 us -> 228 us
    ppermute x36, waiting for transfers between devices: 24.7 us -> 59 us  [swap_face(): lax.ppermute(blocks[f ^ 1], 'sub', UP[f // 2] if f % 2 else DOWN[f // 2])]
    all_to_all x5, starting transfers between devices: 39.3 us -> 25.1 us  [shards(): lax.all_to_all(spread.reshape(PLANE, ROWS, LOADS), 'sub', 0, 0, axis_inde...]
    ppermute x36, starting transfers between devices: 113 us -> 120 us  [swap_face(): lax.ppermute(blocks[f ^ 1], 'sub', UP[f // 2] if f % 2 else DOWN[f // 2])]
  transfers between devices with their start and end apart: 47 -> 47, of which waited for: 11 -> 15; matrix products, arithmetic and copies ran while one was open for 1% -> 1% of each run, Pallas kernels for 2% -> 2%
where the time goes in v2:
time: 595 us; the launch traced here: 588 us
  local copies, waits for them, and re-layouts  228 us (38%)
  starting transfers between devices  191 us (32%)
  waiting for transfers between devices  67.3 us (11%)
  blocking collectives  59.1 us (10%)
  Pallas kernels  33.8 us (6%)
  other arithmetic  6.95 us (1%)
    unnamed x549, local copies, waits for them, and re-layouts  228 us
    ppermute x36, starting transfers between devices, swap_face(): lax.ppermute(blocks[f ^ 1], 'sub', UP[f // 2] if f % 2 else DOWN[f // 2])  120 us
    all_to_all x4, blocking collectives, shards(): lines = lax.all_to_all(lines, 'sub', 0, 0, axis_index_groups=LINES)  59.1 us
    ppermute x36, waiting for transfers between devices, swap_face(): lax.ppermute(blocks[f ^ 1], 'sub', UP[f // 2] if f % 2 else DOWN[f // 2])  59 us
    all_to_all x5, starting transfers between devices, shards(): whole = lax.all_to_all(whole, 'sub', 0, 0, axis_index_groups=PLANES)  41.9 us
    pallas_call x24, Pallas kernels, call(): pl.pallas_call(kernel, out_shape=shapes, in_specs=[pl.BlockSpec(memory_sp...  33.8 us
    all_to_all x5, starting transfers between devices, shards(): lax.all_to_all(spread.reshape(PLANE, ROWS, LOADS), 'sub', 0, 0, axis_inde...  25.1 us
  transfers between devices with their start and end apart: 47, of which 15 were waited for; matrix products, arithmetic and copies ran while one was open for 1% of the time, Pallas kernels for 2%

profile of v2, /device:TPU:24, one launch (start us, length us, event | category | flops | bytes accessed | tf_op | source)
XLA Modules:
  0.0 588.1 jit_solution(15578212026892813377)
XLA Ops:
  6.0 3.0 collective-permute-start.1
  10.3 6.1 %collective-permute-start.3 = (f32[312,128]{1,0:T(8,128)S(1)}, f32[312,128]{1,0:T(8,128)S(1)}, u32[]{:S(2)}, u32[]{:S(2)}) collective-permute-start(f32[312,128]{1,0:T(8,128)S(1)} %get-tuple-element.114.refs_6_), channel_id=1, source_target_pairs={{0,4},{1,5},{2,6},{3,7},{4,8},{5,9},{6,10},{7,11},{8,12},{9,13},{1... | collective-permute-start | bytes 479240 | tf_op jit(solution)/shard_map/ppermute | solution.py:51
  16.4 8.4 %collective-permute-start.4 = (f32[312,128]{1,0:T(8,128)S(1)}, f32[312,128]{1,0:T(8,128)S(1)}, u32[]{:S(2)}, u32[]{:S(2)}) collective-permute-start(f32[312,128]{1,0:T(8,128)S(1)} %get-tuple-element.115.refs_9_), channel_id=1, source_target_pairs={{16,0},{17,1},{18,2},{19,3},{20,4},{21,5},{22,6},{23,7},{24,8},{25... | collective-permute-start | bytes 479240 | tf_op jit(solution)/shard_map/ppermute | solution.py:51
  27.7 2.3 copy-done.273
  34.0 5.7 collective-permute-done.5.refs_15_.refs_7_
  43.9 5.1 all-to-all-start
  59.5 3.0 collective-permute-start.7
  66.4 6.2 %collective-permute-done.8.refs_2_.refs_16_ = f32[256,128]{1,0:T(8,128)S(1)} collective-permute-done((f32[256,128]{1,0:T(8,128)S(1)}, f32[256,128]{1,0:T(8,128)S(1)}, u32[]{:S(2)}, u32[]{:S(2)}) %collective-permute-start.8) | collective-permute-done | bytes 131104 | tf_op jit(solution)/shard_map/ppermute | solution.py:51
  77.6 4.0 all-to-all-start.1
  83.0 8.3 %all-to-all-done.1.parts = f32[8,32,128]{2,1,0:T(8,128)} async-done(((f32[8,32,128]{2,1,0:T(8,128)}), f32[8,32,128]{2,1,0:T(8,128)}, u32[]{:S(2)}, u32[]{:S(2)}) %all-to-all-start.1) | async-done | bytes 131104 | tf_op jit(solution)/shard_map/all_to_all | solution.py:349
  97.8 8.3 %all-to-all-start.2 = ((f32[32,32,128]{2,1,0:T(8,128)}), f32[32,32,128]{2,1,0:T(8,128)}, u32[]{:S(2)}, u32[]{:S(2)}) async-start(f32[32,32,128]{2,1,0:T(8,128)} %copy-done.166), calls=%async_computation.2 | async-start | bytes 1048576 | tf_op jit(solution)/shard_map/all_to_all | solution.py:360
  107.5 5.5 collective-permute-start.9
  115.0 6.8 %collective-permute-start.10 = (f32[256,128]{1,0:T(8,128)}, f32[256,128]{1,0:T(8,128)}, u32[]{:S(2)}, u32[]{:S(2)}) collective-permute-start(f32[256,128]{1,0:T(8,128)} %copy-done.115), channel_id=1, source_target_pairs={{16,0},{17,1},{18,2},{19,3},{20,4},{21,5},{22,6},{23,7},{24,8},{25... | collective-permute-start | bytes 393224 | tf_op jit(solution)/shard_map/ppermute | solution.py:51
  142.6 3.1 shard_map.102
  152.3 5.0 all-to-all-start.3
  167.7 3.0 collective-permute-start.13
  173.3 7.5 %collective-permute-done.14.refs_2_.refs_16_ = f32[256,128]{1,0:T(8,128)S(1)} collective-permute-done((f32[256,128]{1,0:T(8,128)S(1)}, f32[256,128]{1,0:T(8,128)S(1)}, u32[]{:S(2)}, u32[]{:S(2)}) %collective-permute-start.14) | collective-permute-done | bytes 131104 | tf_op jit(solution)/shard_map/ppermute | solution.py:51
  184.1 12.3 %all_to_all.75.parts = f32[8,32,128]{2,1,0:T(8,128)S(1)} all-to-all(f32[8,32,128]{2,1,0:T(8,128)S(1)} %shard_map.104), channel_id=1, replica_groups={{0,8,16,24,32,40,48,56},{1,9,17,25,33,41,49,57},{2,10,18,26,34,42,50,58..., dimensions={0} | all-to-all | bytes 262144 | tf_op jit(solution)/shard_map/all_to_all | solution.py:349
  201.9 8.5 %all-to-all-start.5 = ((f32[32,32,128]{2,1,0:T(8,128)}), f32[32,32,128]{2,1,0:T(8,128)}, u32[]{:S(2)}, u32[]{:S(2)}) async-start(f32[32,32,128]{2,1,0:T(8,128)} %copy-done.167), calls=%async_computation.5 | async-start | bytes 1048576 | tf_op jit(solution)/shard_map/all_to_all | solution.py:360
  210.4 4.9 collective-permute-start.15
  217.3 6.9 %collective-permute-start.16 = (f32[256,128]{1,0:T(8,128)}, f32[256,128]{1,0:T(8,128)S(1)}, u32[]{:S(2)}, u32[]{:S(2)}) collective-permute-start(f32[256,128]{1,0:T(8,128)} %copy-done.139), channel_id=1, source_target_pairs={{16,0},{17,1},{18,2},{19,3},{20,4},{21,5},{22,6},{23,7},{24,8},{25... | collective-permute-start | bytes 393224 | tf_op jit(solution)/shard_map/ppermute | solution.py:51
  250.1 3.1 shard_map.106
  260.4 5.0 all-to-all-start.6
  276.4 3.0 collective-permute-start.19
  282.0 7.5 %collective-permute-done.20.refs_2_.refs_16_ = f32[256,128]{1,0:T(8,128)S(1)} collective-permute-done((f32[256,128]{1,0:T(8,128)S(1)}, f32[256,128]{1,0:T(8,128)S(1)}, u32[]{:S(2)}, u32[]{:S(2)}) %collective-permute-start.20) | collective-permute-done | bytes 131104 | tf_op jit(solution)/shard_map/ppermute | solution.py:51
  292.8 15.6 %all_to_all.76.parts = f32[8,32,128]{2,1,0:T(8,128)S(1)} all-to-all(f32[8,32,128]{2,1,0:T(8,128)S(1)} %shard_map.108), channel_id=1, replica_groups={{0,8,16,24,32,40,48,56},{1,9,17,25,33,41,49,57},{2,10,18,26,34,42,50,58..., dimensions={0} | all-to-all | bytes 262144 | tf_op jit(solution)/shard_map/all_to_all | solution.py:349
  314.0 8.3 %all-to-all-start.8 = ((f32[32,32,128]{2,1,0:T(8,128)}), f32[32,32,128]{2,1,0:T(8,128)}, u32[]{:S(2)}, u32[]{:S(2)}) async-start(f32[32,32,128]{2,1,0:T(8,128)} %copy-done.168), calls=%async_computation.8 | async-start | bytes 1048576 | tf_op jit(solution)/shard_map/all_to_all | solution.py:360
  322.3 4.9 collective-permute-start.21
  329.2 6.9 %collective-permute-start.22 = (f32[256,128]{1,0:T(8,128)}, f32[256,128]{1,0:T(8,128)S(1)}, u32[]{:S(2)}, u32[]{:S(2)}) collective-permute-start(f32[256,128]{1,0:T(8,128)} %copy-done.151), channel_id=1, source_target_pairs={{16,0},{17,1},{18,2},{19,3},{20,4},{21,5},{22,6},{23,7},{24,8},{25... | collective-permute-start | bytes 393224 | tf_op jit(solution)/shard_map/ppermute | solution.py:51
  362.0 3.1 shard_map.110
  372.3 5.0 all-to-all-start.9
  388.3 3.0 collective-permute-start.25
  393.9 7.5 %collective-permute-done.26.refs_2_.refs_16_ = f32[256,128]{1,0:T(8,128)S(1)} collective-permute-done((f32[256,128]{1,0:T(8,128)S(1)}, f32[256,128]{1,0:T(8,128)S(1)}, u32[]{:S(2)}, u32[]{:S(2)}) %collective-permute-start.26) | collective-permute-done | bytes 131104 | tf_op jit(solution)/shard_map/ppermute | solution.py:51
  404.7 15.6 %all_to_all.77.parts = f32[8,32,128]{2,1,0:T(8,128)S(1)} all-to-all(f32[8,32,128]{2,1,0:T(8,128)S(1)} %shard_map.112), channel_id=1, replica_groups={{0,8,16,24,32,40,48,56},{1,9,17,25,33,41,49,57},{2,10,18,26,34,42,50,58..., dimensions={0} | all-to-all | bytes 262144 | tf_op jit(solution)/shard_map/all_to_all | solution.py:349
  425.9 8.3 %all-to-all-start.11 = ((f32[32,32,128]{2,1,0:T(8,128)}), f32[32,32,128]{2,1,0:T(8,128)}, u32[]{:S(2)}, u32[]{:S(2)}) async-start(f32[32,32,128]{2,1,0:T(8,128)} %copy-done.169), calls=%async_computation.11 | async-start | bytes 1048576 | tf_op jit(solution)/shard_map/all_to_all | solution.py:360
  434.2 4.9 collective-permute-start.27
  441.0 7.2 %collective-permute-start.28 = (f32[256,128]{1,0:T(8,128)}, f32[256,128]{1,0:T(8,128)S(1)}, u32[]{:S(2)}, u32[]{:S(2)}) collective-permute-start(f32[256,128]{1,0:T(8,128)} %copy-done.163), channel_id=1, source_target_pairs={{16,0},{17,1},{18,2},{19,3},{20,4},{21,5},{22,6},{23,7},{24,8},{25... | collective-permute-start | bytes 393224 | tf_op jit(solution)/shard_map/ppermute | solution.py:51
  473.9 3.1 shard_map.114
  484.1 5.0 all-to-all-start.12
  500.3 3.0 collective-permute-start.31
  507.2 6.2 %collective-permute-done.32.refs_2_.refs_16_ = f32[256,128]{1,0:T(8,128)S(1)} collective-permute-done((f32[256,128]{1,0:T(8,128)S(1)}, f32[256,128]{1,0:T(8,128)S(1)}, u32[]{:S(2)}, u32[]{:S(2)}) %collective-permute-start.32) | collective-permute-done | bytes 131104 | tf_op jit(solution)/shard_map/ppermute | solution.py:51
  517.4 15.6 %all_to_all.78.parts = f32[8,32,128]{2,1,0:T(8,128)S(1)} all-to-all(f32[8,32,128]{2,1,0:T(8,128)S(1)} %shard_map.116), channel_id=1, replica_groups={{0,8,16,24,32,40,48,56},{1,9,17,25,33,41,49,57},{2,10,18,26,34,42,50,58..., dimensions={0} | all-to-all | bytes 262144 | tf_op jit(solution)/shard_map/all_to_all | solution.py:349
  538.5 8.3 %all-to-all-start.14 = ((f32[32,32,128]{2,1,0:T(8,128)}), f32[32,32,128]{2,1,0:T(8,128)}, u32[]{:S(2)}, u32[]{:S(2)}) async-start(f32[32,32,128]{2,1,0:T(8,128)} %copy-done.170), calls=%async_computation.14 | async-start | bytes 1048576 | tf_op jit(solution)/shard_map/all_to_all | solution.py:360
  546.9 4.9 collective-permute-start.33
  553.7 6.9 %collective-permute-start.34 = (f32[256,128]{1,0:T(8,128)}, f32[256,128]{1,0:T(8,128)S(1)}, u32[]{:S(2)}, u32[]{:S(2)}) collective-permute-start(f32[256,128]{1,0:T(8,128)} %copy-done.127), channel_id=1, source_target_pairs={{16,0},{17,1},{18,2},{19,3},{20,4},{21,5},{22,6},{23,7},{24,8},{25... | collective-permute-start | bytes 393224 | tf_op jit(solution)/shard_map/ppermute | solution.py:51
  560.7 3.0 collective-permute-done.35.refs_19_
  563.6 2.7 collective-permute-done.34.refs_18_
  583.7 4.3 shard_map.118
  (635 shorter events, 290.3 us)
Async XLA Ops:
  4.7 20.8 %collective-permute-start = (f32[312,128]{1,0:T(8,128)S(1)}, f32[312,128]{1,0:T(8,128)S(1)}, u32[]{:S(2)}, u32[]{:S(2)}) collective-permute-start(f32[312,128]{1,0:T(8,128)S(1)} %get-tuple-element.111.refs_5_), channel_id=1, source_target_pairs={{1,0},{2,1},{3,2},{5,4},{6,5},{7,6},{9,8},{10,9},{11,10},{13,12},{... | collective-permute-start | bytes 479240 | tf_op jit(solution)/shard_map/ppermute | solution.py:51
  6.0 28.0 %collective-permute-start.1 = (f32[312,128]{1,0:T(8,128)S(1)}, f32[312,128]{1,0:T(8,128)S(1)}, u32[]{:S(2)}, u32[]{:S(2)}) collective-permute-start(f32[312,128]{1,0:T(8,128)S(1)} %get-tuple-element.112.refs_4_), channel_id=1, source_target_pairs={{0,1},{1,2},{2,3},{4,5},{5,6},{6,7},{8,9},{9,10},{10,11},{12,13},{... | collective-permute-start | bytes 479240 | tf_op jit(solution)/shard_map/ppermute | solution.py:51
  9.0 24.9 %collective-permute-start.2 = (f32[312,128]{1,0:T(8,128)S(1)}, f32[312,128]{1,0:T(8,128)S(1)}, u32[]{:S(2)}, u32[]{:S(2)}) collective-permute-start(f32[312,128]{1,0:T(8,128)S(1)} %get-tuple-element.113.refs_7_), channel_id=1, source_target_pairs={{4,0},{5,1},{6,2},{7,3},{8,4},{9,5},{10,6},{11,7},{12,8},{13,9},{1... | collective-permute-start | bytes 479240 | tf_op jit(solution)/shard_map/ppermute | solution.py:51
  10.3 23.7 %collective-permute-start.3 = (f32[312,128]{1,0:T(8,128)S(1)}, f32[312,128]{1,0:T(8,128)S(1)}, u32[]{:S(2)}, u32[]{:S(2)}) collective-permute-start(f32[312,128]{1,0:T(8,128)S(1)} %get-tuple-element.114.refs_6_), channel_id=1, source_target_pairs={{0,4},{1,5},{2,6},{3,7},{4,8},{5,9},{6,10},{7,11},{8,12},{9,13},{1... | collective-permute-start | bytes 479240 | tf_op jit(solution)/shard_map/ppermute | solution.py:51
  16.4 17.6 %collective-permute-start.4 = (f32[312,128]{1,0:T(8,128)S(1)}, f32[312,128]{1,0:T(8,128)S(1)}, u32[]{:S(2)}, u32[]{:S(2)}) collective-permute-start(f32[312,128]{1,0:T(8,128)S(1)} %get-tuple-element.115.refs_9_), channel_id=1, source_target_pairs={{16,0},{17,1},{18,2},{19,3},{20,4},{21,5},{22,6},{23,7},{24,8},{25... | collective-permute-start | bytes 479240 | tf_op jit(solution)/shard_map/ppermute | solution.py:51
  25.5 14.2 %collective-permute-start.5 = (f32[312,128]{1,0:T(8,128)S(1)}, f32[312,128]{1,0:T(8,128)S(1)}, u32[]{:S(2)}, u32[]{:S(2)}) collective-permute-start(f32[312,128]{1,0:T(8,128)S(1)} %get-tuple-element.116.refs_8_), channel_id=1, source_target_pairs={{0,16},{1,17},{2,18},{3,19},{4,20},{5,21},{6,22},{7,23},{8,24},{9,... | collective-permute-start | bytes 479240 | tf_op jit(solution)/shard_map/ppermute | solution.py:51
  43.9 29.3 %all-to-all-start = ((f32[32,24,128]{2,1,0:T(8,128)}), f32[32,24,128]{2,1,0:T(8,128)}, u32[]{:S(2)}, u32[]{:S(2)}) async-start(f32[32,24,128]{2,1,0:T(8,128)} %bitcast.3), calls=%async_computation | async-start | bytes 786432 | tf_op jit(solution)/shard_map/all_to_all | solution.py:330
  57.5 7.5 %collective-permute-start.6 = (f32[256,128]{1,0:T(8,128)S(1)}, f32[256,128]{1,0:T(8,128)S(1)}, u32[]{:S(2)}, u32[]{:S(2)}) collective-permute-start(f32[256,128]{1,0:T(8,128)S(1)} %get-tuple-element.125.refs_9_), channel_id=1, source_target_pairs={{1,0},{2,1},{3,2},{5,4},{6,5},{7,6},{9,8},{10,9},{11,10},{13,12},{... | collective-permute-start | bytes 393224 | tf_op jit(solution)/shard_map/ppermute | solution.py:51
  59.5 6.3 %collective-permute-start.7 = (f32[256,128]{1,0:T(8,128)S(1)}, f32[256,128]{1,0:T(8,128)S(1)}, u32[]{:S(2)}, u32[]{:S(2)}) collective-permute-start(f32[256,128]{1,0:T(8,128)S(1)} %get-tuple-element.126.refs_8_), channel_id=1, source_target_pairs={{0,1},{1,2},{2,3},{4,5},{5,6},{6,7},{8,9},{9,10},{10,11},{12,13},{... | collective-permute-start | bytes 393224 | tf_op jit(solution)/shard_map/ppermute | solution.py:51
  63.1 9.4 %collective-permute-start.8 = (f32[256,128]{1,0:T(8,128)S(1)}, f32[256,128]{1,0:T(8,128)S(1)}, u32[]{:S(2)}, u32[]{:S(2)}) collective-permute-start(f32[256,128]{1,0:T(8,128)S(1)} %get-tuple-element.127.refs_11_), channel_id=1, source_target_pairs={{4,0},{5,1},{6,2},{7,3},{8,4},{9,5},{10,6},{11,7},{12,8},{13,9},{1... | collective-permute-start | bytes 393224 | tf_op jit(solution)/shard_map/ppermute | solution.py:51
  77.6 13.7 %all-to-all-start.1 = ((f32[8,32,128]{2,1,0:T(8,128)}), f32[8,32,128]{2,1,0:T(8,128)}, u32[]{:S(2)}, u32[]{:S(2)}) async-start(f32[8,32,128]{2,1,0:T(8,128)} %copy-done.165), calls=%async_computation.1 | async-start | bytes 262144 | tf_op jit(solution)/shard_map/all_to_all | solution.py:349
  97.8 32.1 %all-to-all-start.2 = ((f32[32,32,128]{2,1,0:T(8,128)}), f32[32,32,128]{2,1,0:T(8,128)}, u32[]{:S(2)}, u32[]{:S(2)}) async-start(f32[32,32,128]{2,1,0:T(8,128)} %copy-done.166), calls=%async_computation.2 | async-start | bytes 1048576 | tf_op jit(solution)/shard_map/all_to_all | solution.py:360
  107.5 22.4 %collective-permute-start.9 = (f32[256,128]{1,0:T(8,128)}, f32[256,128]{1,0:T(8,128)}, u32[]{:S(2)}, u32[]{:S(2)}) collective-permute-start(f32[256,128]{1,0:T(8,128)} %copy-done.107), channel_id=1, source_target_pairs={{0,4},{1,5},{2,6},{3,7},{4,8},{5,9},{6,10},{7,11},{8,12},{9,13},{1... | collective-permute-start | bytes 393224 | tf_op jit(solution)/shard_map/ppermute | solution.py:51
  113.0 16.9 %collective-permute-start.11 = (f32[256,128]{1,0:T(8,128)}, f32[256,128]{1,0:T(8,128)}, u32[]{:S(2)}, u32[]{:S(2)}) collective-permute-start(f32[256,128]{1,0:T(8,128)} %copy-done.111), channel_id=1, source_target_pairs={{0,16},{1,17},{2,18},{3,19},{4,20},{5,21},{6,22},{7,23},{8,24},{9,... | collective-permute-start | bytes 393224 | tf_op jit(solution)/shard_map/ppermute | solution.py:51
  115.0 14.9 %collective-permute-start.10 = (f32[256,128]{1,0:T(8,128)}, f32[256,128]{1,0:T(8,128)}, u32[]{:S(2)}, u32[]{:S(2)}) collective-permute-start(f32[256,128]{1,0:T(8,128)} %copy-done.115), channel_id=1, source_target_pairs={{16,0},{17,1},{18,2},{19,3},{20,4},{21,5},{22,6},{23,7},{24,8},{25... | collective-permute-start | bytes 393224 | tf_op jit(solution)/shard_map/ppermute | solution.py:51
  152.3 29.1 %all-to-all-start.3 = ((f32[32,24,128]{2,1,0:T(8,128)}), f32[32,24,128]{2,1,0:T(8,128)}, u32[]{:S(2)}, u32[]{:S(2)}) async-start(f32[32,24,128]{2,1,0:T(8,128)} %bitcast.17), calls=%async_computation.3 | async-start | bytes 786432 | tf_op jit(solution)/shard_map/all_to_all | solution.py:330
  165.8 7.6 %collective-permute-start.12 = (f32[256,128]{1,0:T(8,128)S(1)}, f32[256,128]{1,0:T(8,128)S(1)}, u32[]{:S(2)}, u32[]{:S(2)}) collective-permute-start(f32[256,128]{1,0:T(8,128)S(1)} %get-tuple-element.143.refs_9_), channel_id=1, source_target_pairs={{1,0},{2,1},{3,2},{5,4},{6,5},{7,6},{9,8},{10,9},{11,10},{13,12},{... | collective-permute-start | bytes 393224 | tf_op jit(solution)/shard_map/ppermute | solution.py:51
  167.7 5.6 collective-permute-start.13
  171.4 9.4 %collective-permute-start.14 = (f32[256,128]{1,0:T(8,128)S(1)}, f32[256,128]{1,0:T(8,128)S(1)}, u32[]{:S(2)}, u32[]{:S(2)}) collective-permute-start(f32[256,128]{1,0:T(8,128)S(1)} %get-tuple-element.145.refs_11_), channel_id=1, source_target_pairs={{4,0},{5,1},{6,2},{7,3},{8,4},{9,5},{10,6},{11,7},{12,8},{13,9},{1... | collective-permute-start | bytes 393224 | tf_op jit(solution)/shard_map/ppermute | solution.py:51
  201.9 28.6 %all-to-all-start.5 = ((f32[32,32,128]{2,1,0:T(8,128)}), f32[32,32,128]{2,1,0:T(8,128)}, u32[]{:S(2)}, u32[]{:S(2)}) async-start(f32[32,32,128]{2,1,0:T(8,128)} %copy-done.167), calls=%async_computation.5 | async-start | bytes 1048576 | tf_op jit(solution)/shard_map/all_to_all | solution.py:360
  210.4 13.8 %collective-permute-start.15 = (f32[256,128]{1,0:T(8,128)}, f32[256,128]{1,0:T(8,128)S(1)}, u32[]{:S(2)}, u32[]{:S(2)}) collective-permute-start(f32[256,128]{1,0:T(8,128)} %copy-done.131), channel_id=1, source_target_pairs={{0,4},{1,5},{2,6},{3,7},{4,8},{5,9},{6,10},{7,11},{8,12},{9,13},{1... | collective-permute-start | bytes 393224 | tf_op jit(solution)/shard_map/ppermute | solution.py:51
  215.3 11.8 %collective-permute-start.17 = (f32[256,128]{1,0:T(8,128)}, f32[256,128]{1,0:T(8,128)S(1)}, u32[]{:S(2)}, u32[]{:S(2)}) collective-permute-start(f32[256,128]{1,0:T(8,128)} %copy-done.135), channel_id=1, source_target_pairs={{0,16},{1,17},{2,18},{3,19},{4,20},{5,21},{6,22},{7,23},{8,24},{9,... | collective-permute-start | bytes 393224 | tf_op jit(solution)/shard_map/ppermute | solution.py:51
  217.3 12.6 %collective-permute-start.16 = (f32[256,128]{1,0:T(8,128)}, f32[256,128]{1,0:T(8,128)S(1)}, u32[]{:S(2)}, u32[]{:S(2)}) collective-permute-start(f32[256,128]{1,0:T(8,128)} %copy-done.139), channel_id=1, source_target_pairs={{16,0},{17,1},{18,2},{19,3},{20,4},{21,5},{22,6},{23,7},{24,8},{25... | collective-permute-start | bytes 393224 | tf_op jit(solution)/shard_map/ppermute | solution.py:51
  260.4 29.8 %all-to-all-start.6 = ((f32[32,24,128]{2,1,0:T(8,128)}), f32[32,24,128]{2,1,0:T(8,128)}, u32[]{:S(2)}, u32[]{:S(2)}) async-start(f32[32,24,128]{2,1,0:T(8,128)} %bitcast.15), calls=%async_computation.6 | async-start | bytes 786432 | tf_op jit(solution)/shard_map/all_to_all | solution.py:330
  274.5 7.6 %collective-permute-start.18 = (f32[256,128]{1,0:T(8,128)S(1)}, f32[256,128]{1,0:T(8,128)S(1)}, u32[]{:S(2)}, u32[]{:S(2)}) collective-permute-start(f32[256,128]{1,0:T(8,128)S(1)} %get-tuple-element.163.refs_9_), channel_id=1, source_target_pairs={{1,0},{2,1},{3,2},{5,4},{6,5},{7,6},{9,8},{10,9},{11,10},{13,12},{... | collective-permute-start | bytes 393224 | tf_op jit(solution)/shard_map/ppermute | solution.py:51
  276.4 5.6 collective-permute-start.19
  280.1 9.4 %collective-permute-start.20 = (f32[256,128]{1,0:T(8,128)S(1)}, f32[256,128]{1,0:T(8,128)S(1)}, u32[]{:S(2)}, u32[]{:S(2)}) collective-permute-start(f32[256,128]{1,0:T(8,128)S(1)} %get-tuple-element.165.refs_11_), channel_id=1, source_target_pairs={{4,0},{5,1},{6,2},{7,3},{8,4},{9,5},{10,6},{11,7},{12,8},{13,9},{1... | collective-permute-start | bytes 393224 | tf_op jit(solution)/shard_map/ppermute | solution.py:51
  314.0 28.4 %all-to-all-start.8 = ((f32[32,32,128]{2,1,0:T(8,128)}), f32[32,32,128]{2,1,0:T(8,128)}, u32[]{:S(2)}, u32[]{:S(2)}) async-start(f32[32,32,128]{2,1,0:T(8,128)} %copy-done.168), calls=%async_computation.8 | async-start | bytes 1048576 | tf_op jit(solution)/shard_map/all_to_all | solution.py:360
  322.3 13.8 %collective-permute-start.21 = (f32[256,128]{1,0:T(8,128)}, f32[256,128]{1,0:T(8,128)S(1)}, u32[]{:S(2)}, u32[]{:S(2)}) collective-permute-start(f32[256,128]{1,0:T(8,128)} %copy-done.143), channel_id=1, source_target_pairs={{0,4},{1,5},{2,6},{3,7},{4,8},{5,9},{6,10},{7,11},{8,12},{9,13},{1... | collective-permute-start | bytes 393224 | tf_op jit(solution)/shard_map/ppermute | solution.py:51
  327.2 11.8 %collective-permute-start.23 = (f32[256,128]{1,0:T(8,128)}, f32[256,128]{1,0:T(8,128)S(1)}, u32[]{:S(2)}, u32[]{:S(2)}) collective-permute-start(f32[256,128]{1,0:T(8,128)} %copy-done.147), channel_id=1, source_target_pairs={{0,16},{1,17},{2,18},{3,19},{4,20},{5,21},{6,22},{7,23},{8,24},{9,... | collective-permute-start | bytes 393224 | tf_op jit(solution)/shard_map/ppermute | solution.py:51
  329.2 12.6 %collective-permute-start.22 = (f32[256,128]{1,0:T(8,128)}, f32[256,128]{1,0:T(8,128)S(1)}, u32[]{:S(2)}, u32[]{:S(2)}) collective-permute-start(f32[256,128]{1,0:T(8,128)} %copy-done.151), channel_id=1, source_target_pairs={{16,0},{17,1},{18,2},{19,3},{20,4},{21,5},{22,6},{23,7},{24,8},{25... | collective-permute-start | bytes 393224 | tf_op jit(solution)/shard_map/ppermute | solution.py:51
  372.3 29.8 %all-to-all-start.9 = ((f32[32,24,128]{2,1,0:T(8,128)}), f32[32,24,128]{2,1,0:T(8,128)}, u32[]{:S(2)}, u32[]{:S(2)}) async-start(f32[32,24,128]{2,1,0:T(8,128)} %bitcast.16), calls=%async_computation.9 | async-start | bytes 786432 | tf_op jit(solution)/shard_map/all_to_all | solution.py:330
  386.3 7.6 %collective-permute-start.24 = (f32[256,128]{1,0:T(8,128)S(1)}, f32[256,128]{1,0:T(8,128)S(1)}, u32[]{:S(2)}, u32[]{:S(2)}) collective-permute-start(f32[256,128]{1,0:T(8,128)S(1)} %get-tuple-element.183.refs_9_), channel_id=1, source_target_pairs={{1,0},{2,1},{3,2},{5,4},{6,5},{7,6},{9,8},{10,9},{11,10},{13,12},{... | collective-permute-start | bytes 393224 | tf_op jit(solution)/shard_map/ppermute | solution.py:51
  388.3 5.6 collective-permute-start.25
  392.0 9.4 %collective-permute-start.26 = (f32[256,128]{1,0:T(8,128)S(1)}, f32[256,128]{1,0:T(8,128)S(1)}, u32[]{:S(2)}, u32[]{:S(2)}) collective-permute-start(f32[256,128]{1,0:T(8,128)S(1)} %get-tuple-element.185.refs_11_), channel_id=1, source_target_pairs={{4,0},{5,1},{6,2},{7,3},{8,4},{9,5},{10,6},{11,7},{12,8},{13,9},{1... | collective-permute-start | bytes 393224 | tf_op jit(solution)/shard_map/ppermute | solution.py:51
  425.9 28.4 %all-to-all-start.11 = ((f32[32,32,128]{2,1,0:T(8,128)}), f32[32,32,128]{2,1,0:T(8,128)}, u32[]{:S(2)}, u32[]{:S(2)}) async-start(f32[32,32,128]{2,1,0:T(8,128)} %copy-done.169), calls=%async_computation.11 | async-start | bytes 1048576 | tf_op jit(solution)/shard_map/all_to_all | solution.py:360
  434.2 14.0 %collective-permute-start.27 = (f32[256,128]{1,0:T(8,128)}, f32[256,128]{1,0:T(8,128)S(1)}, u32[]{:S(2)}, u32[]{:S(2)}) collective-permute-start(f32[256,128]{1,0:T(8,128)} %copy-done.155), channel_id=1, source_target_pairs={{0,4},{1,5},{2,6},{3,7},{4,8},{5,9},{6,10},{7,11},{8,12},{9,13},{1... | collective-permute-start | bytes 393224 | tf_op jit(solution)/shard_map/ppermute | solution.py:51
  439.1 11.8 %collective-permute-start.29 = (f32[256,128]{1,0:T(8,128)}, f32[256,128]{1,0:T(8,128)S(1)}, u32[]{:S(2)}, u32[]{:S(2)}) collective-permute-start(f32[256,128]{1,0:T(8,128)} %copy-done.159), channel_id=1, source_target_pairs={{0,16},{1,17},{2,18},{3,19},{4,20},{5,21},{6,22},{7,23},{8,24},{9,... | collective-permute-start | bytes 393224 | tf_op jit(solution)/shard_map/ppermute | solution.py:51
  441.0 12.6 %collective-permute-start.28 = (f32[256,128]{1,0:T(8,128)}, f32[256,128]{1,0:T(8,128)S(1)}, u32[]{:S(2)}, u32[]{:S(2)}) collective-permute-start(f32[256,128]{1,0:T(8,128)} %copy-done.163), channel_id=1, source_target_pairs={{16,0},{17,1},{18,2},{19,3},{20,4},{21,5},{22,6},{23,7},{24,8},{25... | collective-permute-start | bytes 393224 | tf_op jit(solution)/shard_map/ppermute | solution.py:51
  484.1 29.9 %all-to-all-start.12 = ((f32[32,24,128]{2,1,0:T(8,128)}), f32[32,24,128]{2,1,0:T(8,128)S(1)}, u32[]{:S(2)}, u32[]{:S(2)}) async-start(f32[32,24,128]{2,1,0:T(8,128)} %bitcast.14), calls=%async_computation.12 | async-start | bytes 786432 | tf_op jit(solution)/shard_map/all_to_all | solution.py:330
  494.2 72.0 %copy-start.235 = (s32[1,6,256]{2,1,0:T(8,128)S(1)}, s32[1,6,256]{2,1,0:T(8,128)}, u32[]{:S(2)}) copy-start(s32[1,6,256]{2,1,0:T(8,128)} %copy-done.234) | copy-start | bytes 18436
  498.2 7.7 %collective-permute-start.30 = (f32[256,128]{1,0:T(8,128)S(1)}, f32[256,128]{1,0:T(8,128)S(1)}, u32[]{:S(2)}, u32[]{:S(2)}) collective-permute-start(f32[256,128]{1,0:T(8,128)S(1)} %get-tuple-element.203.refs_9_), channel_id=1, source_target_pairs={{1,0},{2,1},{3,2},{5,4},{6,5},{7,6},{9,8},{10,9},{11,10},{13,12},{... | collective-permute-start | bytes 393224 | tf_op jit(solution)/shard_map/ppermute | solution.py:51
  500.3 6.3 %collective-permute-start.31 = (f32[256,128]{1,0:T(8,128)S(1)}, f32[256,128]{1,0:T(8,128)S(1)}, u32[]{:S(2)}, u32[]{:S(2)}) collective-permute-start(f32[256,128]{1,0:T(8,128)S(1)} %get-tuple-element.204.refs_8_), channel_id=1, source_target_pairs={{0,1},{1,2},{2,3},{4,5},{5,6},{6,7},{8,9},{9,10},{10,11},{12,13},{... | collective-permute-start | bytes 393224 | tf_op jit(solution)/shard_map/ppermute | solution.py:51
  503.9 9.4 %collective-permute-start.32 = (f32[256,128]{1,0:T(8,128)S(1)}, f32[256,128]{1,0:T(8,128)S(1)}, u32[]{:S(2)}, u32[]{:S(2)}) collective-permute-start(f32[256,128]{1,0:T(8,128)S(1)} %get-tuple-element.205.refs_11_), channel_id=1, source_target_pairs={{4,0},{5,1},{6,2},{7,3},{8,4},{9,5},{10,6},{11,7},{12,8},{13,9},{1... | collective-permute-start | bytes 393224 | tf_op jit(solution)/shard_map/ppermute | solution.py:51
  538.5 27.8 %all-to-all-start.14 = ((f32[32,32,128]{2,1,0:T(8,128)}), f32[32,32,128]{2,1,0:T(8,128)}, u32[]{:S(2)}, u32[]{:S(2)}) async-start(f32[32,32,128]{2,1,0:T(8,128)} %copy-done.170), calls=%async_computation.14 | async-start | bytes 1048576 | tf_op jit(solution)/shard_map/all_to_all | solution.py:360
  546.9 13.8 %collective-permute-start.33 = (f32[256,128]{1,0:T(8,128)}, f32[256,128]{1,0:T(8,128)S(1)}, u32[]{:S(2)}, u32[]{:S(2)}) collective-permute-start(f32[256,128]{1,0:T(8,128)} %copy-done.119), channel_id=1, source_target_pairs={{0,4},{1,5},{2,6},{3,7},{4,8},{5,9},{6,10},{7,11},{8,12},{9,13},{1... | collective-permute-start | bytes 393224 | tf_op jit(solution)/shard_map/ppermute | solution.py:51
  551.8 11.8 %collective-permute-start.35 = (f32[256,128]{1,0:T(8,128)}, f32[256,128]{1,0:T(8,128)S(1)}, u32[]{:S(2)}, u32[]{:S(2)}) collective-permute-start(f32[256,128]{1,0:T(8,128)} %copy-done.123), channel_id=1, source_target_pairs={{0,16},{1,17},{2,18},{3,19},{4,20},{5,21},{6,22},{7,23},{8,24},{9,... | collective-permute-start | bytes 393224 | tf_op jit(solution)/shard_map/ppermute | solution.py:51
  553.7 12.6 %collective-permute-start.34 = (f32[256,128]{1,0:T(8,128)}, f32[256,128]{1,0:T(8,128)S(1)}, u32[]{:S(2)}, u32[]{:S(2)}) collective-permute-start(f32[256,128]{1,0:T(8,128)} %copy-done.127), channel_id=1, source_target_pairs={{16,0},{17,1},{18,2},{19,3},{20,4},{21,5},{22,6},{23,7},{24,8},{25... | collective-permute-start | bytes 393224 | tf_op jit(solution)/shard_map/ppermute | solution.py:51
  (273 other events, 477.6 us)

commit v3 on v1

v3 whole, which is shorter than its diff:
```python
import functools

import jax
import jax.numpy as jnp
import numpy as np
from jax import lax
from jax.experimental import pallas as pl
from jax.experimental.pallas import tpu as pltpu
from jax.sharding import PartitionSpec as P

ITERS = 5
STRIDES = (1, 4, 16)
GRID = (4, 4, 16)
NSUB = 256
FACES = 6
FD = 256
DOFS = FACES * FD
LOADS = 128
CORNERS = 24
COARSE = 768
NEAR = 256
DOTS = 8
PACKED = FD + 2 * CORNERS + 8
PLACES = np.arange(NSUB).reshape(4, 8, 8)
PLANES = PLACES.transpose(1, 0, 2).reshape(8, 32).tolist()
LINES = PLACES.transpose(0, 2, 1).reshape(32, 8).tolist()
PLANE = 32
LINE = 8
ROWS = COARSE // PLANE
f32 = jnp.float32
bf16 = jnp.bfloat16


def route(direction, sign):
    stride, extent = STRIDES[direction], GRID[direction]
    pairs = []
    for i in range(NSUB):
        place = i // stride % extent
        if 0 <= place + sign < extent:
            pairs.append((i, i + sign * stride))
    return pairs


UP = [route(d, 1) for d in range(3)]
DOWN = [route(d, -1) for d in range(3)]


def swap_faces(blocks):
    received = []
    for d in range(3):
        received.append(lax.ppermute(blocks[2 * d + 1], "sub", DOWN[d]))
        received.append(lax.ppermute(blocks[2 * d], "sub", UP[d]))
    return received


def block_of(shape, kind):
    if kind == "smem":
        return pl.BlockSpec(memory_space=pltpu.SMEM)
    if kind == "rows":
        return pl.BlockSpec((FD, shape[1]), lambda f: (f, 0))
    if kind == "columns":
        return pl.BlockSpec((shape[0], FD), lambda f: (0, f))
    return pl.BlockSpec(shape, lambda f: (0,) * len(shape))


def call(kernel, steps, outs, inputs, scratch=(), flops=0):
    inputs = [x if isinstance(x, tuple) else (x, "whole") for x in inputs]
    outs = [x if len(x) == 3 else (*x, "whole") for x in outs]
    size = sum(int(np.prod(s)) * jnp.dtype(t).itemsize for s, t, _ in outs)
    size += sum(x.size * x.dtype.itemsize for x, _ in inputs)
    return pl.pallas_call(
        kernel,
        grid=(steps,),
        out_shape=[jax.ShapeDtypeStruct(s, t) for s, t, _ in outs],
        in_specs=[block_of(x.shape, kind) for x, kind in inputs],
        out_specs=[block_of(s, kind) for s, _, kind in outs],
        scratch_shapes=list(scratch),
        compiler_params=pltpu.CompilerParams(vmem_limit_bytes=56 * 2**20),
        cost_estimate=pl.CostEstimate(flops=flops, bytes_accessed=size, transcendentals=0),
    )(*[x for x, _ in inputs])


def mm(a, b):
    return lax.dot_general(a, b, (((1,), (0,)), ((), ())), preferred_element_type=f32)


def mm_t(a, b):
    return lax.dot_general(a, b, (((1,), (1,)), ((), ())), preferred_element_type=f32)


def split(values):
    high = values.astype(bf16)
    return high, (values - high.astype(f32)).astype(bf16)


def split3(values):
    high = values.astype(bf16)
    rest = values - high.astype(f32)
    middle = rest.astype(bf16)
    return high, middle, (rest - middle.astype(f32)).astype(bf16)


def face(f):
    return slice(f * FD, (f + 1) * FD)


def order_of(links_ref, f):
    place = lax.broadcasted_iota(jnp.int32, (FD, FD), 0)
    return jnp.where(place == links_ref[f : f + 1, :], 1.0, 0.0).astype(bf16)


def reorder(order, values):
    high, middle, low = split3(values)
    both = mm(order, jnp.concatenate([high, middle], 1))
    return both[:, :LOADS] + both[:, LOADS:] + mm(order, low)


def pack_kernel(jumps, coupling, links, ids, couple, halves, *packs):
    for f in range(FACES):
        part = coupling[:, face(f)]
        jump = jumps[face(f), :]
        if f % 2:
            order = order_of(links, f)
            jump = -reorder(order, jump)
            high, middle, low = split3(part)
            part = -(mm_t(high, order) + mm_t(middle, order) + mm_t(low, order))
        couple[:, face(f)] = part
        high, low = split(part)
        both = jnp.concatenate([high.astype(f32), low.astype(f32)], 0)
        halves[:, face(f)] = both.astype(bf16)
        packs[f][:FD, :] = jump
        packs[f][FD : FD + CORNERS, :] = part[:, :LOADS]
        packs[f][FD + CORNERS : FD + 2 * CORNERS, :] = part[:, LOADS:]
        packs[f][FD + 2 * CORNERS :, :] = ids[...]


def arrange_kernel(schur, links, weights, schur_out, weights_out, half):
    for f in range(FACES):
        if f % 2:
            order = order_of(links, f)
            half[face(f), :] = (-mm(order, schur[face(f), :])).astype(bf16)
            weights_out[face(f), :] = reorder(order, weights[face(f), :])
        else:
            half[face(f), :] = schur[face(f), :]
            weights_out[face(f), :] = weights[face(f), :]
    for f in range(FACES):
        if f % 2:
            order = order_of(links, f)
            schur_out[:, face(f)] = (-mm_t(half[:, face(f)], order)).astype(bf16)
        else:
            schur_out[:, face(f)] = half[:, face(f)]


def lift_kernel(*refs):
    glued, couple = refs[:2]
    packs = refs[2 : 2 + FACES]
    high, low, rows = refs[2 + FACES :]
    step = pl.program_id(0)
    mask = glued[0, step].astype(f32)
    rows[...] = jnp.zeros_like(rows)
    rows[:CORNERS, :] = couple[...] * mask
    for f in range(FACES):

        @pl.when(step == f)
        def _():
            start = CORNERS * (f + 1)
            rows[start : start + CORNERS, :LOADS] = packs[f][FD : FD + CORNERS, :] * mask
            rows[start : start + CORNERS, LOADS:] = (
                packs[f][FD + CORNERS : FD + 2 * CORNERS, :] * mask
            )

    both = split(rows[...].T)
    high[...] = both[0]
    low[...] = both[1]


def open_face(weights, halves, residual, precond, rounded, state, terms):
    now = weights * residual
    precond[...] = now
    high, low = split(now)
    rounded[...] = high
    state[0:1, :] += 0.5 * jnp.sum(now * residual, 0, keepdims=True)
    terms[...] += mm(halves, jnp.concatenate([high, low], 1))


def place_terms(ids, terms, spread):
    total = terms[:, :LOADS] + terms[:, LOADS:]
    total = total[:CORNERS] + total[CORNERS:]
    spread[...] = jnp.zeros_like(spread)
    for j in range(CORNERS):
        spread[pl.ds(ids[0, j], 1), :] = total[j : j + 1]


def begin_kernel(*refs):
    glued, ids, halves, weights = refs[:4]
    sent = refs[4 : 4 + FACES]
    got = refs[4 + FACES : 4 + 2 * FACES]
    residual, precond, rounded, spread, state, terms = refs[4 + 2 * FACES :]
    step = pl.program_id(0)

    @pl.when(step == 0)
    def _():
        state[...] = jnp.zeros_like(state)
        terms[...] = jnp.zeros_like(terms)

    for f in range(FACES):

        @pl.when(step == f)
        def _():
            residual[...] = glued[0, f].astype(f32) * (sent[f][:FD, :] + got[f][:FD, :])

    open_face(weights[...], halves[...], residual[...], precond, rounded, state, terms)

    @pl.when(step == FACES - 1)
    def _():
        place_terms(ids, terms, spread)


def local_kernel(schur, rounded, precond, state, *refs):
    faces, local, dots = refs[:FACES], refs[FACES], refs[FACES + 1]
    step = pl.program_id(0)
    now = mm(schur[...], rounded[...])
    local[...] = now
    for f in range(FACES):

        @pl.when(step == f)
        def _():
            faces[f][...] = now

    @pl.when(step == 0)
    def _():
        dots[...] = state[...]

    dots[1:2, :] += jnp.sum(now * precond[...], 0, keepdims=True)


def fold_plane_kernel(parts, dots, out):
    total = jnp.sum(parts[...], 0)
    for i in range(LINE):
        out[i, :ROWS, :] = total
        out[i, ROWS:, :] = dots[...]


def fold_line_kernel(parts, out):
    total = jnp.sum(parts[...], 0)
    for i in range(PLANE):
        out[i] = total


def advance_kernel(first, last, *refs):
    glued, ids, near_ids, whole, inverse_high, inverse_low, lift_high, lift_low = refs[:8]
    local, got, refs = refs[8], refs[9 : 9 + FACES], refs[9 + FACES :]
    weights, precond, residual, history = refs[:4]
    refs = refs[4:]
    if not first:
        multipliers, direction, image = refs[:3]
        refs = refs[3:]
    if last:
        links, multipliers_out, residual_out = refs[:3]
    else:
        halves, multipliers_out, residual_out, direction_out, image_out = refs[:5]
        history_out, precond_out, rounded, spread, state = refs[5:10]
    solved, near, near_both, scalars, partner, terms = refs[-6:]
    face_id = pl.program_id(0)

    @pl.when(face_id == 0)
    def _():
        coarse = whole[:, :ROWS, :].reshape(COARSE, LOADS)
        sums = jnp.sum(whole[:, ROWS:, :], 0)
        coarse_high, coarse_low = split(coarse)
        both = mm(inverse_high[...], jnp.concatenate([coarse_high, coarse_low], 1))
        solution_rows = both[:, :LOADS] + both[:, LOADS:] + mm(inverse_low[...], coarse_high)
        solved[...] = solution_rows
        near[...] = jnp.zeros_like(near)
        for j in range(CORNERS * (FACES + 1)):
            near[pl.ds(j, 1), :] = solved[pl.ds(near_ids[0, j], 1), :]
        near_high, near_low = split(near[...])
        near_both[...] = jnp.concatenate([near_high, near_low], 1)
        energy = sums[0:1]
        curvature = sums[1:2] + jnp.sum(coarse * solution_rows, 0, keepdims=True)
        if not first:
            ratio = energy / history[0:1, :]
            curvature = curvature + ratio * (2.0 * sums[2:3] + ratio * history[1:2, :])
            scalars[1:2, :] = ratio
        scalars[0:1, :] = energy / curvature
        if not last:
            history_out[0:1, :] = energy
            history_out[1:2, :] = curvature
            state[...] = jnp.zeros_like(state)
            terms[...] = jnp.zeros_like(terms)

    for f in range(FACES):

        @pl.when(face_id == f)
        def _():
            partner[...] = got[f][...]

    mask = glued[0, face_id].astype(f32)
    lift = mm(lift_high[...], near_both[...])
    lift = lift[:, :LOADS] + lift[:, LOADS:] + mm(lift_low[...], near_both[:, :LOADS])
    now = mask * (local[...] + partner[...]) + lift
    way = precond[...]
    step = scalars[0:1, :]
    if not first:
        ratio = scalars[1:2, :]
        now = now + ratio * image[...]
        way = way + ratio * direction[...]
    move = step * way
    if not first:
        move = multipliers[...] + move
    rest = residual[...] - step * now
    if last:
        multipliers_out[...] = move
        residual_out[...] = rest

        @pl.when(face_id % 2 == 1)
        def _():
            place = lax.broadcasted_iota(jnp.int32, (FD, FD), 0)
            order = jnp.where(place == links[pl.ds(face_id, 1), :], 1.0, 0.0).T.astype(bf16)
            multipliers_out[...] = reorder(order, move)
            residual_out[...] = reorder(order, rest)

    else:
        multipliers_out[...] = move
        residual_out[...] = rest
        direction_out[...] = way
        image_out[...] = now
        open_face(weights[...], halves[...], rest, precond_out, rounded, state, terms)
        state[2:3, :] += 0.5 * jnp.sum(weights[...] * rest * now, 0, keepdims=True)

        @pl.when(face_id == FACES - 1)
        def _():
            place_terms(ids, terms, spread)


def shards(jumps, schur, coupling, coarse_inverse, scaling, glued, matching, corners):
    links = matching[0]
    field = ((DOFS, LOADS), f32, "rows")
    small = ((DOTS, LOADS), f32)
    open_outs = [field, ((DOFS, LOADS), bf16, "rows"), ((COARSE, LOADS), f32), small]
    terms = pltpu.VMEM((2 * CORNERS, 2 * LOADS), f32)
    masks = (glued, "smem")
    own_ids = (corners, "smem")

    ids_row = jnp.pad(corners.astype(f32), ((0, 7), (0, LOADS - CORNERS)))
    couple, halves, *sent = call(
        pack_kernel,
        1,
        [((CORNERS, DOFS), f32), ((2 * CORNERS, DOFS), bf16)] + [((PACKED, LOADS), f32)] * FACES,
        [jumps[0], coupling[0], links, ids_row],
    )
    halves = (halves, "columns")
    got = swap_faces(sent)
    schur_block, weights = call(
        arrange_kernel,
        1,
        [((DOFS, DOFS), bf16), ((DOFS, LOADS), f32)],
        [schur[0], links, jnp.broadcast_to(scaling[0][:, None], (DOFS, LOADS))],
        scratch=[pltpu.VMEM((DOFS, DOFS), bf16)],
        flops=4 * DOFS * DOFS * FD,
    )
    weights = (weights, "rows")
    residual, precond, rounded, spread, state = call(
        begin_kernel,
        FACES,
        [field] + open_outs,
        [masks, own_ids, halves, weights, *sent, *got],
        scratch=[terms],
    )
    lift_high, lift_low = call(
        lift_kernel,
        FACES,
        [((DOFS, NEAR), bf16, "rows")] * 2,
        [masks, (couple, "columns"), *got],
        scratch=[pltpu.VMEM((NEAR, FD), f32)],
    )
    near_ids = jnp.concatenate(
        [corners] + [g[FD + 2 * CORNERS :][:1, :CORNERS].astype(jnp.int32) for g in got], 1
    )
    kept = lax.reduce_precision(coarse_inverse, 8, 7)
    inverse_high, inverse_low = kept.astype(bf16), (coarse_inverse - kept).astype(bf16)

    multipliers = direction = image = history = None
    for iteration in range(ITERS):
        first, last = iteration == 0, iteration + 1 == ITERS
        parts = lax.all_to_all(
            spread.reshape(PLANE, ROWS, LOADS), "sub", 0, 0, axis_index_groups=PLANES
        )
        *faces, local, dots = call(
            local_kernel,
            FACES,
            [((FD, LOADS), f32)] * FACES + [field, small],
            [(schur_block, "rows"), rounded, (precond, "rows"), state],
            flops=2 * DOFS * DOFS * LOADS,
        )
        received = swap_faces(faces)
        (lines,) = call(fold_plane_kernel, 1, [((LINE, ROWS + DOTS, LOADS), f32)], [parts, dots])
        lines = lax.all_to_all(lines, "sub", 0, 0, axis_index_groups=LINES)
        (whole,) = call(fold_line_kernel, 1, [((PLANE, ROWS + DOTS, LOADS), f32)], [lines])
        whole = lax.all_to_all(whole, "sub", 0, 0, axis_index_groups=PLANES)
        inputs = [masks, own_ids, (near_ids, "smem"), whole, inverse_high, inverse_low]
        inputs += [(lift_high, "rows"), (lift_low, "rows"), (local, "rows"), *received]
        inputs += [weights, (precond, "rows"), (residual, "rows"), state if first else history]
        if not first:
            inputs += [(multipliers, "rows"), (direction, "rows"), (image, "rows")]
        inputs += [links if last else halves]
        outs = [field, field]
        if not last:
            outs += [field, field, small] + open_outs
        results = call(
            functools.partial(advance_kernel, first, last),
            FACES,
            outs,
            inputs,
            scratch=[
                pltpu.VMEM((COARSE, LOADS), f32),
                pltpu.VMEM((NEAR, LOADS), f32),
                pltpu.VMEM((NEAR, 2 * LOADS), bf16),
                pltpu.VMEM((8, LOADS), f32),
                pltpu.VMEM((FD, LOADS), f32),
                terms,
            ],
        )
        multipliers, residual = results[:2]
        if not last:
            direction, image, history, precond, rounded, spread, state = results[2:]
    return (multipliers[None], residual[None])


def solution(mesh):
    return jax.shard_map(
        shards,
        mesh=mesh,
        in_specs=(
            P("sub", None, None),
            P("sub", None, None),
            P("sub", None, None),
            P(),
            P("sub", None),
            P("sub", None),
            P("sub", None, None),
            P("sub", None),
        ),
        out_specs=(P("sub", None, None), P("sub", None, None)),
        check_vma=False,
    )
```

time: 513 us -> 440 us (0.86)
  local copies, waits for them, and re-layouts: 170 us -> 13 us
  Pallas kernels: 37 us -> 119 us
  waiting for transfers between devices: 33.3 us -> 59.1 us
  starting transfers between devices: 196 us -> 179 us
    unnamed x415 -> x149, local copies, waits for them, and re-layouts: 170 us -> 10.6 us
    pallas_call x24, Pallas kernels: 37 us -> 119 us  [call(): pl.pallas_call(kernel, grid=(steps,), out_shape=[jax.ShapeDtypeStruct(s,...]
    ppermute x18, starting transfers between devices: 58.2 us -> 75.2 us  [swap_faces(): received.append(lax.ppermute(blocks[2 * d], 'sub', UP[d]))]
    ppermute x18, starting transfers between devices: 54.7 us -> 40.1 us  [swap_faces(): received.append(lax.ppermute(blocks[2 * d + 1], 'sub', DOWN[d]))]
    ppermute x18, waiting for transfers between devices: 5.55 us -> 18.6 us  [swap_faces(): received.append(lax.ppermute(blocks[2 * d + 1], 'sub', DOWN[d]))]
    all_to_all x5, starting transfers between devices: 39.3 us -> 28.9 us  [shards(): lax.all_to_all(spread.reshape(PLANE, ROWS, LOADS), 'sub', 0, 0, axis_inde...]
    all_to_all x5, starting transfers between devices: 38.6 us -> 31.1 us  [shards(): whole = lax.all_to_all(whole, 'sub', 0, 0, axis_index_groups=PLANES)]
    ppermute x18, waiting for transfers between devices: 19.2 us -> 26 us  [swap_faces(): received.append(lax.ppermute(blocks[2 * d], 'sub', UP[d]))]
  transfers between devices with their start and end apart: 47 -> 47, of which waited for: 11 -> 15; matrix products, arithmetic and copies ran while one was open for 1% -> 2% of each run, Pallas kernels for 2% -> 11%
where the time goes in v3:
time: 440 us; the launch traced here: 435 us
  starting transfers between devices  179 us (41%)
  Pallas kernels  119 us (27%)
  waiting for transfers between devices  59.1 us (13%)
  blocking collectives  55.9 us (13%)
  local copies, waits for them, and re-layouts  13 us (3%)
  other arithmetic  7.16 us (2%)
    pallas_call x24, Pallas kernels, call(): pl.pallas_call(kernel, grid=(steps,), out_shape=[jax.ShapeDtypeStruct(s,...  119 us
    ppermute x18, starting transfers between devices, swap_faces(): received.append(lax.ppermute(blocks[2 * d], 'sub', UP[d]))  75.2 us
    all_to_all x4, blocking collectives, shards(): lines = lax.all_to_all(lines, 'sub', 0, 0, axis_index_groups=LINES)  55.9 us
    ppermute x18, starting transfers between devices, swap_faces(): received.append(lax.ppermute(blocks[2 * d + 1], 'sub', DOWN[d]))  40.1 us
    all_to_all x5, starting transfers between devices, shards(): whole = lax.all_to_all(whole, 'sub', 0, 0, axis_index_groups=PLANES)  31.1 us
    all_to_all x5, starting transfers between devices, shards(): lax.all_to_all(spread.reshape(PLANE, ROWS, LOADS), 'sub', 0, 0, axis_inde...  28.9 us
    ppermute x18, waiting for transfers between devices, swap_faces(): received.append(lax.ppermute(blocks[2 * d], 'sub', UP[d]))  26 us
    ppermute x18, waiting for transfers between devices, swap_faces(): received.append(lax.ppermute(blocks[2 * d + 1], 'sub', DOWN[d]))  18.6 us
  transfers between devices with their start and end apart: 47, of which 15 were waited for; matrix products, arithmetic and copies ran while one was open for 2% of the time, Pallas kernels for 11%

profile of v3, /device:TPU:24, one launch (start us, length us, event | category | flops | bytes accessed | tf_op | source)
XLA Modules:
  0.0 435.3 jit_solution(17211379810450948746)
XLA Ops:
  11.6 6.1 %collective-permute-start.3 = (f32[312,128]{1,0:T(8,128)}, f32[312,128]{1,0:T(8,128)S(1)}, u32[]{:S(2)}, u32[]{:S(2)}) collective-permute-start(f32[312,128]{1,0:T(8,128)} %get-tuple-element.100.refs_6_), channel_id=1, source_target_pairs={{0,4},{1,5},{2,6},{3,7},{4,8},{5,9},{6,10},{7,11},{8,12},{9,13},{1... | collective-permute-start | bytes 479240 | tf_op jit(solution)/shard_map/ppermute | solution.py:52
  17.6 8.4 %collective-permute-start.4 = (f32[312,128]{1,0:T(8,128)}, f32[312,128]{1,0:T(8,128)S(1)}, u32[]{:S(2)}, u32[]{:S(2)}) collective-permute-start(f32[312,128]{1,0:T(8,128)} %get-tuple-element.101.refs_9_), channel_id=1, source_target_pairs={{16,0},{17,1},{18,2},{19,3},{20,4},{21,5},{22,6},{23,7},{24,8},{25... | collective-permute-start | bytes 479240 | tf_op jit(solution)/shard_map/ppermute | solution.py:51
  29.9 6.7 %shard_map.96 = (bf16[1536,1536]{1,0:T(8,128)(2,1)}, f32[1536,128]{1,0:T(8,128)}) custom-call(bf16[1536,1536]{1,0:T(8,128)(2,1)} %bitcast.23, s32[6,256]{1,0:T(8,128)} %bitcast.21, f32[1536,128]{1,0:T(8,128)} %broadcast_in_dim.14.weights), custom_call_target="tpu_custom_call" | custom-call | flops 2415919104 | bytes 11016192 | tf_op jit(solution)/shard_map/pallas_call | solution.py:71
  36.6 4.5 %collective-permute-done.5.refs_15_.refs_7_ = f32[312,128]{1,0:T(8,128)S(1)} collective-permute-done((f32[312,128]{1,0:T(8,128)}, f32[312,128]{1,0:T(8,128)S(1)}, u32[]{:S(2)}, u32[]{:S(2)}) %collective-permute-start.5) | collective-permute-done | bytes 159776 | tf_op jit(solution)/shard_map/ppermute | solution.py:52
  41.8 5.9 %shard_map.97 = (f32[1536,128]{1,0:T(8,128)}, f32[1536,128]{1,0:T(8,128)}, bf16[1536,128]{1,0:T(8,128)(2,1)}, f32[768,128]{1,0:T(8,128)}, f32[8,128]{1,0:T(8,128)}) custom-call(s32[1,6]{1,0:T(1,128)} %refs_0_.13, s32[1,24]{1,0:T(1,128)} %refs_1_.11, bf16[48,1536]{1,0:T(8,128)(2,1)} %get-tuple-element.103.refs_2_.refs_19_.refs_22_, ...), custom_call_target="tpu_custom_call" | custom-call | bytes 5214328 | tf_op jit(solution)/shard_map/pallas_call | solution.py:71
  47.7 5.1 %all-to-all-start = ((f32[32,24,128]{2,1,0:T(8,128)}), f32[32,24,128]{2,1,0:T(8,128)S(1)}, u32[]{:S(2)}, u32[]{:S(2)}) async-start(f32[32,24,128]{2,1,0:T(8,128)} %bitcast.14), calls=%async_computation | async-start | bytes 786432 | tf_op jit(solution)/shard_map/all_to_all | solution.py:386
  54.5 6.5 %shard_map.98 = (f32[256,128]{1,0:T(8,128)}, f32[256,128]{1,0:T(8,128)}, f32[256,128]{1,0:T(8,128)}, f32[256,128]{1,0:T(8,128)}, f32[256,128]{1,0:T(8,128)}, /*i...) custom-call(bf16[1536,1536]{1,0:T(8,128)(2,1)} %get-tuple-element.106.schur, ...), custom_call_target="tpu_custom_call" | custom-call | flops 603979776 | bytes 7479296 | tf_op jit(solution)/shard_map/pallas_call | solution.py:71
  66.8 6.1 %collective-permute-start.9 = (f32[256,128]{1,0:T(8,128)}, f32[256,128]{1,0:T(8,128)S(1)}, u32[]{:S(2)}, u32[]{:S(2)}) collective-permute-start(f32[256,128]{1,0:T(8,128)} %get-tuple-element.118), channel_id=1, source_target_pairs={{0,4},{1,5},{2,6},{3,7},{4,8},{5,9},{6,10},{7,11},{8,12},{9,13},{1... | collective-permute-start | bytes 393224 | tf_op jit(solution)/shard_map/ppermute | solution.py:52
  72.9 5.9 %collective-permute-start.10 = (f32[256,128]{1,0:T(8,128)}, f32[256,128]{1,0:T(8,128)S(1)}, u32[]{:S(2)}, u32[]{:S(2)}) collective-permute-start(f32[256,128]{1,0:T(8,128)} %get-tuple-element.119), channel_id=1, source_target_pairs={{16,0},{17,1},{18,2},{19,3},{20,4},{21,5},{22,6},{23,7},{24,8},{25... | collective-permute-start | bytes 393224 | tf_op jit(solution)/shard_map/ppermute | solution.py:51
  86.7 8.6 %all-to-all-done.1.parts = f32[8,32,128]{2,1,0:T(8,128)S(1)} async-done(((f32[8,32,128]{2,1,0:T(8,128)}), f32[8,32,128]{2,1,0:T(8,128)S(1)}, u32[]{:S(2)}, u32[]{:S(2)}) %all-to-all-start.1) | async-done | bytes 131104 | tf_op jit(solution)/shard_map/all_to_all | solution.py:398
  97.7 8.0 %all-to-all-start.2 = ((f32[32,32,128]{2,1,0:T(8,128)}), f32[32,32,128]{2,1,0:T(8,128)S(1)}, u32[]{:S(2)}, u32[]{:S(2)}) async-start(f32[32,32,128]{2,1,0:T(8,128)} %shard_map.100), calls=%async_computation.2 | async-start | bytes 1048576 | tf_op jit(solution)/shard_map/all_to_all | solution.py:400
  110.5 4.8 %shard_map.101 = (bf16[1536,256]{1,0:T(8,128)(2,1)}, bf16[1536,256]{1,0:T(8,128)(2,1)}) custom-call(s32[1,6]{1,0:T(1,128)} %refs_0_.13, f32[24,1536]{1,0:T(8,128)} %get-tuple-element.111.refs_1_, f32[312,128]{1,0:T(8,128)} %copy-done.11, f32[312,128]{1,0:T(8,128)} %copy-done.12, f32[312,128]{1,0:T(8,128)} %copy-done.13, f32[312,128]{1,0:T(8,128)} %copy-done.14, ...), custom_call_target="tpu_custom_call" | custom-call | bytes 2678808 | tf_op jit(solution)/shard_map/pallas_call | solution.py:71
  119.7 9.5 %shard_map.102 = (f32[1536,128]{1,0:T(8,128)}, f32[1536,128]{1,0:T(8,128)}, f32[1536,128]{1,0:T(8,128)}, f32[1536,128]{1,0:T(8,128)}, f32[8,128]{1,0:T(8,128)}, ...) custom-call(s32[1,6]{1,0:T(1,128)} %refs_0_.13, s32[1,24]{1,0:T(1,128)} %refs_1_.11, ...), custom_call_target="tpu_custom_call" | custom-call | bytes 13267736 | tf_op jit(solution)/shard_map/pallas_call | solution.py:71
  129.2 7.4 %all-to-all-start.3 = ((f32[32,24,128]{2,1,0:T(8,128)}), f32[32,24,128]{2,1,0:T(8,128)S(1)}, u32[]{:S(2)}, u32[]{:S(2)}) async-start(f32[32,24,128]{2,1,0:T(8,128)} %bitcast.18), calls=%async_computation.3 | async-start | bytes 786432 | tf_op jit(solution)/shard_map/all_to_all | solution.py:386
  136.6 6.5 %shard_map.103 = (f32[256,128]{1,0:T(8,128)}, f32[256,128]{1,0:T(8,128)}, f32[256,128]{1,0:T(8,128)}, f32[256,128]{1,0:T(8,128)}, f32[256,128]{1,0:T(8,128)}, /*...) custom-call(bf16[1536,1536]{1,0:T(8,128)(2,1)} %get-tuple-element.106.schur, ...), custom_call_target="tpu_custom_call" | custom-call | flops 603979776 | bytes 7479296 | tf_op jit(solution)/shard_map/pallas_call | solution.py:71
  147.1 14.0 %all_to_all.75.parts = f32[8,32,128]{2,1,0:T(8,128)} all-to-all(f32[8,32,128]{2,1,0:T(8,128)} %shard_map.104), channel_id=1, replica_groups={{0,8,16,24,32,40,48,56},{1,9,17,25,33,41,49,57},{2,10,18,26,34,42,50,58..., dimensions={0} | all-to-all | bytes 262144 | tf_op jit(solution)/shard_map/all_to_all | solution.py:398
  162.8 5.8 %all-to-all-start.5 = ((f32[32,32,128]{2,1,0:T(8,128)}), f32[32,32,128]{2,1,0:T(8,128)S(1)}, u32[]{:S(2)}, u32[]{:S(2)}) async-start(f32[32,32,128]{2,1,0:T(8,128)} %shard_map.105), calls=%async_computation.5 | async-start | bytes 1048576 | tf_op jit(solution)/shard_map/all_to_all | solution.py:400
  174.3 6.1 %collective-permute-start.15 = (f32[256,128]{1,0:T(8,128)S(1)}, f32[256,128]{1,0:T(8,128)S(1)}, u32[]{:S(2)}, u32[]{:S(2)}) collective-permute-start(f32[256,128]{1,0:T(8,128)S(1)} %copy-done.59), channel_id=1, source_target_pairs={{0,4},{1,5},{2,6},{3,7},{4,8},{5,9},{6,10},{7,11},{8,12},{9,13},{1... | collective-permute-start | bytes 393224 | tf_op jit(solution)/shard_map/ppermute | solution.py:52
  182.9 4.2 collective-permute-start.17
  187.2 5.0 %collective-permute-done.16.refs_13_ = f32[256,128]{1,0:T(8,128)S(1)} collective-permute-done((f32[256,128]{1,0:T(8,128)S(1)}, f32[256,128]{1,0:T(8,128)S(1)}, u32[]{:S(2)}, u32[]{:S(2)}) %collective-permute-start.16) | collective-permute-done | bytes 131104 | tf_op jit(solution)/shard_map/ppermute | solution.py:51
  197.2 10.0 %shard_map.106 = (f32[1536,128]{1,0:T(8,128)}, f32[1536,128]{1,0:T(8,128)}, f32[1536,128]{1,0:T(8,128)}, f32[1536,128]{1,0:T(8,128)}, f32[8,128]{1,0:T(8,128)}, ...) custom-call(s32[1,6]{1,0:T(1,128)} %refs_0_.13, s32[1,24]{1,0:T(1,128)} %refs_1_.11, ...), custom_call_target="tpu_custom_call" | custom-call | bytes 15627032 | tf_op jit(solution)/shard_map/pallas_call | solution.py:71
  207.2 5.5 %all-to-all-start.6 = ((f32[32,24,128]{2,1,0:T(8,128)}), f32[32,24,128]{2,1,0:T(8,128)S(1)}, u32[]{:S(2)}, u32[]{:S(2)}) async-start(f32[32,24,128]{2,1,0:T(8,128)} %bitcast.16), calls=%async_computation.6 | async-start | bytes 786432 | tf_op jit(solution)/shard_map/all_to_all | solution.py:386
  212.7 6.5 %shard_map.107 = (f32[256,128]{1,0:T(8,128)}, f32[256,128]{1,0:T(8,128)}, f32[256,128]{1,0:T(8,128)}, f32[256,128]{1,0:T(8,128)}, f32[256,128]{1,0:T(8,128)}, /*...) custom-call(bf16[1536,1536]{1,0:T(8,128)(2,1)} %get-tuple-element.106.schur, ...), custom_call_target="tpu_custom_call" | custom-call | flops 603979776 | bytes 7479296 | tf_op jit(solution)/shard_map/pallas_call | solution.py:71
  223.2 14.0 %all_to_all.76.parts = f32[8,32,128]{2,1,0:T(8,128)} all-to-all(f32[8,32,128]{2,1,0:T(8,128)} %shard_map.108), channel_id=1, replica_groups={{0,8,16,24,32,40,48,56},{1,9,17,25,33,41,49,57},{2,10,18,26,34,42,50,58..., dimensions={0} | all-to-all | bytes 262144 | tf_op jit(solution)/shard_map/all_to_all | solution.py:398
  239.0 5.8 %all-to-all-start.8 = ((f32[32,32,128]{2,1,0:T(8,128)}), f32[32,32,128]{2,1,0:T(8,128)S(1)}, u32[]{:S(2)}, u32[]{:S(2)}) async-start(f32[32,32,128]{2,1,0:T(8,128)} %shard_map.109), calls=%async_computation.8 | async-start | bytes 1048576 | tf_op jit(solution)/shard_map/all_to_all | solution.py:400
  250.4 6.1 %collective-permute-start.21 = (f32[256,128]{1,0:T(8,128)S(1)}, f32[256,128]{1,0:T(8,128)S(1)}, u32[]{:S(2)}, u32[]{:S(2)}) collective-permute-start(f32[256,128]{1,0:T(8,128)S(1)} %copy-done.60), channel_id=1, source_target_pairs={{0,4},{1,5},{2,6},{3,7},{4,8},{5,9},{6,10},{7,11},{8,12},{9,13},{1... | collective-permute-start | bytes 393224 | tf_op jit(solution)/shard_map/ppermute | solution.py:52
  259.1 4.2 collective-permute-start.23
  263.4 4.6 %collective-permute-done.22.refs_13_ = f32[256,128]{1,0:T(8,128)S(1)} collective-permute-done((f32[256,128]{1,0:T(8,128)S(1)}, f32[256,128]{1,0:T(8,128)S(1)}, u32[]{:S(2)}, u32[]{:S(2)}) %collective-permute-start.22) | collective-permute-done | bytes 131104 | tf_op jit(solution)/shard_map/ppermute | solution.py:51
  268.0 4.5 %collective-permute-done.23.refs_14_ = f32[256,128]{1,0:T(8,128)S(1)} collective-permute-done((f32[256,128]{1,0:T(8,128)S(1)}, f32[256,128]{1,0:T(8,128)S(1)}, u32[]{:S(2)}, u32[]{:S(2)}) %collective-permute-start.23) | collective-permute-done | bytes 131104 | tf_op jit(solution)/shard_map/ppermute | solution.py:52
  273.4 10.1 %shard_map.110 = (f32[1536,128]{1,0:T(8,128)}, f32[1536,128]{1,0:T(8,128)}, f32[1536,128]{1,0:T(8,128)}, f32[1536,128]{1,0:T(8,128)}, f32[8,128]{1,0:T(8,128)}, ...) custom-call(s32[1,6]{1,0:T(1,128)} %refs_0_.13, s32[1,24]{1,0:T(1,128)} %refs_1_.11, ...), custom_call_target="tpu_custom_call" | custom-call | bytes 15627032 | tf_op jit(solution)/shard_map/pallas_call | solution.py:71
  283.4 5.5 %all-to-all-start.9 = ((f32[32,24,128]{2,1,0:T(8,128)}), f32[32,24,128]{2,1,0:T(8,128)S(1)}, u32[]{:S(2)}, u32[]{:S(2)}) async-start(f32[32,24,128]{2,1,0:T(8,128)} %bitcast.17), calls=%async_computation.9 | async-start | bytes 786432 | tf_op jit(solution)/shard_map/all_to_all | solution.py:386
  288.9 6.5 %shard_map.111 = (f32[256,128]{1,0:T(8,128)}, f32[256,128]{1,0:T(8,128)}, f32[256,128]{1,0:T(8,128)}, f32[256,128]{1,0:T(8,128)}, f32[256,128]{1,0:T(8,128)}, /*...) custom-call(bf16[1536,1536]{1,0:T(8,128)(2,1)} %get-tuple-element.106.schur, ...), custom_call_target="tpu_custom_call" | custom-call | flops 603979776 | bytes 7479296 | tf_op jit(solution)/shard_map/pallas_call | solution.py:71
  299.4 14.0 %all_to_all.77.parts = f32[8,32,128]{2,1,0:T(8,128)} all-to-all(f32[8,32,128]{2,1,0:T(8,128)} %shard_map.112), channel_id=1, replica_groups={{0,8,16,24,32,40,48,56},{1,9,17,25,33,41,49,57},{2,10,18,26,34,42,50,58..., dimensions={0} | all-to-all | bytes 262144 | tf_op jit(solution)/shard_map/all_to_all | solution.py:398
  315.1 5.8 %all-to-all-start.11 = ((f32[32,32,128]{2,1,0:T(8,128)}), f32[32,32,128]{2,1,0:T(8,128)S(1)}, u32[]{:S(2)}, u32[]{:S(2)}) async-start(f32[32,32,128]{2,1,0:T(8,128)} %shard_map.113), calls=%async_computation.11 | async-start | bytes 1048576 | tf_op jit(solution)/shard_map/all_to_all | solution.py:400
  326.6 6.1 %collective-permute-start.27 = (f32[256,128]{1,0:T(8,128)S(1)}, f32[256,128]{1,0:T(8,128)S(1)}, u32[]{:S(2)}, u32[]{:S(2)}) collective-permute-start(f32[256,128]{1,0:T(8,128)S(1)} %copy-done.61), channel_id=1, source_target_pairs={{0,4},{1,5},{2,6},{3,7},{4,8},{5,9},{6,10},{7,11},{8,12},{9,13},{1... | collective-permute-start | bytes 393224 | tf_op jit(solution)/shard_map/ppermute | solution.py:52
  335.3 4.2 collective-permute-start.29
  339.5 4.5 %collective-permute-done.28.refs_13_ = f32[256,128]{1,0:T(8,128)S(1)} collective-permute-done((f32[256,128]{1,0:T(8,128)S(1)}, f32[256,128]{1,0:T(8,128)S(1)}, u32[]{:S(2)}, u32[]{:S(2)}) %collective-permute-start.28) | collective-permute-done | bytes 131104 | tf_op jit(solution)/shard_map/ppermute | solution.py:51
  344.0 4.7 %collective-permute-done.29.refs_14_ = f32[256,128]{1,0:T(8,128)S(1)} collective-permute-done((f32[256,128]{1,0:T(8,128)S(1)}, f32[256,128]{1,0:T(8,128)S(1)}, u32[]{:S(2)}, u32[]{:S(2)}) %collective-permute-start.29) | collective-permute-done | bytes 131104 | tf_op jit(solution)/shard_map/ppermute | solution.py:52
  349.5 10.1 %shard_map.114 = (f32[1536,128]{1,0:T(8,128)}, f32[1536,128]{1,0:T(8,128)}, f32[1536,128]{1,0:T(8,128)}, f32[1536,128]{1,0:T(8,128)}, f32[8,128]{1,0:T(8,128)}, ...) custom-call(s32[1,6]{1,0:T(1,128)} %refs_0_.13, s32[1,24]{1,0:T(1,128)} %refs_1_.11, ...), custom_call_target="tpu_custom_call" | custom-call | bytes 15627032 | tf_op jit(solution)/shard_map/pallas_call | solution.py:71
  359.6 5.5 %all-to-all-start.12 = ((f32[32,24,128]{2,1,0:T(8,128)}), f32[32,24,128]{2,1,0:T(8,128)S(1)}, u32[]{:S(2)}, u32[]{:S(2)}) async-start(f32[32,24,128]{2,1,0:T(8,128)} %bitcast.15), calls=%async_computation.12 | async-start | bytes 786432 | tf_op jit(solution)/shard_map/all_to_all | solution.py:386
  365.1 6.5 %shard_map.115 = (f32[256,128]{1,0:T(8,128)}, f32[256,128]{1,0:T(8,128)}, f32[256,128]{1,0:T(8,128)}, f32[256,128]{1,0:T(8,128)}, f32[256,128]{1,0:T(8,128)}, /*...) custom-call(bf16[1536,1536]{1,0:T(8,128)(2,1)} %get-tuple-element.106.schur, ...), custom_call_target="tpu_custom_call" | custom-call | flops 603979776 | bytes 7479296 | tf_op jit(solution)/shard_map/pallas_call | solution.py:71
  375.6 14.0 %all_to_all.78.parts = f32[8,32,128]{2,1,0:T(8,128)} all-to-all(f32[8,32,128]{2,1,0:T(8,128)} %shard_map.116), channel_id=1, replica_groups={{0,8,16,24,32,40,48,56},{1,9,17,25,33,41,49,57},{2,10,18,26,34,42,50,58..., dimensions={0} | all-to-all | bytes 262144 | tf_op jit(solution)/shard_map/all_to_all | solution.py:398
  391.3 5.8 %all-to-all-start.14 = ((f32[32,32,128]{2,1,0:T(8,128)}), f32[32,32,128]{2,1,0:T(8,128)S(1)}, u32[]{:S(2)}, u32[]{:S(2)}) async-start(f32[32,32,128]{2,1,0:T(8,128)} %shard_map.117), calls=%async_computation.14 | async-start | bytes 1048576 | tf_op jit(solution)/shard_map/all_to_all | solution.py:400
  402.8 6.1 %collective-permute-start.33 = (f32[256,128]{1,0:T(8,128)S(1)}, f32[256,128]{1,0:T(8,128)S(1)}, u32[]{:S(2)}, u32[]{:S(2)}) collective-permute-start(f32[256,128]{1,0:T(8,128)S(1)} %copy-done.58), channel_id=1, source_target_pairs={{0,4},{1,5},{2,6},{3,7},{4,8},{5,9},{6,10},{7,11},{8,12},{9,13},{1... | collective-permute-start | bytes 393224 | tf_op jit(solution)/shard_map/ppermute | solution.py:52
  411.5 4.2 collective-permute-start.35
  415.7 4.5 %collective-permute-done.34.refs_13_ = f32[256,128]{1,0:T(8,128)S(1)} collective-permute-done((f32[256,128]{1,0:T(8,128)S(1)}, f32[256,128]{1,0:T(8,128)S(1)}, u32[]{:S(2)}, u32[]{:S(2)}) %collective-permute-start.34) | collective-permute-done | bytes 131104 | tf_op jit(solution)/shard_map/ppermute | solution.py:51
  420.2 4.7 %collective-permute-done.35.refs_14_ = f32[256,128]{1,0:T(8,128)S(1)} collective-permute-done((f32[256,128]{1,0:T(8,128)S(1)}, f32[256,128]{1,0:T(8,128)S(1)}, u32[]{:S(2)}, u32[]{:S(2)}) %collective-permute-start.35) | collective-permute-done | bytes 131104 | tf_op jit(solution)/shard_map/ppermute | solution.py:52
  425.7 9.4 %shard_map.118 = (f32[1536,128]{1,0:T(8,128)}, f32[1536,128]{1,0:T(8,128)}) custom-call(s32[1,6]{1,0:T(1,128)} %refs_0_.13, s32[1,24]{1,0:T(1,128)} %refs_1_.11, s32[1,168]{1,0:T(1,128)} %concatenate.3.refs_2_, f32[32,32,128]{2,1,0:T(8,128)} %copy-done.5, bf16[768,768]{1,0:T(8,128)(2,1)} %get-tuple-element.193.refs_4_, ...), custom_call_target="tpu_custom_call" | custom-call | bytes 12331800 | tf_op jit(solution)/shard_map/pallas_call | solution.py:71
  (235 shorter events, 105.1 us)
Async XLA Ops:
  5.9 20.8 %collective-permute-start = (f32[312,128]{1,0:T(8,128)}, f32[312,128]{1,0:T(8,128)S(1)}, u32[]{:S(2)}, u32[]{:S(2)}) collective-permute-start(f32[312,128]{1,0:T(8,128)} %get-tuple-element.97.refs_5_), channel_id=1, source_target_pairs={{1,0},{2,1},{3,2},{5,4},{6,5},{7,6},{9,8},{10,9},{11,10},{13,12},{... | collective-permute-start | bytes 479240 | tf_op jit(solution)/shard_map/ppermute | solution.py:51
  7.2 29.3 %collective-permute-start.1 = (f32[312,128]{1,0:T(8,128)}, f32[312,128]{1,0:T(8,128)S(1)}, u32[]{:S(2)}, u32[]{:S(2)}) collective-permute-start(f32[312,128]{1,0:T(8,128)} %get-tuple-element.98.refs_4_), channel_id=1, source_target_pairs={{0,1},{1,2},{2,3},{4,5},{5,6},{6,7},{8,9},{9,10},{10,11},{12,13},{... | collective-permute-start | bytes 479240 | tf_op jit(solution)/shard_map/ppermute | solution.py:52
  10.3 26.3 %collective-permute-start.2 = (f32[312,128]{1,0:T(8,128)}, f32[312,128]{1,0:T(8,128)S(1)}, u32[]{:S(2)}, u32[]{:S(2)}) collective-permute-start(f32[312,128]{1,0:T(8,128)} %get-tuple-element.99.refs_7_), channel_id=1, source_target_pairs={{4,0},{5,1},{6,2},{7,3},{8,4},{9,5},{10,6},{11,7},{12,8},{13,9},{1... | collective-permute-start | bytes 479240 | tf_op jit(solution)/shard_map/ppermute | solution.py:51
  11.6 25.0 %collective-permute-start.3 = (f32[312,128]{1,0:T(8,128)}, f32[312,128]{1,0:T(8,128)S(1)}, u32[]{:S(2)}, u32[]{:S(2)}) collective-permute-start(f32[312,128]{1,0:T(8,128)} %get-tuple-element.100.refs_6_), channel_id=1, source_target_pairs={{0,4},{1,5},{2,6},{3,7},{4,8},{5,9},{6,10},{7,11},{8,12},{9,13},{1... | collective-permute-start | bytes 479240 | tf_op jit(solution)/shard_map/ppermute | solution.py:52
  17.6 19.0 %collective-permute-start.4 = (f32[312,128]{1,0:T(8,128)}, f32[312,128]{1,0:T(8,128)S(1)}, u32[]{:S(2)}, u32[]{:S(2)}) collective-permute-start(f32[312,128]{1,0:T(8,128)} %get-tuple-element.101.refs_9_), channel_id=1, source_target_pairs={{16,0},{17,1},{18,2},{19,3},{20,4},{21,5},{22,6},{23,7},{24,8},{25... | collective-permute-start | bytes 479240 | tf_op jit(solution)/shard_map/ppermute | solution.py:51
  26.8 14.4 %collective-permute-start.5 = (f32[312,128]{1,0:T(8,128)}, f32[312,128]{1,0:T(8,128)S(1)}, u32[]{:S(2)}, u32[]{:S(2)}) collective-permute-start(f32[312,128]{1,0:T(8,128)} %get-tuple-element.102.refs_8_), channel_id=1, source_target_pairs={{0,16},{1,17},{2,18},{3,19},{4,20},{5,21},{6,22},{7,23},{8,24},{9,... | collective-permute-start | bytes 479240 | tf_op jit(solution)/shard_map/ppermute | solution.py:52
  47.7 31.8 %all-to-all-start = ((f32[32,24,128]{2,1,0:T(8,128)}), f32[32,24,128]{2,1,0:T(8,128)S(1)}, u32[]{:S(2)}, u32[]{:S(2)}) async-start(f32[32,24,128]{2,1,0:T(8,128)} %bitcast.14), calls=%async_computation | async-start | bytes 786432 | tf_op jit(solution)/shard_map/all_to_all | solution.py:386
  61.1 48.7 %copy-start.48 = (s32[1,24]{1,0:T(1,128)S(1)}, s32[1,24]{1,0:T(1,128)}, u32[]{:S(2)}) copy-start(s32[1,24]{1,0:T(1,128)} %refs_1_.11) | copy-start | bytes 292
  61.1 46.1 %collective-permute-start.6 = (f32[256,128]{1,0:T(8,128)}, f32[256,128]{1,0:T(8,128)S(1)}, u32[]{:S(2)}, u32[]{:S(2)}) collective-permute-start(f32[256,128]{1,0:T(8,128)} %get-tuple-element.115), channel_id=1, source_target_pairs={{1,0},{2,1},{3,2},{5,4},{6,5},{7,6},{9,8},{10,9},{11,10},{13,12},{... | collective-permute-start | bytes 393224 | tf_op jit(solution)/shard_map/ppermute | solution.py:51
  62.5 52.8 %collective-permute-start.7 = (f32[256,128]{1,0:T(8,128)}, f32[256,128]{1,0:T(8,128)S(1)}, u32[]{:S(2)}, u32[]{:S(2)}) collective-permute-start(f32[256,128]{1,0:T(8,128)} %get-tuple-element.116), channel_id=1, source_target_pairs={{0,1},{1,2},{2,3},{4,5},{5,6},{6,7},{8,9},{9,10},{10,11},{12,13},{... | collective-permute-start | bytes 393224 | tf_op jit(solution)/shard_map/ppermute | solution.py:52
  65.5 49.8 %collective-permute-start.8 = (f32[256,128]{1,0:T(8,128)}, f32[256,128]{1,0:T(8,128)S(1)}, u32[]{:S(2)}, u32[]{:S(2)}) collective-permute-start(f32[256,128]{1,0:T(8,128)} %get-tuple-element.117), channel_id=1, source_target_pairs={{4,0},{5,1},{6,2},{7,3},{8,4},{9,5},{10,6},{11,7},{12,8},{13,9},{1... | collective-permute-start | bytes 393224 | tf_op jit(solution)/shard_map/ppermute | solution.py:51
  66.8 48.5 %collective-permute-start.9 = (f32[256,128]{1,0:T(8,128)}, f32[256,128]{1,0:T(8,128)S(1)}, u32[]{:S(2)}, u32[]{:S(2)}) collective-permute-start(f32[256,128]{1,0:T(8,128)} %get-tuple-element.118), channel_id=1, source_target_pairs={{0,4},{1,5},{2,6},{3,7},{4,8},{5,9},{6,10},{7,11},{8,12},{9,13},{1... | collective-permute-start | bytes 393224 | tf_op jit(solution)/shard_map/ppermute | solution.py:52
  72.9 42.5 %collective-permute-start.10 = (f32[256,128]{1,0:T(8,128)}, f32[256,128]{1,0:T(8,128)S(1)}, u32[]{:S(2)}, u32[]{:S(2)}) collective-permute-start(f32[256,128]{1,0:T(8,128)} %get-tuple-element.119), channel_id=1, source_target_pairs={{16,0},{17,1},{18,2},{19,3},{20,4},{21,5},{22,6},{23,7},{24,8},{25... | collective-permute-start | bytes 393224 | tf_op jit(solution)/shard_map/ppermute | solution.py:51
  81.9 13.3 %all-to-all-start.1 = ((f32[8,32,128]{2,1,0:T(8,128)}), f32[8,32,128]{2,1,0:T(8,128)S(1)}, u32[]{:S(2)}, u32[]{:S(2)}) async-start(f32[8,32,128]{2,1,0:T(8,128)} %shard_map.99), calls=%async_computation.1 | async-start | bytes 262144 | tf_op jit(solution)/shard_map/all_to_all | solution.py:398
  97.7 21.1 %all-to-all-start.2 = ((f32[32,32,128]{2,1,0:T(8,128)}), f32[32,32,128]{2,1,0:T(8,128)S(1)}, u32[]{:S(2)}, u32[]{:S(2)}) async-start(f32[32,32,128]{2,1,0:T(8,128)} %shard_map.100), calls=%async_computation.2 | async-start | bytes 1048576 | tf_op jit(solution)/shard_map/all_to_all | solution.py:400
  107.1 11.7 %collective-permute-start.11 = (f32[256,128]{1,0:T(8,128)S(1)}, f32[256,128]{1,0:T(8,128)S(1)}, u32[]{:S(2)}, u32[]{:S(2)}) collective-permute-start(f32[256,128]{1,0:T(8,128)S(1)} %copy-done.49), channel_id=1, source_target_pairs={{0,16},{1,17},{2,18},{3,19},{4,20},{5,21},{6,22},{7,23},{8,24},{9,... | collective-permute-start | bytes 393224 | tf_op jit(solution)/shard_map/ppermute | solution.py:52
  129.2 15.5 %all-to-all-start.3 = ((f32[32,24,128]{2,1,0:T(8,128)}), f32[32,24,128]{2,1,0:T(8,128)S(1)}, u32[]{:S(2)}, u32[]{:S(2)}) async-start(f32[32,24,128]{2,1,0:T(8,128)} %bitcast.18), calls=%async_computation.3 | async-start | bytes 786432 | tf_op jit(solution)/shard_map/all_to_all | solution.py:386
  162.8 33.6 %all-to-all-start.5 = ((f32[32,32,128]{2,1,0:T(8,128)}), f32[32,32,128]{2,1,0:T(8,128)S(1)}, u32[]{:S(2)}, u32[]{:S(2)}) async-start(f32[32,32,128]{2,1,0:T(8,128)} %shard_map.105), calls=%async_computation.5 | async-start | bytes 1048576 | tf_op jit(solution)/shard_map/all_to_all | solution.py:400
  168.6 14.3 %collective-permute-start.12 = (f32[256,128]{1,0:T(8,128)S(1)}, f32[256,128]{1,0:T(8,128)S(1)}, u32[]{:S(2)}, u32[]{:S(2)}) collective-permute-start(f32[256,128]{1,0:T(8,128)S(1)} %copy-done.71), channel_id=1, source_target_pairs={{1,0},{2,1},{3,2},{5,4},{6,5},{7,6},{9,8},{10,9},{11,10},{13,12},{... | collective-permute-start | bytes 393224 | tf_op jit(solution)/shard_map/ppermute | solution.py:51
  169.9 17.2 %collective-permute-start.13 = (f32[256,128]{1,0:T(8,128)S(1)}, f32[256,128]{1,0:T(8,128)S(1)}, u32[]{:S(2)}, u32[]{:S(2)}) collective-permute-start(f32[256,128]{1,0:T(8,128)S(1)} %copy-done.67), channel_id=1, source_target_pairs={{0,1},{1,2},{2,3},{4,5},{5,6},{6,7},{8,9},{9,10},{10,11},{12,13},{... | collective-permute-start | bytes 393224 | tf_op jit(solution)/shard_map/ppermute | solution.py:52
  173.0 14.2 %collective-permute-start.14 = (f32[256,128]{1,0:T(8,128)S(1)}, f32[256,128]{1,0:T(8,128)S(1)}, u32[]{:S(2)}, u32[]{:S(2)}) collective-permute-start(f32[256,128]{1,0:T(8,128)S(1)} %copy-done.63), channel_id=1, source_target_pairs={{4,0},{5,1},{6,2},{7,3},{8,4},{9,5},{10,6},{11,7},{12,8},{13,9},{1... | collective-permute-start | bytes 393224 | tf_op jit(solution)/shard_map/ppermute | solution.py:51
  174.3 12.9 %collective-permute-start.15 = (f32[256,128]{1,0:T(8,128)S(1)}, f32[256,128]{1,0:T(8,128)S(1)}, u32[]{:S(2)}, u32[]{:S(2)}) collective-permute-start(f32[256,128]{1,0:T(8,128)S(1)} %copy-done.59), channel_id=1, source_target_pairs={{0,4},{1,5},{2,6},{3,7},{4,8},{5,9},{6,10},{7,11},{8,12},{9,13},{1... | collective-permute-start | bytes 393224 | tf_op jit(solution)/shard_map/ppermute | solution.py:52
  180.3 11.8 %collective-permute-start.16 = (f32[256,128]{1,0:T(8,128)S(1)}, f32[256,128]{1,0:T(8,128)S(1)}, u32[]{:S(2)}, u32[]{:S(2)}) collective-permute-start(f32[256,128]{1,0:T(8,128)S(1)} %copy-done.55), channel_id=1, source_target_pairs={{16,0},{17,1},{18,2},{19,3},{20,4},{21,5},{22,6},{23,7},{24,8},{25... | collective-permute-start | bytes 393224 | tf_op jit(solution)/shard_map/ppermute | solution.py:51
  182.9 13.4 %collective-permute-start.17 = (f32[256,128]{1,0:T(8,128)S(1)}, f32[256,128]{1,0:T(8,128)S(1)}, u32[]{:S(2)}, u32[]{:S(2)}) collective-permute-start(f32[256,128]{1,0:T(8,128)S(1)} %copy-done.51), channel_id=1, source_target_pairs={{0,16},{1,17},{2,18},{3,19},{4,20},{5,21},{6,22},{7,23},{8,24},{9,... | collective-permute-start | bytes 393224 | tf_op jit(solution)/shard_map/ppermute | solution.py:52
  207.2 13.6 %all-to-all-start.6 = ((f32[32,24,128]{2,1,0:T(8,128)}), f32[32,24,128]{2,1,0:T(8,128)S(1)}, u32[]{:S(2)}, u32[]{:S(2)}) async-start(f32[32,24,128]{2,1,0:T(8,128)} %bitcast.16), calls=%async_computation.6 | async-start | bytes 786432 | tf_op jit(solution)/shard_map/all_to_all | solution.py:386
  239.0 33.6 %all-to-all-start.8 = ((f32[32,32,128]{2,1,0:T(8,128)}), f32[32,32,128]{2,1,0:T(8,128)S(1)}, u32[]{:S(2)}, u32[]{:S(2)}) async-start(f32[32,32,128]{2,1,0:T(8,128)} %shard_map.109), calls=%async_computation.8 | async-start | bytes 1048576 | tf_op jit(solution)/shard_map/all_to_all | solution.py:400
  244.8 14.3 %collective-permute-start.18 = (f32[256,128]{1,0:T(8,128)S(1)}, f32[256,128]{1,0:T(8,128)S(1)}, u32[]{:S(2)}, u32[]{:S(2)}) collective-permute-start(f32[256,128]{1,0:T(8,128)S(1)} %copy-done.72), channel_id=1, source_target_pairs={{1,0},{2,1},{3,2},{5,4},{6,5},{7,6},{9,8},{10,9},{11,10},{13,12},{... | collective-permute-start | bytes 393224 | tf_op jit(solution)/shard_map/ppermute | solution.py:51
  246.1 17.2 %collective-permute-start.19 = (f32[256,128]{1,0:T(8,128)S(1)}, f32[256,128]{1,0:T(8,128)S(1)}, u32[]{:S(2)}, u32[]{:S(2)}) collective-permute-start(f32[256,128]{1,0:T(8,128)S(1)} %copy-done.68), channel_id=1, source_target_pairs={{0,1},{1,2},{2,3},{4,5},{5,6},{6,7},{8,9},{9,10},{10,11},{12,13},{... | collective-permute-start | bytes 393224 | tf_op jit(solution)/shard_map/ppermute | solution.py:52
  249.1 14.2 %collective-permute-start.20 = (f32[256,128]{1,0:T(8,128)S(1)}, f32[256,128]{1,0:T(8,128)S(1)}, u32[]{:S(2)}, u32[]{:S(2)}) collective-permute-start(f32[256,128]{1,0:T(8,128)S(1)} %copy-done.64), channel_id=1, source_target_pairs={{4,0},{5,1},{6,2},{7,3},{8,4},{9,5},{10,6},{11,7},{12,8},{13,9},{1... | collective-permute-start | bytes 393224 | tf_op jit(solution)/shard_map/ppermute | solution.py:51
  250.4 12.9 %collective-permute-start.21 = (f32[256,128]{1,0:T(8,128)S(1)}, f32[256,128]{1,0:T(8,128)S(1)}, u32[]{:S(2)}, u32[]{:S(2)}) collective-permute-start(f32[256,128]{1,0:T(8,128)S(1)} %copy-done.60), channel_id=1, source_target_pairs={{0,4},{1,5},{2,6},{3,7},{4,8},{5,9},{6,10},{7,11},{8,12},{9,13},{1... | collective-permute-start | bytes 393224 | tf_op jit(solution)/shard_map/ppermute | solution.py:52
  256.5 11.5 %collective-permute-start.22 = (f32[256,128]{1,0:T(8,128)S(1)}, f32[256,128]{1,0:T(8,128)S(1)}, u32[]{:S(2)}, u32[]{:S(2)}) collective-permute-start(f32[256,128]{1,0:T(8,128)S(1)} %copy-done.56), channel_id=1, source_target_pairs={{16,0},{17,1},{18,2},{19,3},{20,4},{21,5},{22,6},{23,7},{24,8},{25... | collective-permute-start | bytes 393224 | tf_op jit(solution)/shard_map/ppermute | solution.py:51
  259.1 13.4 %collective-permute-start.23 = (f32[256,128]{1,0:T(8,128)S(1)}, f32[256,128]{1,0:T(8,128)S(1)}, u32[]{:S(2)}, u32[]{:S(2)}) collective-permute-start(f32[256,128]{1,0:T(8,128)S(1)} %copy-done.52), channel_id=1, source_target_pairs={{0,16},{1,17},{2,18},{3,19},{4,20},{5,21},{6,22},{7,23},{8,24},{9,... | collective-permute-start | bytes 393224 | tf_op jit(solution)/shard_map/ppermute | solution.py:52
  283.4 13.6 %all-to-all-start.9 = ((f32[32,24,128]{2,1,0:T(8,128)}), f32[32,24,128]{2,1,0:T(8,128)S(1)}, u32[]{:S(2)}, u32[]{:S(2)}) async-start(f32[32,24,128]{2,1,0:T(8,128)} %bitcast.17), calls=%async_computation.9 | async-start | bytes 786432 | tf_op jit(solution)/shard_map/all_to_all | solution.py:386
  315.1 33.5 %all-to-all-start.11 = ((f32[32,32,128]{2,1,0:T(8,128)}), f32[32,32,128]{2,1,0:T(8,128)S(1)}, u32[]{:S(2)}, u32[]{:S(2)}) async-start(f32[32,32,128]{2,1,0:T(8,128)} %shard_map.113), calls=%async_computation.11 | async-start | bytes 1048576 | tf_op jit(solution)/shard_map/all_to_all | solution.py:400
  320.9 14.3 %collective-permute-start.24 = (f32[256,128]{1,0:T(8,128)S(1)}, f32[256,128]{1,0:T(8,128)S(1)}, u32[]{:S(2)}, u32[]{:S(2)}) collective-permute-start(f32[256,128]{1,0:T(8,128)S(1)} %copy-done.73), channel_id=1, source_target_pairs={{1,0},{2,1},{3,2},{5,4},{6,5},{7,6},{9,8},{10,9},{11,10},{13,12},{... | collective-permute-start | bytes 393224 | tf_op jit(solution)/shard_map/ppermute | solution.py:51
  322.3 17.2 %collective-permute-start.25 = (f32[256,128]{1,0:T(8,128)S(1)}, f32[256,128]{1,0:T(8,128)S(1)}, u32[]{:S(2)}, u32[]{:S(2)}) collective-permute-start(f32[256,128]{1,0:T(8,128)S(1)} %copy-done.69), channel_id=1, source_target_pairs={{0,1},{1,2},{2,3},{4,5},{5,6},{6,7},{8,9},{9,10},{10,11},{12,13},{... | collective-permute-start | bytes 393224 | tf_op jit(solution)/shard_map/ppermute | solution.py:52
  325.3 14.2 %collective-permute-start.26 = (f32[256,128]{1,0:T(8,128)S(1)}, f32[256,128]{1,0:T(8,128)S(1)}, u32[]{:S(2)}, u32[]{:S(2)}) collective-permute-start(f32[256,128]{1,0:T(8,128)S(1)} %copy-done.65), channel_id=1, source_target_pairs={{4,0},{5,1},{6,2},{7,3},{8,4},{9,5},{10,6},{11,7},{12,8},{13,9},{1... | collective-permute-start | bytes 393224 | tf_op jit(solution)/shard_map/ppermute | solution.py:51
  326.6 12.9 %collective-permute-start.27 = (f32[256,128]{1,0:T(8,128)S(1)}, f32[256,128]{1,0:T(8,128)S(1)}, u32[]{:S(2)}, u32[]{:S(2)}) collective-permute-start(f32[256,128]{1,0:T(8,128)S(1)} %copy-done.61), channel_id=1, source_target_pairs={{0,4},{1,5},{2,6},{3,7},{4,8},{5,9},{6,10},{7,11},{8,12},{9,13},{1... | collective-permute-start | bytes 393224 | tf_op jit(solution)/shard_map/ppermute | solution.py:52
  332.7 11.3 %collective-permute-start.28 = (f32[256,128]{1,0:T(8,128)S(1)}, f32[256,128]{1,0:T(8,128)S(1)}, u32[]{:S(2)}, u32[]{:S(2)}) collective-permute-start(f32[256,128]{1,0:T(8,128)S(1)} %copy-done.57), channel_id=1, source_target_pairs={{16,0},{17,1},{18,2},{19,3},{20,4},{21,5},{22,6},{23,7},{24,8},{25... | collective-permute-start | bytes 393224 | tf_op jit(solution)/shard_map/ppermute | solution.py:51
  335.3 13.4 %collective-permute-start.29 = (f32[256,128]{1,0:T(8,128)S(1)}, f32[256,128]{1,0:T(8,128)S(1)}, u32[]{:S(2)}, u32[]{:S(2)}) collective-permute-start(f32[256,128]{1,0:T(8,128)S(1)} %copy-done.53), channel_id=1, source_target_pairs={{0,16},{1,17},{2,18},{3,19},{4,20},{5,21},{6,22},{7,23},{8,24},{9,... | collective-permute-start | bytes 393224 | tf_op jit(solution)/shard_map/ppermute | solution.py:52
  359.6 13.6 %all-to-all-start.12 = ((f32[32,24,128]{2,1,0:T(8,128)}), f32[32,24,128]{2,1,0:T(8,128)S(1)}, u32[]{:S(2)}, u32[]{:S(2)}) async-start(f32[32,24,128]{2,1,0:T(8,128)} %bitcast.15), calls=%async_computation.12 | async-start | bytes 786432 | tf_op jit(solution)/shard_map/all_to_all | solution.py:386
  391.3 33.6 %all-to-all-start.14 = ((f32[32,32,128]{2,1,0:T(8,128)}), f32[32,32,128]{2,1,0:T(8,128)S(1)}, u32[]{:S(2)}, u32[]{:S(2)}) async-start(f32[32,32,128]{2,1,0:T(8,128)} %shard_map.117), calls=%async_computation.14 | async-start | bytes 1048576 | tf_op jit(solution)/shard_map/all_to_all | solution.py:400
  397.1 14.3 %collective-permute-start.30 = (f32[256,128]{1,0:T(8,128)S(1)}, f32[256,128]{1,0:T(8,128)S(1)}, u32[]{:S(2)}, u32[]{:S(2)}) collective-permute-start(f32[256,128]{1,0:T(8,128)S(1)} %copy-done.70), channel_id=1, source_target_pairs={{1,0},{2,1},{3,2},{5,4},{6,5},{7,6},{9,8},{10,9},{11,10},{13,12},{... | collective-permute-start | bytes 393224 | tf_op jit(solution)/shard_map/ppermute | solution.py:51
  398.4 17.2 %collective-permute-start.31 = (f32[256,128]{1,0:T(8,128)S(1)}, f32[256,128]{1,0:T(8,128)S(1)}, u32[]{:S(2)}, u32[]{:S(2)}) collective-permute-start(f32[256,128]{1,0:T(8,128)S(1)} %copy-done.66), channel_id=1, source_target_pairs={{0,1},{1,2},{2,3},{4,5},{5,6},{6,7},{8,9},{9,10},{10,11},{12,13},{... | collective-permute-start | bytes 393224 | tf_op jit(solution)/shard_map/ppermute | solution.py:52
  401.5 14.2 %collective-permute-start.32 = (f32[256,128]{1,0:T(8,128)S(1)}, f32[256,128]{1,0:T(8,128)S(1)}, u32[]{:S(2)}, u32[]{:S(2)}) collective-permute-start(f32[256,128]{1,0:T(8,128)S(1)} %copy-done.62), channel_id=1, source_target_pairs={{4,0},{5,1},{6,2},{7,3},{8,4},{9,5},{10,6},{11,7},{12,8},{13,9},{1... | collective-permute-start | bytes 393224 | tf_op jit(solution)/shard_map/ppermute | solution.py:51
  402.8 12.9 %collective-permute-start.33 = (f32[256,128]{1,0:T(8,128)S(1)}, f32[256,128]{1,0:T(8,128)S(1)}, u32[]{:S(2)}, u32[]{:S(2)}) collective-permute-start(f32[256,128]{1,0:T(8,128)S(1)} %copy-done.58), channel_id=1, source_target_pairs={{0,4},{1,5},{2,6},{3,7},{4,8},{5,9},{6,10},{7,11},{8,12},{9,13},{1... | collective-permute-start | bytes 393224 | tf_op jit(solution)/shard_map/ppermute | solution.py:52
  408.9 11.3 %collective-permute-start.34 = (f32[256,128]{1,0:T(8,128)S(1)}, f32[256,128]{1,0:T(8,128)S(1)}, u32[]{:S(2)}, u32[]{:S(2)}) collective-permute-start(f32[256,128]{1,0:T(8,128)S(1)} %copy-done.54), channel_id=1, source_target_pairs={{16,0},{17,1},{18,2},{19,3},{20,4},{21,5},{22,6},{23,7},{24,8},{25... | collective-permute-start | bytes 393224 | tf_op jit(solution)/shard_map/ppermute | solution.py:51
  411.5 13.4 %collective-permute-start.35 = (f32[256,128]{1,0:T(8,128)S(1)}, f32[256,128]{1,0:T(8,128)S(1)}, u32[]{:S(2)}, u32[]{:S(2)}) collective-permute-start(f32[256,128]{1,0:T(8,128)S(1)} %copy-done.50), channel_id=1, source_target_pairs={{0,16},{1,17},{2,18},{3,19},{4,20},{5,21},{6,22},{7,23},{8,24},{9,... | collective-permute-start | bytes 393224 | tf_op jit(solution)/shard_map/ppermute | solution.py:52
  (73 other events, 1072.1 us)

commit v4 on v3

--- a/solution.py
+++ b/solution.py
@@ -46,10 +46,11 @@
 
 
 def swap_faces(blocks):
-    received = []
+    received = [None] * FACES
     for d in range(3):
-        received.append(lax.ppermute(blocks[2 * d + 1], "sub", DOWN[d]))
-        received.append(lax.ppermute(blocks[2 * d], "sub", UP[d]))
+        received[2 * d] = lax.ppermute(blocks[2 * d + 1], "sub", DOWN[d])
+    for d in range(3):
+        received[2 * d + 1] = lax.ppermute(blocks[2 * d], "sub", UP[d])
     return received
 
 

time: 440 us -> 440 us (level)
  no operation moved by 1% of the time
where the time goes in v4:
time: 440 us; the launch traced here: 435 us
  starting transfers between devices  179 us (41%)
  Pallas kernels  119 us (27%)
  waiting for transfers between devices  59.1 us (13%)
  blocking collectives  55.9 us (13%)
  local copies, waits for them, and re-layouts  13 us (3%)
  other arithmetic  7.16 us (2%)
    pallas_call x24, Pallas kernels, call(): pl.pallas_call(kernel, grid=(steps,), out_shape=[jax.ShapeDtypeStruct(s,...  119 us
    ppermute x18, starting transfers between devices, swap_faces(): received[2 * d + 1] = lax.ppermute(blocks[2 * d], 'sub', UP[d])  75.2 us
    all_to_all x4, blocking collectives, shards(): lines = lax.all_to_all(lines, 'sub', 0, 0, axis_index_groups=LINES)  55.9 us
    ppermute x18, starting transfers between devices, swap_faces(): received[2 * d] = lax.ppermute(blocks[2 * d + 1], 'sub', DOWN[d])  40.1 us
    all_to_all x5, starting transfers between devices, shards(): whole = lax.all_to_all(whole, 'sub', 0, 0, axis_index_groups=PLANES)  31.1 us
    all_to_all x5, starting transfers between devices, shards(): lax.all_to_all(spread.reshape(PLANE, ROWS, LOADS), 'sub', 0, 0, axis_inde...  28.9 us
    ppermute x18, waiting for transfers between devices, swap_faces(): received[2 * d + 1] = lax.ppermute(blocks[2 * d], 'sub', UP[d])  26 us
    ppermute x18, waiting for transfers between devices, swap_faces(): received[2 * d] = lax.ppermute(blocks[2 * d + 1], 'sub', DOWN[d])  18.6 us
  transfers between devices with their start and end apart: 47, of which 15 were waited for; matrix products, arithmetic and copies ran while one was open for 2% of the time, Pallas kernels for 11%

profile of v4, /device:TPU:24, one launch (start us, length us, event | category | flops | bytes accessed | tf_op | source)
XLA Modules:
  0.0 435.3 jit_solution(17211379810450948746)
XLA Ops:
  11.6 6.1 %collective-permute-start.3 = (f32[312,128]{1,0:T(8,128)}, f32[312,128]{1,0:T(8,128)S(1)}, u32[]{:S(2)}, u32[]{:S(2)}) collective-permute-start(f32[312,128]{1,0:T(8,128)} %get-tuple-element.100.refs_6_), channel_id=1, source_target_pairs={{0,4},{1,5},{2,6},{3,7},{4,8},{5,9},{6,10},{7,11},{8,12},{9,13},{1... | collective-permute-start | bytes 479240 | tf_op jit(solution)/shard_map/ppermute | solution.py:53
  17.6 8.4 %collective-permute-start.4 = (f32[312,128]{1,0:T(8,128)}, f32[312,128]{1,0:T(8,128)S(1)}, u32[]{:S(2)}, u32[]{:S(2)}) collective-permute-start(f32[312,128]{1,0:T(8,128)} %get-tuple-element.101.refs_9_), channel_id=1, source_target_pairs={{16,0},{17,1},{18,2},{19,3},{20,4},{21,5},{22,6},{23,7},{24,8},{25... | collective-permute-start | bytes 479240 | tf_op jit(solution)/shard_map/ppermute | solution.py:51
  29.9 6.7 %shard_map.96 = (bf16[1536,1536]{1,0:T(8,128)(2,1)}, f32[1536,128]{1,0:T(8,128)}) custom-call(bf16[1536,1536]{1,0:T(8,128)(2,1)} %bitcast.23, s32[6,256]{1,0:T(8,128)} %bitcast.21, f32[1536,128]{1,0:T(8,128)} %broadcast_in_dim.14.weights), custom_call_target="tpu_custom_call" | custom-call | flops 2415919104 | bytes 11016192 | tf_op jit(solution)/shard_map/pallas_call | solution.py:72
  36.6 4.5 %collective-permute-done.5.refs_15_.refs_7_ = f32[312,128]{1,0:T(8,128)S(1)} collective-permute-done((f32[312,128]{1,0:T(8,128)}, f32[312,128]{1,0:T(8,128)S(1)}, u32[]{:S(2)}, u32[]{:S(2)}) %collective-permute-start.5) | collective-permute-done | bytes 159776 | tf_op jit(solution)/shard_map/ppermute | solution.py:53
  41.8 5.9 %shard_map.97 = (f32[1536,128]{1,0:T(8,128)}, f32[1536,128]{1,0:T(8,128)}, bf16[1536,128]{1,0:T(8,128)(2,1)}, f32[768,128]{1,0:T(8,128)}, f32[8,128]{1,0:T(8,128)}) custom-call(s32[1,6]{1,0:T(1,128)} %refs_0_.13, s32[1,24]{1,0:T(1,128)} %refs_1_.11, bf16[48,1536]{1,0:T(8,128)(2,1)} %get-tuple-element.103.refs_2_.refs_19_.refs_22_, ...), custom_call_target="tpu_custom_call" | custom-call | bytes 5214328 | tf_op jit(solution)/shard_map/pallas_call | solution.py:72
  47.7 5.1 %all-to-all-start = ((f32[32,24,128]{2,1,0:T(8,128)}), f32[32,24,128]{2,1,0:T(8,128)S(1)}, u32[]{:S(2)}, u32[]{:S(2)}) async-start(f32[32,24,128]{2,1,0:T(8,128)} %bitcast.14), calls=%async_computation | async-start | bytes 786432 | tf_op jit(solution)/shard_map/all_to_all | solution.py:387
  54.5 6.5 %shard_map.98 = (f32[256,128]{1,0:T(8,128)}, f32[256,128]{1,0:T(8,128)}, f32[256,128]{1,0:T(8,128)}, f32[256,128]{1,0:T(8,128)}, f32[256,128]{1,0:T(8,128)}, /*i...) custom-call(bf16[1536,1536]{1,0:T(8,128)(2,1)} %get-tuple-element.106.schur, ...), custom_call_target="tpu_custom_call" | custom-call | flops 603979776 | bytes 7479296 | tf_op jit(solution)/shard_map/pallas_call | solution.py:72
  66.8 6.1 %collective-permute-start.9 = (f32[256,128]{1,0:T(8,128)}, f32[256,128]{1,0:T(8,128)S(1)}, u32[]{:S(2)}, u32[]{:S(2)}) collective-permute-start(f32[256,128]{1,0:T(8,128)} %get-tuple-element.118), channel_id=1, source_target_pairs={{0,4},{1,5},{2,6},{3,7},{4,8},{5,9},{6,10},{7,11},{8,12},{9,13},{1... | collective-permute-start | bytes 393224 | tf_op jit(solution)/shard_map/ppermute | solution.py:53
  72.9 5.9 %collective-permute-start.10 = (f32[256,128]{1,0:T(8,128)}, f32[256,128]{1,0:T(8,128)S(1)}, u32[]{:S(2)}, u32[]{:S(2)}) collective-permute-start(f32[256,128]{1,0:T(8,128)} %get-tuple-element.119), channel_id=1, source_target_pairs={{16,0},{17,1},{18,2},{19,3},{20,4},{21,5},{22,6},{23,7},{24,8},{25... | collective-permute-start | bytes 393224 | tf_op jit(solution)/shard_map/ppermute | solution.py:51
  86.7 8.6 %all-to-all-done.1.parts = f32[8,32,128]{2,1,0:T(8,128)S(1)} async-done(((f32[8,32,128]{2,1,0:T(8,128)}), f32[8,32,128]{2,1,0:T(8,128)S(1)}, u32[]{:S(2)}, u32[]{:S(2)}) %all-to-all-start.1) | async-done | bytes 131104 | tf_op jit(solution)/shard_map/all_to_all | solution.py:399
  97.7 8.0 %all-to-all-start.2 = ((f32[32,32,128]{2,1,0:T(8,128)}), f32[32,32,128]{2,1,0:T(8,128)S(1)}, u32[]{:S(2)}, u32[]{:S(2)}) async-start(f32[32,32,128]{2,1,0:T(8,128)} %shard_map.100), calls=%async_computation.2 | async-start | bytes 1048576 | tf_op jit(solution)/shard_map/all_to_all | solution.py:401
  110.5 4.8 %shard_map.101 = (bf16[1536,256]{1,0:T(8,128)(2,1)}, bf16[1536,256]{1,0:T(8,128)(2,1)}) custom-call(s32[1,6]{1,0:T(1,128)} %refs_0_.13, f32[24,1536]{1,0:T(8,128)} %get-tuple-element.111.refs_1_, f32[312,128]{1,0:T(8,128)} %copy-done.11, f32[312,128]{1,0:T(8,128)} %copy-done.12, f32[312,128]{1,0:T(8,128)} %copy-done.13, f32[312,128]{1,0:T(8,128)} %copy-done.14, ...), custom_call_target="tpu_custom_call" | custom-call | bytes 2678808 | tf_op jit(solution)/shard_map/pallas_call | solution.py:72
  119.7 9.5 %shard_map.102 = (f32[1536,128]{1,0:T(8,128)}, f32[1536,128]{1,0:T(8,128)}, f32[1536,128]{1,0:T(8,128)}, f32[1536,128]{1,0:T(8,128)}, f32[8,128]{1,0:T(8,128)}, ...) custom-call(s32[1,6]{1,0:T(1,128)} %refs_0_.13, s32[1,24]{1,0:T(1,128)} %refs_1_.11, ...), custom_call_target="tpu_custom_call" | custom-call | bytes 13267736 | tf_op jit(solution)/shard_map/pallas_call | solution.py:72
  129.2 7.4 %all-to-all-start.3 = ((f32[32,24,128]{2,1,0:T(8,128)}), f32[32,24,128]{2,1,0:T(8,128)S(1)}, u32[]{:S(2)}, u32[]{:S(2)}) async-start(f32[32,24,128]{2,1,0:T(8,128)} %bitcast.18), calls=%async_computation.3 | async-start | bytes 786432 | tf_op jit(solution)/shard_map/all_to_all | solution.py:387
  136.6 6.5 %shard_map.103 = (f32[256,128]{1,0:T(8,128)}, f32[256,128]{1,0:T(8,128)}, f32[256,128]{1,0:T(8,128)}, f32[256,128]{1,0:T(8,128)}, f32[256,128]{1,0:T(8,128)}, /*...) custom-call(bf16[1536,1536]{1,0:T(8,128)(2,1)} %get-tuple-element.106.schur, ...), custom_call_target="tpu_custom_call" | custom-call | flops 603979776 | bytes 7479296 | tf_op jit(solution)/shard_map/pallas_call | solution.py:72
  147.1 14.0 %all_to_all.75.parts = f32[8,32,128]{2,1,0:T(8,128)} all-to-all(f32[8,32,128]{2,1,0:T(8,128)} %shard_map.104), channel_id=1, replica_groups={{0,8,16,24,32,40,48,56},{1,9,17,25,33,41,49,57},{2,10,18,26,34,42,50,58..., dimensions={0} | all-to-all | bytes 262144 | tf_op jit(solution)/shard_map/all_to_all | solution.py:399
  162.8 5.8 %all-to-all-start.5 = ((f32[32,32,128]{2,1,0:T(8,128)}), f32[32,32,128]{2,1,0:T(8,128)S(1)}, u32[]{:S(2)}, u32[]{:S(2)}) async-start(f32[32,32,128]{2,1,0:T(8,128)} %shard_map.105), calls=%async_computation.5 | async-start | bytes 1048576 | tf_op jit(solution)/shard_map/all_to_all | solution.py:401
  174.3 6.1 %collective-permute-start.15 = (f32[256,128]{1,0:T(8,128)S(1)}, f32[256,128]{1,0:T(8,128)S(1)}, u32[]{:S(2)}, u32[]{:S(2)}) collective-permute-start(f32[256,128]{1,0:T(8,128)S(1)} %copy-done.59), channel_id=1, source_target_pairs={{0,4},{1,5},{2,6},{3,7},{4,8},{5,9},{6,10},{7,11},{8,12},{9,13},{1... | collective-permute-start | bytes 393224 | tf_op jit(solution)/shard_map/ppermute | solution.py:53
  182.9 4.2 collective-permute-start.17
  187.2 5.0 %collective-permute-done.16.refs_13_ = f32[256,128]{1,0:T(8,128)S(1)} collective-permute-done((f32[256,128]{1,0:T(8,128)S(1)}, f32[256,128]{1,0:T(8,128)S(1)}, u32[]{:S(2)}, u32[]{:S(2)}) %collective-permute-start.16) | collective-permute-done | bytes 131104 | tf_op jit(solution)/shard_map/ppermute | solution.py:51
  197.2 10.0 %shard_map.106 = (f32[1536,128]{1,0:T(8,128)}, f32[1536,128]{1,0:T(8,128)}, f32[1536,128]{1,0:T(8,128)}, f32[1536,128]{1,0:T(8,128)}, f32[8,128]{1,0:T(8,128)}, ...) custom-call(s32[1,6]{1,0:T(1,128)} %refs_0_.13, s32[1,24]{1,0:T(1,128)} %refs_1_.11, ...), custom_call_target="tpu_custom_call" | custom-call | bytes 15627032 | tf_op jit(solution)/shard_map/pallas_call | solution.py:72
  207.2 5.5 %all-to-all-start.6 = ((f32[32,24,128]{2,1,0:T(8,128)}), f32[32,24,128]{2,1,0:T(8,128)S(1)}, u32[]{:S(2)}, u32[]{:S(2)}) async-start(f32[32,24,128]{2,1,0:T(8,128)} %bitcast.16), calls=%async_computation.6 | async-start | bytes 786432 | tf_op jit(solution)/shard_map/all_to_all | solution.py:387
  212.7 6.5 %shard_map.107 = (f32[256,128]{1,0:T(8,128)}, f32[256,128]{1,0:T(8,128)}, f32[256,128]{1,0:T(8,128)}, f32[256,128]{1,0:T(8,128)}, f32[256,128]{1,0:T(8,128)}, /*...) custom-call(bf16[1536,1536]{1,0:T(8,128)(2,1)} %get-tuple-element.106.schur, ...), custom_call_target="tpu_custom_call" | custom-call | flops 603979776 | bytes 7479296 | tf_op jit(solution)/shard_map/pallas_call | solution.py:72
  223.2 14.0 %all_to_all.76.parts = f32[8,32,128]{2,1,0:T(8,128)} all-to-all(f32[8,32,128]{2,1,0:T(8,128)} %shard_map.108), channel_id=1, replica_groups={{0,8,16,24,32,40,48,56},{1,9,17,25,33,41,49,57},{2,10,18,26,34,42,50,58..., dimensions={0} | all-to-all | bytes 262144 | tf_op jit(solution)/shard_map/all_to_all | solution.py:399
  239.0 5.8 %all-to-all-start.8 = ((f32[32,32,128]{2,1,0:T(8,128)}), f32[32,32,128]{2,1,0:T(8,128)S(1)}, u32[]{:S(2)}, u32[]{:S(2)}) async-start(f32[32,32,128]{2,1,0:T(8,128)} %shard_map.109), calls=%async_computation.8 | async-start | bytes 1048576 | tf_op jit(solution)/shard_map/all_to_all | solution.py:401
  250.4 6.1 %collective-permute-start.21 = (f32[256,128]{1,0:T(8,128)S(1)}, f32[256,128]{1,0:T(8,128)S(1)}, u32[]{:S(2)}, u32[]{:S(2)}) collective-permute-start(f32[256,128]{1,0:T(8,128)S(1)} %copy-done.60), channel_id=1, source_target_pairs={{0,4},{1,5},{2,6},{3,7},{4,8},{5,9},{6,10},{7,11},{8,12},{9,13},{1... | collective-permute-start | bytes 393224 | tf_op jit(solution)/shard_map/ppermute | solution.py:53
  259.1 4.2 collective-permute-start.23
  263.4 4.6 %collective-permute-done.22.refs_13_ = f32[256,128]{1,0:T(8,128)S(1)} collective-permute-done((f32[256,128]{1,0:T(8,128)S(1)}, f32[256,128]{1,0:T(8,128)S(1)}, u32[]{:S(2)}, u32[]{:S(2)}) %collective-permute-start.22) | collective-permute-done | bytes 131104 | tf_op jit(solution)/shard_map/ppermute | solution.py:51
  268.0 4.5 %collective-permute-done.23.refs_14_ = f32[256,128]{1,0:T(8,128)S(1)} collective-permute-done((f32[256,128]{1,0:T(8,128)S(1)}, f32[256,128]{1,0:T(8,128)S(1)}, u32[]{:S(2)}, u32[]{:S(2)}) %collective-permute-start.23) | collective-permute-done | bytes 131104 | tf_op jit(solution)/shard_map/ppermute | solution.py:53
  273.4 10.1 %shard_map.110 = (f32[1536,128]{1,0:T(8,128)}, f32[1536,128]{1,0:T(8,128)}, f32[1536,128]{1,0:T(8,128)}, f32[1536,128]{1,0:T(8,128)}, f32[8,128]{1,0:T(8,128)}, ...) custom-call(s32[1,6]{1,0:T(1,128)} %refs_0_.13, s32[1,24]{1,0:T(1,128)} %refs_1_.11, ...), custom_call_target="tpu_custom_call" | custom-call | bytes 15627032 | tf_op jit(solution)/shard_map/pallas_call | solution.py:72
  283.4 5.5 %all-to-all-start.9 = ((f32[32,24,128]{2,1,0:T(8,128)}), f32[32,24,128]{2,1,0:T(8,128)S(1)}, u32[]{:S(2)}, u32[]{:S(2)}) async-start(f32[32,24,128]{2,1,0:T(8,128)} %bitcast.17), calls=%async_computation.9 | async-start | bytes 786432 | tf_op jit(solution)/shard_map/all_to_all | solution.py:387
  288.9 6.5 %shard_map.111 = (f32[256,128]{1,0:T(8,128)}, f32[256,128]{1,0:T(8,128)}, f32[256,128]{1,0:T(8,128)}, f32[256,128]{1,0:T(8,128)}, f32[256,128]{1,0:T(8,128)}, /*...) custom-call(bf16[1536,1536]{1,0:T(8,128)(2,1)} %get-tuple-element.106.schur, ...), custom_call_target="tpu_custom_call" | custom-call | flops 603979776 | bytes 7479296 | tf_op jit(solution)/shard_map/pallas_call | solution.py:72
  299.4 14.0 %all_to_all.77.parts = f32[8,32,128]{2,1,0:T(8,128)} all-to-all(f32[8,32,128]{2,1,0:T(8,128)} %shard_map.112), channel_id=1, replica_groups={{0,8,16,24,32,40,48,56},{1,9,17,25,33,41,49,57},{2,10,18,26,34,42,50,58..., dimensions={0} | all-to-all | bytes 262144 | tf_op jit(solution)/shard_map/all_to_all | solution.py:399
  315.1 5.8 %all-to-all-start.11 = ((f32[32,32,128]{2,1,0:T(8,128)}), f32[32,32,128]{2,1,0:T(8,128)S(1)}, u32[]{:S(2)}, u32[]{:S(2)}) async-start(f32[32,32,128]{2,1,0:T(8,128)} %shard_map.113), calls=%async_computation.11 | async-start | bytes 1048576 | tf_op jit(solution)/shard_map/all_to_all | solution.py:401
  326.6 6.1 %collective-permute-start.27 = (f32[256,128]{1,0:T(8,128)S(1)}, f32[256,128]{1,0:T(8,128)S(1)}, u32[]{:S(2)}, u32[]{:S(2)}) collective-permute-start(f32[256,128]{1,0:T(8,128)S(1)} %copy-done.61), channel_id=1, source_target_pairs={{0,4},{1,5},{2,6},{3,7},{4,8},{5,9},{6,10},{7,11},{8,12},{9,13},{1... | collective-permute-start | bytes 393224 | tf_op jit(solution)/shard_map/ppermute | solution.py:53
  335.3 4.2 collective-permute-start.29
  339.5 4.5 %collective-permute-done.28.refs_13_ = f32[256,128]{1,0:T(8,128)S(1)} collective-permute-done((f32[256,128]{1,0:T(8,128)S(1)}, f32[256,128]{1,0:T(8,128)S(1)}, u32[]{:S(2)}, u32[]{:S(2)}) %collective-permute-start.28) | collective-permute-done | bytes 131104 | tf_op jit(solution)/shard_map/ppermute | solution.py:51
  344.0 4.7 %collective-permute-done.29.refs_14_ = f32[256,128]{1,0:T(8,128)S(1)} collective-permute-done((f32[256,128]{1,0:T(8,128)S(1)}, f32[256,128]{1,0:T(8,128)S(1)}, u32[]{:S(2)}, u32[]{:S(2)}) %collective-permute-start.29) | collective-permute-done | bytes 131104 | tf_op jit(solution)/shard_map/ppermute | solution.py:53
  349.5 10.1 %shard_map.114 = (f32[1536,128]{1,0:T(8,128)}, f32[1536,128]{1,0:T(8,128)}, f32[1536,128]{1,0:T(8,128)}, f32[1536,128]{1,0:T(8,128)}, f32[8,128]{1,0:T(8,128)}, ...) custom-call(s32[1,6]{1,0:T(1,128)} %refs_0_.13, s32[1,24]{1,0:T(1,128)} %refs_1_.11, ...), custom_call_target="tpu_custom_call" | custom-call | bytes 15627032 | tf_op jit(solution)/shard_map/pallas_call | solution.py:72
  359.6 5.5 %all-to-all-start.12 = ((f32[32,24,128]{2,1,0:T(8,128)}), f32[32,24,128]{2,1,0:T(8,128)S(1)}, u32[]{:S(2)}, u32[]{:S(2)}) async-start(f32[32,24,128]{2,1,0:T(8,128)} %bitcast.15), calls=%async_computation.12 | async-start | bytes 786432 | tf_op jit(solution)/shard_map/all_to_all | solution.py:387
  365.1 6.5 %shard_map.115 = (f32[256,128]{1,0:T(8,128)}, f32[256,128]{1,0:T(8,128)}, f32[256,128]{1,0:T(8,128)}, f32[256,128]{1,0:T(8,128)}, f32[256,128]{1,0:T(8,128)}, /*...) custom-call(bf16[1536,1536]{1,0:T(8,128)(2,1)} %get-tuple-element.106.schur, ...), custom_call_target="tpu_custom_call" | custom-call | flops 603979776 | bytes 7479296 | tf_op jit(solution)/shard_map/pallas_call | solution.py:72
  375.6 14.0 %all_to_all.78.parts = f32[8,32,128]{2,1,0:T(8,128)} all-to-all(f32[8,32,128]{2,1,0:T(8,128)} %shard_map.116), channel_id=1, replica_groups={{0,8,16,24,32,40,48,56},{1,9,17,25,33,41,49,57},{2,10,18,26,34,42,50,58..., dimensions={0} | all-to-all | bytes 262144 | tf_op jit(solution)/shard_map/all_to_all | solution.py:399
  391.3 5.8 %all-to-all-start.14 = ((f32[32,32,128]{2,1,0:T(8,128)}), f32[32,32,128]{2,1,0:T(8,128)S(1)}, u32[]{:S(2)}, u32[]{:S(2)}) async-start(f32[32,32,128]{2,1,0:T(8,128)} %shard_map.117), calls=%async_computation.14 | async-start | bytes 1048576 | tf_op jit(solution)/shard_map/all_to_all | solution.py:401
  402.8 6.1 %collective-permute-start.33 = (f32[256,128]{1,0:T(8,128)S(1)}, f32[256,128]{1,0:T(8,128)S(1)}, u32[]{:S(2)}, u32[]{:S(2)}) collective-permute-start(f32[256,128]{1,0:T(8,128)S(1)} %copy-done.58), channel_id=1, source_target_pairs={{0,4},{1,5},{2,6},{3,7},{4,8},{5,9},{6,10},{7,11},{8,12},{9,13},{1... | collective-permute-start | bytes 393224 | tf_op jit(solution)/shard_map/ppermute | solution.py:53
  411.5 4.2 collective-permute-start.35
  415.7 4.5 %collective-permute-done.34.refs_13_ = f32[256,128]{1,0:T(8,128)S(1)} collective-permute-done((f32[256,128]{1,0:T(8,128)S(1)}, f32[256,128]{1,0:T(8,128)S(1)}, u32[]{:S(2)}, u32[]{:S(2)}) %collective-permute-start.34) | collective-permute-done | bytes 131104 | tf_op jit(solution)/shard_map/ppermute | solution.py:51
  420.2 4.7 %collective-permute-done.35.refs_14_ = f32[256,128]{1,0:T(8,128)S(1)} collective-permute-done((f32[256,128]{1,0:T(8,128)S(1)}, f32[256,128]{1,0:T(8,128)S(1)}, u32[]{:S(2)}, u32[]{:S(2)}) %collective-permute-start.35) | collective-permute-done | bytes 131104 | tf_op jit(solution)/shard_map/ppermute | solution.py:53
  425.7 9.4 %shard_map.118 = (f32[1536,128]{1,0:T(8,128)}, f32[1536,128]{1,0:T(8,128)}) custom-call(s32[1,6]{1,0:T(1,128)} %refs_0_.13, s32[1,24]{1,0:T(1,128)} %refs_1_.11, s32[1,168]{1,0:T(1,128)} %concatenate.3.refs_2_, f32[32,32,128]{2,1,0:T(8,128)} %copy-done.5, bf16[768,768]{1,0:T(8,128)(2,1)} %get-tuple-element.193.refs_4_, ...), custom_call_target="tpu_custom_call" | custom-call | bytes 12331800 | tf_op jit(solution)/shard_map/pallas_call | solution.py:72
  (235 shorter events, 105.1 us)
Async XLA Ops:
  5.9 20.8 %collective-permute-start = (f32[312,128]{1,0:T(8,128)}, f32[312,128]{1,0:T(8,128)S(1)}, u32[]{:S(2)}, u32[]{:S(2)}) collective-permute-start(f32[312,128]{1,0:T(8,128)} %get-tuple-element.97.refs_5_), channel_id=1, source_target_pairs={{1,0},{2,1},{3,2},{5,4},{6,5},{7,6},{9,8},{10,9},{11,10},{13,12},{... | collective-permute-start | bytes 479240 | tf_op jit(solution)/shard_map/ppermute | solution.py:51
  7.2 29.3 %collective-permute-start.1 = (f32[312,128]{1,0:T(8,128)}, f32[312,128]{1,0:T(8,128)S(1)}, u32[]{:S(2)}, u32[]{:S(2)}) collective-permute-start(f32[312,128]{1,0:T(8,128)} %get-tuple-element.98.refs_4_), channel_id=1, source_target_pairs={{0,1},{1,2},{2,3},{4,5},{5,6},{6,7},{8,9},{9,10},{10,11},{12,13},{... | collective-permute-start | bytes 479240 | tf_op jit(solution)/shard_map/ppermute | solution.py:53
  10.3 26.3 %collective-permute-start.2 = (f32[312,128]{1,0:T(8,128)}, f32[312,128]{1,0:T(8,128)S(1)}, u32[]{:S(2)}, u32[]{:S(2)}) collective-permute-start(f32[312,128]{1,0:T(8,128)} %get-tuple-element.99.refs_7_), channel_id=1, source_target_pairs={{4,0},{5,1},{6,2},{7,3},{8,4},{9,5},{10,6},{11,7},{12,8},{13,9},{1... | collective-permute-start | bytes 479240 | tf_op jit(solution)/shard_map/ppermute | solution.py:51
  11.6 25.0 %collective-permute-start.3 = (f32[312,128]{1,0:T(8,128)}, f32[312,128]{1,0:T(8,128)S(1)}, u32[]{:S(2)}, u32[]{:S(2)}) collective-permute-start(f32[312,128]{1,0:T(8,128)} %get-tuple-element.100.refs_6_), channel_id=1, source_target_pairs={{0,4},{1,5},{2,6},{3,7},{4,8},{5,9},{6,10},{7,11},{8,12},{9,13},{1... | collective-permute-start | bytes 479240 | tf_op jit(solution)/shard_map/ppermute | solution.py:53
  17.6 19.0 %collective-permute-start.4 = (f32[312,128]{1,0:T(8,128)}, f32[312,128]{1,0:T(8,128)S(1)}, u32[]{:S(2)}, u32[]{:S(2)}) collective-permute-start(f32[312,128]{1,0:T(8,128)} %get-tuple-element.101.refs_9_), channel_id=1, source_target_pairs={{16,0},{17,1},{18,2},{19,3},{20,4},{21,5},{22,6},{23,7},{24,8},{25... | collective-permute-start | bytes 479240 | tf_op jit(solution)/shard_map/ppermute | solution.py:51
  26.8 14.4 %collective-permute-start.5 = (f32[312,128]{1,0:T(8,128)}, f32[312,128]{1,0:T(8,128)S(1)}, u32[]{:S(2)}, u32[]{:S(2)}) collective-permute-start(f32[312,128]{1,0:T(8,128)} %get-tuple-element.102.refs_8_), channel_id=1, source_target_pairs={{0,16},{1,17},{2,18},{3,19},{4,20},{5,21},{6,22},{7,23},{8,24},{9,... | collective-permute-start | bytes 479240 | tf_op jit(solution)/shard_map/ppermute | solution.py:53
  47.7 31.8 %all-to-all-start = ((f32[32,24,128]{2,1,0:T(8,128)}), f32[32,24,128]{2,1,0:T(8,128)S(1)}, u32[]{:S(2)}, u32[]{:S(2)}) async-start(f32[32,24,128]{2,1,0:T(8,128)} %bitcast.14), calls=%async_computation | async-start | bytes 786432 | tf_op jit(solution)/shard_map/all_to_all | solution.py:387
  61.1 48.7 %copy-start.48 = (s32[1,24]{1,0:T(1,128)S(1)}, s32[1,24]{1,0:T(1,128)}, u32[]{:S(2)}) copy-start(s32[1,24]{1,0:T(1,128)} %refs_1_.11) | copy-start | bytes 292
  61.1 46.1 %collective-permute-start.6 = (f32[256,128]{1,0:T(8,128)}, f32[256,128]{1,0:T(8,128)S(1)}, u32[]{:S(2)}, u32[]{:S(2)}) collective-permute-start(f32[256,128]{1,0:T(8,128)} %get-tuple-element.115), channel_id=1, source_target_pairs={{1,0},{2,1},{3,2},{5,4},{6,5},{7,6},{9,8},{10,9},{11,10},{13,12},{... | collective-permute-start | bytes 393224 | tf_op jit(solution)/shard_map/ppermute | solution.py:51
  62.5 52.8 %collective-permute-start.7 = (f32[256,128]{1,0:T(8,128)}, f32[256,128]{1,0:T(8,128)S(1)}, u32[]{:S(2)}, u32[]{:S(2)}) collective-permute-start(f32[256,128]{1,0:T(8,128)} %get-tuple-element.116), channel_id=1, source_target_pairs={{0,1},{1,2},{2,3},{4,5},{5,6},{6,7},{8,9},{9,10},{10,11},{12,13},{... | collective-permute-start | bytes 393224 | tf_op jit(solution)/shard_map/ppermute | solution.py:53
  65.5 49.8 %collective-permute-start.8 = (f32[256,128]{1,0:T(8,128)}, f32[256,128]{1,0:T(8,128)S(1)}, u32[]{:S(2)}, u32[]{:S(2)}) collective-permute-start(f32[256,128]{1,0:T(8,128)} %get-tuple-element.117), channel_id=1, source_target_pairs={{4,0},{5,1},{6,2},{7,3},{8,4},{9,5},{10,6},{11,7},{12,8},{13,9},{1... | collective-permute-start | bytes 393224 | tf_op jit(solution)/shard_map/ppermute | solution.py:51
  66.8 48.5 %collective-permute-start.9 = (f32[256,128]{1,0:T(8,128)}, f32[256,128]{1,0:T(8,128)S(1)}, u32[]{:S(2)}, u32[]{:S(2)}) collective-permute-start(f32[256,128]{1,0:T(8,128)} %get-tuple-element.118), channel_id=1, source_target_pairs={{0,4},{1,5},{2,6},{3,7},{4,8},{5,9},{6,10},{7,11},{8,12},{9,13},{1... | collective-permute-start | bytes 393224 | tf_op jit(solution)/shard_map/ppermute | solution.py:53
  72.9 42.5 %collective-permute-start.10 = (f32[256,128]{1,0:T(8,128)}, f32[256,128]{1,0:T(8,128)S(1)}, u32[]{:S(2)}, u32[]{:S(2)}) collective-permute-start(f32[256,128]{1,0:T(8,128)} %get-tuple-element.119), channel_id=1, source_target_pairs={{16,0},{17,1},{18,2},{19,3},{20,4},{21,5},{22,6},{23,7},{24,8},{25... | collective-permute-start | bytes 393224 | tf_op jit(solution)/shard_map/ppermute | solution.py:51
  81.9 13.3 %all-to-all-start.1 = ((f32[8,32,128]{2,1,0:T(8,128)}), f32[8,32,128]{2,1,0:T(8,128)S(1)}, u32[]{:S(2)}, u32[]{:S(2)}) async-start(f32[8,32,128]{2,1,0:T(8,128)} %shard_map.99), calls=%async_computation.1 | async-start | bytes 262144 | tf_op jit(solution)/shard_map/all_to_all | solution.py:399
  97.7 21.1 %all-to-all-start.2 = ((f32[32,32,128]{2,1,0:T(8,128)}), f32[32,32,128]{2,1,0:T(8,128)S(1)}, u32[]{:S(2)}, u32[]{:S(2)}) async-start(f32[32,32,128]{2,1,0:T(8,128)} %shard_map.100), calls=%async_computation.2 | async-start | bytes 1048576 | tf_op jit(solution)/shard_map/all_to_all | solution.py:401
  107.1 11.7 %collective-permute-start.11 = (f32[256,128]{1,0:T(8,128)S(1)}, f32[256,128]{1,0:T(8,128)S(1)}, u32[]{:S(2)}, u32[]{:S(2)}) collective-permute-start(f32[256,128]{1,0:T(8,128)S(1)} %copy-done.49), channel_id=1, source_target_pairs={{0,16},{1,17},{2,18},{3,19},{4,20},{5,21},{6,22},{7,23},{8,24},{9,... | collective-permute-start | bytes 393224 | tf_op jit(solution)/shard_map/ppermute | solution.py:53
  129.2 15.5 %all-to-all-start.3 = ((f32[32,24,128]{2,1,0:T(8,128)}), f32[32,24,128]{2,1,0:T(8,128)S(1)}, u32[]{:S(2)}, u32[]{:S(2)}) async-start(f32[32,24,128]{2,1,0:T(8,128)} %bitcast.18), calls=%async_computation.3 | async-start | bytes 786432 | tf_op jit(solution)/shard_map/all_to_all | solution.py:387
  162.8 33.6 %all-to-all-start.5 = ((f32[32,32,128]{2,1,0:T(8,128)}), f32[32,32,128]{2,1,0:T(8,128)S(1)}, u32[]{:S(2)}, u32[]{:S(2)}) async-start(f32[32,32,128]{2,1,0:T(8,128)} %shard_map.105), calls=%async_computation.5 | async-start | bytes 1048576 | tf_op jit(solution)/shard_map/all_to_all | solution.py:401
  168.6 14.3 %collective-permute-start.12 = (f32[256,128]{1,0:T(8,128)S(1)}, f32[256,128]{1,0:T(8,128)S(1)}, u32[]{:S(2)}, u32[]{:S(2)}) collective-permute-start(f32[256,128]{1,0:T(8,128)S(1)} %copy-done.71), channel_id=1, source_target_pairs={{1,0},{2,1},{3,2},{5,4},{6,5},{7,6},{9,8},{10,9},{11,10},{13,12},{... | collective-permute-start | bytes 393224 | tf_op jit(solution)/shard_map/ppermute | solution.py:51
  169.9 17.2 %collective-permute-start.13 = (f32[256,128]{1,0:T(8,128)S(1)}, f32[256,128]{1,0:T(8,128)S(1)}, u32[]{:S(2)}, u32[]{:S(2)}) collective-permute-start(f32[256,128]{1,0:T(8,128)S(1)} %copy-done.67), channel_id=1, source_target_pairs={{0,1},{1,2},{2,3},{4,5},{5,6},{6,7},{8,9},{9,10},{10,11},{12,13},{... | collective-permute-start | bytes 393224 | tf_op jit(solution)/shard_map/ppermute | solution.py:53
  173.0 14.2 %collective-permute-start.14 = (f32[256,128]{1,0:T(8,128)S(1)}, f32[256,128]{1,0:T(8,128)S(1)}, u32[]{:S(2)}, u32[]{:S(2)}) collective-permute-start(f32[256,128]{1,0:T(8,128)S(1)} %copy-done.63), channel_id=1, source_target_pairs={{4,0},{5,1},{6,2},{7,3},{8,4},{9,5},{10,6},{11,7},{12,8},{13,9},{1... | collective-permute-start | bytes 393224 | tf_op jit(solution)/shard_map/ppermute | solution.py:51
  174.3 12.9 %collective-permute-start.15 = (f32[256,128]{1,0:T(8,128)S(1)}, f32[256,128]{1,0:T(8,128)S(1)}, u32[]{:S(2)}, u32[]{:S(2)}) collective-permute-start(f32[256,128]{1,0:T(8,128)S(1)} %copy-done.59), channel_id=1, source_target_pairs={{0,4},{1,5},{2,6},{3,7},{4,8},{5,9},{6,10},{7,11},{8,12},{9,13},{1... | collective-permute-start | bytes 393224 | tf_op jit(solution)/shard_map/ppermute | solution.py:53
  180.3 11.8 %collective-permute-start.16 = (f32[256,128]{1,0:T(8,128)S(1)}, f32[256,128]{1,0:T(8,128)S(1)}, u32[]{:S(2)}, u32[]{:S(2)}) collective-permute-start(f32[256,128]{1,0:T(8,128)S(1)} %copy-done.55), channel_id=1, source_target_pairs={{16,0},{17,1},{18,2},{19,3},{20,4},{21,5},{22,6},{23,7},{24,8},{25... | collective-permute-start | bytes 393224 | tf_op jit(solution)/shard_map/ppermute | solution.py:51
  182.9 13.4 %collective-permute-start.17 = (f32[256,128]{1,0:T(8,128)S(1)}, f32[256,128]{1,0:T(8,128)S(1)}, u32[]{:S(2)}, u32[]{:S(2)}) collective-permute-start(f32[256,128]{1,0:T(8,128)S(1)} %copy-done.51), channel_id=1, source_target_pairs={{0,16},{1,17},{2,18},{3,19},{4,20},{5,21},{6,22},{7,23},{8,24},{9,... | collective-permute-start | bytes 393224 | tf_op jit(solution)/shard_map/ppermute | solution.py:53
  207.2 13.6 %all-to-all-start.6 = ((f32[32,24,128]{2,1,0:T(8,128)}), f32[32,24,128]{2,1,0:T(8,128)S(1)}, u32[]{:S(2)}, u32[]{:S(2)}) async-start(f32[32,24,128]{2,1,0:T(8,128)} %bitcast.16), calls=%async_computation.6 | async-start | bytes 786432 | tf_op jit(solution)/shard_map/all_to_all | solution.py:387
  239.0 33.5 %all-to-all-start.8 = ((f32[32,32,128]{2,1,0:T(8,128)}), f32[32,32,128]{2,1,0:T(8,128)S(1)}, u32[]{:S(2)}, u32[]{:S(2)}) async-start(f32[32,32,128]{2,1,0:T(8,128)} %shard_map.109), calls=%async_computation.8 | async-start | bytes 1048576 | tf_op jit(solution)/shard_map/all_to_all | solution.py:401
  244.8 14.3 %collective-permute-start.18 = (f32[256,128]{1,0:T(8,128)S(1)}, f32[256,128]{1,0:T(8,128)S(1)}, u32[]{:S(2)}, u32[]{:S(2)}) collective-permute-start(f32[256,128]{1,0:T(8,128)S(1)} %copy-done.72), channel_id=1, source_target_pairs={{1,0},{2,1},{3,2},{5,4},{6,5},{7,6},{9,8},{10,9},{11,10},{13,12},{... | collective-permute-start | bytes 393224 | tf_op jit(solution)/shard_map/ppermute | solution.py:51
  246.1 17.2 %collective-permute-start.19 = (f32[256,128]{1,0:T(8,128)S(1)}, f32[256,128]{1,0:T(8,128)S(1)}, u32[]{:S(2)}, u32[]{:S(2)}) collective-permute-start(f32[256,128]{1,0:T(8,128)S(1)} %copy-done.68), channel_id=1, source_target_pairs={{0,1},{1,2},{2,3},{4,5},{5,6},{6,7},{8,9},{9,10},{10,11},{12,13},{... | collective-permute-start | bytes 393224 | tf_op jit(solution)/shard_map/ppermute | solution.py:53
  249.1 14.2 %collective-permute-start.20 = (f32[256,128]{1,0:T(8,128)S(1)}, f32[256,128]{1,0:T(8,128)S(1)}, u32[]{:S(2)}, u32[]{:S(2)}) collective-permute-start(f32[256,128]{1,0:T(8,128)S(1)} %copy-done.64), channel_id=1, source_target_pairs={{4,0},{5,1},{6,2},{7,3},{8,4},{9,5},{10,6},{11,7},{12,8},{13,9},{1... | collective-permute-start | bytes 393224 | tf_op jit(solution)/shard_map/ppermute | solution.py:51
  250.4 12.9 %collective-permute-start.21 = (f32[256,128]{1,0:T(8,128)S(1)}, f32[256,128]{1,0:T(8,128)S(1)}, u32[]{:S(2)}, u32[]{:S(2)}) collective-permute-start(f32[256,128]{1,0:T(8,128)S(1)} %copy-done.60), channel_id=1, source_target_pairs={{0,4},{1,5},{2,6},{3,7},{4,8},{5,9},{6,10},{7,11},{8,12},{9,13},{1... | collective-permute-start | bytes 393224 | tf_op jit(solution)/shard_map/ppermute | solution.py:53
  256.5 11.5 %collective-permute-start.22 = (f32[256,128]{1,0:T(8,128)S(1)}, f32[256,128]{1,0:T(8,128)S(1)}, u32[]{:S(2)}, u32[]{:S(2)}) collective-permute-start(f32[256,128]{1,0:T(8,128)S(1)} %copy-done.56), channel_id=1, source_target_pairs={{16,0},{17,1},{18,2},{19,3},{20,4},{21,5},{22,6},{23,7},{24,8},{25... | collective-permute-start | bytes 393224 | tf_op jit(solution)/shard_map/ppermute | solution.py:51
  259.1 13.4 %collective-permute-start.23 = (f32[256,128]{1,0:T(8,128)S(1)}, f32[256,128]{1,0:T(8,128)S(1)}, u32[]{:S(2)}, u32[]{:S(2)}) collective-permute-start(f32[256,128]{1,0:T(8,128)S(1)} %copy-done.52), channel_id=1, source_target_pairs={{0,16},{1,17},{2,18},{3,19},{4,20},{5,21},{6,22},{7,23},{8,24},{9,... | collective-permute-start | bytes 393224 | tf_op jit(solution)/shard_map/ppermute | solution.py:53
  283.4 13.6 %all-to-all-start.9 = ((f32[32,24,128]{2,1,0:T(8,128)}), f32[32,24,128]{2,1,0:T(8,128)S(1)}, u32[]{:S(2)}, u32[]{:S(2)}) async-start(f32[32,24,128]{2,1,0:T(8,128)} %bitcast.17), calls=%async_computation.9 | async-start | bytes 786432 | tf_op jit(solution)/shard_map/all_to_all | solution.py:387
  315.1 33.5 %all-to-all-start.11 = ((f32[32,32,128]{2,1,0:T(8,128)}), f32[32,32,128]{2,1,0:T(8,128)S(1)}, u32[]{:S(2)}, u32[]{:S(2)}) async-start(f32[32,32,128]{2,1,0:T(8,128)} %shard_map.113), calls=%async_computation.11 | async-start | bytes 1048576 | tf_op jit(solution)/shard_map/all_to_all | solution.py:401
  320.9 14.3 %collective-permute-start.24 = (f32[256,128]{1,0:T(8,128)S(1)}, f32[256,128]{1,0:T(8,128)S(1)}, u32[]{:S(2)}, u32[]{:S(2)}) collective-permute-start(f32[256,128]{1,0:T(8,128)S(1)} %copy-done.73), channel_id=1, source_target_pairs={{1,0},{2,1},{3,2},{5,4},{6,5},{7,6},{9,8},{10,9},{11,10},{13,12},{... | collective-permute-start | bytes 393224 | tf_op jit(solution)/shard_map/ppermute | solution.py:51
  322.3 17.2 %collective-permute-start.25 = (f32[256,128]{1,0:T(8,128)S(1)}, f32[256,128]{1,0:T(8,128)S(1)}, u32[]{:S(2)}, u32[]{:S(2)}) collective-permute-start(f32[256,128]{1,0:T(8,128)S(1)} %copy-done.69), channel_id=1, source_target_pairs={{0,1},{1,2},{2,3},{4,5},{5,6},{6,7},{8,9},{9,10},{10,11},{12,13},{... | collective-permute-start | bytes 393224 | tf_op jit(solution)/shard_map/ppermute | solution.py:53
  325.3 14.2 %collective-permute-start.26 = (f32[256,128]{1,0:T(8,128)S(1)}, f32[256,128]{1,0:T(8,128)S(1)}, u32[]{:S(2)}, u32[]{:S(2)}) collective-permute-start(f32[256,128]{1,0:T(8,128)S(1)} %copy-done.65), channel_id=1, source_target_pairs={{4,0},{5,1},{6,2},{7,3},{8,4},{9,5},{10,6},{11,7},{12,8},{13,9},{1... | collective-permute-start | bytes 393224 | tf_op jit(solution)/shard_map/ppermute | solution.py:51
  326.6 12.9 %collective-permute-start.27 = (f32[256,128]{1,0:T(8,128)S(1)}, f32[256,128]{1,0:T(8,128)S(1)}, u32[]{:S(2)}, u32[]{:S(2)}) collective-permute-start(f32[256,128]{1,0:T(8,128)S(1)} %copy-done.61), channel_id=1, source_target_pairs={{0,4},{1,5},{2,6},{3,7},{4,8},{5,9},{6,10},{7,11},{8,12},{9,13},{1... | collective-permute-start | bytes 393224 | tf_op jit(solution)/shard_map/ppermute | solution.py:53
  332.7 11.3 %collective-permute-start.28 = (f32[256,128]{1,0:T(8,128)S(1)}, f32[256,128]{1,0:T(8,128)S(1)}, u32[]{:S(2)}, u32[]{:S(2)}) collective-permute-start(f32[256,128]{1,0:T(8,128)S(1)} %copy-done.57), channel_id=1, source_target_pairs={{16,0},{17,1},{18,2},{19,3},{20,4},{21,5},{22,6},{23,7},{24,8},{25... | collective-permute-start | bytes 393224 | tf_op jit(solution)/shard_map/ppermute | solution.py:51
  335.3 13.4 %collective-permute-start.29 = (f32[256,128]{1,0:T(8,128)S(1)}, f32[256,128]{1,0:T(8,128)S(1)}, u32[]{:S(2)}, u32[]{:S(2)}) collective-permute-start(f32[256,128]{1,0:T(8,128)S(1)} %copy-done.53), channel_id=1, source_target_pairs={{0,16},{1,17},{2,18},{3,19},{4,20},{5,21},{6,22},{7,23},{8,24},{9,... | collective-permute-start | bytes 393224 | tf_op jit(solution)/shard_map/ppermute | solution.py:53
  359.6 13.6 %all-to-all-start.12 = ((f32[32,24,128]{2,1,0:T(8,128)}), f32[32,24,128]{2,1,0:T(8,128)S(1)}, u32[]{:S(2)}, u32[]{:S(2)}) async-start(f32[32,24,128]{2,1,0:T(8,128)} %bitcast.15), calls=%async_computation.12 | async-start | bytes 786432 | tf_op jit(solution)/shard_map/all_to_all | solution.py:387
  391.3 33.6 %all-to-all-start.14 = ((f32[32,32,128]{2,1,0:T(8,128)}), f32[32,32,128]{2,1,0:T(8,128)S(1)}, u32[]{:S(2)}, u32[]{:S(2)}) async-start(f32[32,32,128]{2,1,0:T(8,128)} %shard_map.117), calls=%async_computation.14 | async-start | bytes 1048576 | tf_op jit(solution)/shard_map/all_to_all | solution.py:401
  397.1 14.3 %collective-permute-start.30 = (f32[256,128]{1,0:T(8,128)S(1)}, f32[256,128]{1,0:T(8,128)S(1)}, u32[]{:S(2)}, u32[]{:S(2)}) collective-permute-start(f32[256,128]{1,0:T(8,128)S(1)} %copy-done.70), channel_id=1, source_target_pairs={{1,0},{2,1},{3,2},{5,4},{6,5},{7,6},{9,8},{10,9},{11,10},{13,12},{... | collective-permute-start | bytes 393224 | tf_op jit(solution)/shard_map/ppermute | solution.py:51
  398.4 17.2 %collective-permute-start.31 = (f32[256,128]{1,0:T(8,128)S(1)}, f32[256,128]{1,0:T(8,128)S(1)}, u32[]{:S(2)}, u32[]{:S(2)}) collective-permute-start(f32[256,128]{1,0:T(8,128)S(1)} %copy-done.66), channel_id=1, source_target_pairs={{0,1},{1,2},{2,3},{4,5},{5,6},{6,7},{8,9},{9,10},{10,11},{12,13},{... | collective-permute-start | bytes 393224 | tf_op jit(solution)/shard_map/ppermute | solution.py:53
  401.5 14.2 %collective-permute-start.32 = (f32[256,128]{1,0:T(8,128)S(1)}, f32[256,128]{1,0:T(8,128)S(1)}, u32[]{:S(2)}, u32[]{:S(2)}) collective-permute-start(f32[256,128]{1,0:T(8,128)S(1)} %copy-done.62), channel_id=1, source_target_pairs={{4,0},{5,1},{6,2},{7,3},{8,4},{9,5},{10,6},{11,7},{12,8},{13,9},{1... | collective-permute-start | bytes 393224 | tf_op jit(solution)/shard_map/ppermute | solution.py:51
  402.8 12.9 %collective-permute-start.33 = (f32[256,128]{1,0:T(8,128)S(1)}, f32[256,128]{1,0:T(8,128)S(1)}, u32[]{:S(2)}, u32[]{:S(2)}) collective-permute-start(f32[256,128]{1,0:T(8,128)S(1)} %copy-done.58), channel_id=1, source_target_pairs={{0,4},{1,5},{2,6},{3,7},{4,8},{5,9},{6,10},{7,11},{8,12},{9,13},{1... | collective-permute-start | bytes 393224 | tf_op jit(solution)/shard_map/ppermute | solution.py:53
  408.9 11.3 %collective-permute-start.34 = (f32[256,128]{1,0:T(8,128)S(1)}, f32[256,128]{1,0:T(8,128)S(1)}, u32[]{:S(2)}, u32[]{:S(2)}) collective-permute-start(f32[256,128]{1,0:T(8,128)S(1)} %copy-done.54), channel_id=1, source_target_pairs={{16,0},{17,1},{18,2},{19,3},{20,4},{21,5},{22,6},{23,7},{24,8},{25... | collective-permute-start | bytes 393224 | tf_op jit(solution)/shard_map/ppermute | solution.py:51
  411.5 13.4 %collective-permute-start.35 = (f32[256,128]{1,0:T(8,128)S(1)}, f32[256,128]{1,0:T(8,128)S(1)}, u32[]{:S(2)}, u32[]{:S(2)}) collective-permute-start(f32[256,128]{1,0:T(8,128)S(1)} %copy-done.50), channel_id=1, source_target_pairs={{0,16},{1,17},{2,18},{3,19},{4,20},{5,21},{6,22},{7,23},{8,24},{9,... | collective-permute-start | bytes 393224 | tf_op jit(solution)/shard_map/ppermute | solution.py:53
  (73 other events, 1072.1 us)

commit v5 on v3

--- a/solution.py
+++ b/solution.py
@@ -20,6 +20,8 @@
 COARSE = 768
 NEAR = 256
 DOTS = 8
+TURN = (0, 2, 4, 1, 3, 5)
+EARLY = (0, 1, 2)
 PACKED = FD + 2 * CORNERS + 8
 PLACES = np.arange(NSUB).reshape(4, 8, 8)
 PLANES = PLACES.transpose(1, 0, 2).reshape(8, 32).tolist()
@@ -46,16 +48,16 @@
 
 
 def swap_faces(blocks):
-    received = []
-    for d in range(3):
-        received.append(lax.ppermute(blocks[2 * d + 1], "sub", DOWN[d]))
-        received.append(lax.ppermute(blocks[2 * d], "sub", UP[d]))
-    return received
+    return [
+        lax.ppermute(blocks[f ^ 1], "sub", UP[f // 2] if f % 2 else DOWN[f // 2]) for f in TURN
+    ]
 
 
 def block_of(shape, kind):
     if kind == "smem":
         return pl.BlockSpec(memory_space=pltpu.SMEM)
+    if kind == "held":
+        return pl.BlockSpec(memory_space=pl.ANY)
     if kind == "rows":
         return pl.BlockSpec((FD, shape[1]), lambda f: (f, 0))
     if kind == "columns":
@@ -63,7 +65,7 @@
     return pl.BlockSpec(shape, lambda f: (0,) * len(shape))
 
 
-def call(kernel, steps, outs, inputs, scratch=(), flops=0):
+def call(kernel, steps, outs, inputs, scratch=(), flops=0, alias={}):
     inputs = [x if isinstance(x, tuple) else (x, "whole") for x in inputs]
     outs = [x if len(x) == 3 else (*x, "whole") for x in outs]
     size = sum(int(np.prod(s)) * jnp.dtype(t).itemsize for s, t, _ in outs)
@@ -75,6 +77,7 @@
         in_specs=[block_of(x.shape, kind) for x, kind in inputs],
         out_specs=[block_of(s, kind) for s, _, kind in outs],
         scratch_shapes=list(scratch),
+        input_output_aliases=alias,
         compiler_params=pltpu.CompilerParams(vmem_limit_bytes=56 * 2**20),
         cost_estimate=pl.CostEstimate(flops=flops, bytes_accessed=size, transcendentals=0),
     )(*[x for x, _ in inputs])
@@ -153,7 +156,7 @@
 
 def lift_kernel(*refs):
     glued, couple = refs[:2]
-    packs = refs[2 : 2 + FACES]
+    packs = [refs[2 + TURN.index(f)] for f in range(FACES)]
     high, low, rows = refs[2 + FACES :]
     step = pl.program_id(0)
     mask = glued[0, step].astype(f32)
@@ -194,7 +197,7 @@
 def begin_kernel(*refs):
     glued, ids, halves, weights = refs[:4]
     sent = refs[4 : 4 + FACES]
-    got = refs[4 + FACES : 4 + 2 * FACES]
+    got = [refs[4 + FACES + TURN.index(f)] for f in range(FACES)]
     residual, precond, rounded, spread, state, terms = refs[4 + 2 * FACES :]
     step = pl.program_id(0)
 
@@ -241,7 +244,8 @@
         out[i, ROWS:, :] = dots[...]
 
 
-def fold_line_kernel(parts, out):
+def fold_line_kernel(parts, *refs):
+    out = refs[-1]
     total = jnp.sum(parts[...], 0)
     for i in range(PLANE):
         out[i] = total
@@ -249,7 +253,7 @@
 
 def advance_kernel(first, last, *refs):
     glued, ids, near_ids, whole, inverse_high, inverse_low, lift_high, lift_low = refs[:8]
-    local, got, refs = refs[8], refs[9 : 9 + FACES], refs[9 + FACES :]
+    local, got, refs = refs[8], [refs[9 + TURN.index(f)] for f in range(FACES)], refs[9 + FACES :]
     weights, precond, residual, history = refs[:4]
     refs = refs[4:]
     if not first:
@@ -375,7 +379,12 @@
         scratch=[pltpu.VMEM((NEAR, FD), f32)],
     )
     near_ids = jnp.concatenate(
-        [corners] + [g[FD + 2 * CORNERS :][:1, :CORNERS].astype(jnp.int32) for g in got], 1
+        [corners]
+        + [
+            got[TURN.index(f)][FD + 2 * CORNERS :][:1, :CORNERS].astype(jnp.int32)
+            for f in range(FACES)
+        ],
+        1,
     )
     kept = lax.reduce_precision(coarse_inverse, 8, 7)
     inverse_high, inverse_low = kept.astype(bf16), (coarse_inverse - kept).astype(bf16)
@@ -394,9 +403,10 @@
             flops=2 * DOFS * DOFS * LOADS,
         )
         received = swap_faces(faces)
+        early = [(received[TURN.index(f)], "held") for f in EARLY]
         (lines,) = call(fold_plane_kernel, 1, [((LINE, ROWS + DOTS, LOADS), f32)], [parts, dots])
         lines = lax.all_to_all(lines, "sub", 0, 0, axis_index_groups=LINES)
-        (whole,) = call(fold_line_kernel, 1, [((PLANE, ROWS + DOTS, LOADS), f32)], [lines])
+        (whole,) = call(fold_line_kernel, 1, [((PLANE, ROWS + DOTS, LOADS), f32)], [lines, *early])
         whole = lax.all_to_all(whole, "sub", 0, 0, axis_index_groups=PLANES)
         inputs = [masks, own_ids, (near_ids, "smem"), whole, inverse_high, inverse_low]
         inputs += [(lift_high, "rows"), (lift_low, "rows"), (local, "rows"), *received]

time: 440 us -> 435 us (0.989)
  blocking collectives: 55.9 us -> 0 us
  waiting for transfers between devices: 59.1 us -> 85.3 us
  starting transfers between devices: 179 us -> 199 us
  local copies, waits for them, and re-layouts: 13 us -> 18.1 us
    all_to_all x4 -> x0, blocking collectives: 55.9 us -> none  [shards(): lines = lax.all_to_all(lines, 'sub', 0, 0, axis_index_groups=LINES)]
    ppermute x36, waiting for transfers between devices: 44.6 us -> 73.5 us  [swap_faces(): lax.ppermute(blocks[f ^ 1], 'sub', UP[f // 2] if f % 2 else DOWN[f // 2])]
    all_to_all x1 -> x5, starting transfers between devices: 3.37 us -> 17.9 us  [shards(): lines = lax.all_to_all(lines, 'sub', 0, 0, axis_index_groups=LINES)]
    all_to_all x5, starting transfers between devices: 31.1 us -> 36.5 us  [shards(): whole = lax.all_to_all(whole, 'sub', 0, 0, axis_index_groups=PLANES)]
    unnamed x149 -> x131, local copies, waits for them, and re-layouts: 10.6 us -> 15.7 us
    all_to_all x1 -> x5, waiting for transfers between devices: 8.59 us -> 3.83 us  [shards(): lines = lax.all_to_all(lines, 'sub', 0, 0, axis_index_groups=LINES)]
  transfers between devices with their start and end apart: 47 -> 51, of which waited for: 15 -> 19; matrix products, arithmetic and copies ran while one was open for 2% -> 2% of each run, Pallas kernels for 11% -> 11%
where the time goes in v5:
time: 435 us; the launch traced here: 431 us
  starting transfers between devices  199 us (46%)
  Pallas kernels  119 us (27%)
  waiting for transfers between devices  85.3 us (20%)
  local copies, waits for them, and re-layouts  18.1 us (4%)
  other arithmetic  7.19 us (2%)
    ppermute x36, starting transfers between devices, swap_faces(): lax.ppermute(blocks[f ^ 1], 'sub', UP[f // 2] if f % 2 else DOWN[f // 2])  119 us
    pallas_call x24, Pallas kernels, call(): pl.pallas_call(kernel, grid=(steps,), out_shape=[jax.ShapeDtypeStruct(s,...  119 us
    ppermute x36, waiting for transfers between devices, swap_faces(): lax.ppermute(blocks[f ^ 1], 'sub', UP[f // 2] if f % 2 else DOWN[f // 2])  73.5 us
    all_to_all x5, starting transfers between devices, shards(): whole = lax.all_to_all(whole, 'sub', 0, 0, axis_index_groups=PLANES)  36.5 us
    all_to_all x5, starting transfers between devices, shards(): lax.all_to_all(spread.reshape(PLANE, ROWS, LOADS), 'sub', 0, 0, axis_inde...  25.6 us
    all_to_all x5, starting transfers between devices, shards(): lines = lax.all_to_all(lines, 'sub', 0, 0, axis_index_groups=LINES)  17.9 us
    unnamed x131, local copies, waits for them, and re-layouts  15.7 us
  transfers between devices with their start and end apart: 51, of which 19 were waited for; matrix products, arithmetic and copies ran while one was open for 2% of the time, Pallas kernels for 11%

profile of v5, /device:TPU:24, one launch (start us, length us, event | category | flops | bytes accessed | tf_op | source)
XLA Modules:
  0.0 430.9 jit_solution(14647377621854697665)
XLA Ops:
  11.6 6.1 %collective-permute-start.3 = (f32[312,128]{1,0:T(8,128)}, f32[312,128]{1,0:T(8,128)S(1)}, u32[]{:S(2)}, u32[]{:S(2)}) collective-permute-start(f32[312,128]{1,0:T(8,128)} %get-tuple-element.100.refs_6_), channel_id=1, source_target_pairs={{0,4},{1,5},{2,6},{3,7},{4,8},{5,9},{6,10},{7,11},{8,12},{9,13},{1... | collective-permute-start | bytes 479240 | tf_op jit(solution)/shard_map/ppermute | solution.py:52
  17.6 8.4 %collective-permute-start.4 = (f32[312,128]{1,0:T(8,128)}, f32[312,128]{1,0:T(8,128)S(1)}, u32[]{:S(2)}, u32[]{:S(2)}) collective-permute-start(f32[312,128]{1,0:T(8,128)} %get-tuple-element.101.refs_9_), channel_id=1, source_target_pairs={{16,0},{17,1},{18,2},{19,3},{20,4},{21,5},{22,6},{23,7},{24,8},{25... | collective-permute-start | bytes 479240 | tf_op jit(solution)/shard_map/ppermute | solution.py:52
  29.9 6.7 %shard_map.96 = (bf16[1536,1536]{1,0:T(8,128)(2,1)}, f32[1536,128]{1,0:T(8,128)}) custom-call(bf16[1536,1536]{1,0:T(8,128)(2,1)} %bitcast.23, s32[6,256]{1,0:T(8,128)} %bitcast.21, f32[1536,128]{1,0:T(8,128)} %broadcast_in_dim.14.weights), custom_call_target="tpu_custom_call" | custom-call | flops 2415919104 | bytes 11016192 | tf_op jit(solution)/shard_map/pallas_call | solution.py:73
  36.6 4.5 %collective-permute-done.5.refs_15_.refs_7_ = f32[312,128]{1,0:T(8,128)S(1)} collective-permute-done((f32[312,128]{1,0:T(8,128)}, f32[312,128]{1,0:T(8,128)S(1)}, u32[]{:S(2)}, u32[]{:S(2)}) %collective-permute-start.5) | collective-permute-done | bytes 159776 | tf_op jit(solution)/shard_map/ppermute | solution.py:52
  41.8 5.9 %shard_map.97 = (f32[1536,128]{1,0:T(8,128)}, f32[1536,128]{1,0:T(8,128)}, bf16[1536,128]{1,0:T(8,128)(2,1)}, f32[768,128]{1,0:T(8,128)}, f32[8,128]{1,0:T(8,128)}) custom-call(s32[1,6]{1,0:T(1,128)} %refs_0_.13, s32[1,24]{1,0:T(1,128)} %refs_1_.11, bf16[48,1536]{1,0:T(8,128)(2,1)} %get-tuple-element.103.refs_2_.refs_19_.refs_22_, ...), custom_call_target="tpu_custom_call" | custom-call | bytes 5214328 | tf_op jit(solution)/shard_map/pallas_call | solution.py:73
  47.7 5.1 %all-to-all-start = ((f32[32,24,128]{2,1,0:T(8,128)}), f32[32,24,128]{2,1,0:T(8,128)S(1)}, u32[]{:S(2)}, u32[]{:S(2)}) async-start(f32[32,24,128]{2,1,0:T(8,128)} %bitcast.14), calls=%async_computation | async-start | bytes 786432 | tf_op jit(solution)/shard_map/all_to_all | solution.py:395
  54.5 6.6 %shard_map.98 = (f32[256,128]{1,0:T(8,128)}, f32[256,128]{1,0:T(8,128)}, f32[256,128]{1,0:T(8,128)}, f32[256,128]{1,0:T(8,128)}, f32[256,128]{1,0:T(8,128)}, /*i...) custom-call(bf16[1536,1536]{1,0:T(8,128)(2,1)} %get-tuple-element.106.schur, ...), custom_call_target="tpu_custom_call" | custom-call | flops 603979776 | bytes 7479296 | tf_op jit(solution)/shard_map/pallas_call | solution.py:73
  66.7 5.9 %collective-permute-start.9 = (f32[256,128]{1,0:T(8,128)}, f32[256,128]{1,0:T(8,128)S(1)}, u32[]{:S(2)}, u32[]{:S(2)}) collective-permute-start(f32[256,128]{1,0:T(8,128)} %get-tuple-element.118), channel_id=1, source_target_pairs={{16,0},{17,1},{18,2},{19,3},{20,4},{21,5},{22,6},{23,7},{24,8},{25... | collective-permute-start | bytes 393224 | tf_op jit(solution)/shard_map/ppermute | solution.py:52
  72.6 6.1 %collective-permute-start.10 = (f32[256,128]{1,0:T(8,128)}, f32[256,128]{1,0:T(8,128)S(1)}, u32[]{:S(2)}, u32[]{:S(2)}) collective-permute-start(f32[256,128]{1,0:T(8,128)} %get-tuple-element.119), channel_id=1, source_target_pairs={{0,4},{1,5},{2,6},{3,7},{4,8},{5,9},{6,10},{7,11},{8,12},{9,13},{1... | collective-permute-start | bytes 393224 | tf_op jit(solution)/shard_map/ppermute | solution.py:52
  86.5 4.7 %collective-permute-start.11 = (f32[256,128]{1,0:T(8,128)}, f32[256,128]{1,0:T(8,128)S(1)}, u32[]{:S(2)}, u32[]{:S(2)}) collective-permute-start(f32[256,128]{1,0:T(8,128)} %get-tuple-element.120), channel_id=1, source_target_pairs={{0,16},{1,17},{2,18},{3,19},{4,20},{5,21},{6,22},{7,23},{8,24},{9,... | collective-permute-start | bytes 393224 | tf_op jit(solution)/shard_map/ppermute | solution.py:52
  91.3 3.8 all-to-all-done.1.parts
  97.6 8.1 %all-to-all-start.2 = ((f32[32,32,128]{2,1,0:T(8,128)}), f32[32,32,128]{2,1,0:T(8,128)S(1)}, u32[]{:S(2)}, u32[]{:S(2)}) async-start(f32[32,32,128]{2,1,0:T(8,128)} %shard_map.100), calls=%async_computation.2 | async-start | bytes 1048576 | tf_op jit(solution)/shard_map/all_to_all | solution.py:410
  108.4 4.8 %shard_map.101 = (bf16[1536,256]{1,0:T(8,128)(2,1)}, bf16[1536,256]{1,0:T(8,128)(2,1)}) custom-call(s32[1,6]{1,0:T(1,128)} %refs_0_.13, f32[24,1536]{1,0:T(8,128)} %get-tuple-element.114.refs_1_, f32[312,128]{1,0:T(8,128)} %copy-done.11, f32[312,128]{1,0:T(8,128)} %copy-done.13, f32[312,128]{1,0:T(8,128)} %copy-done.15, f32[312,128]{1,0:T(8,128)} %copy-done.12, ...), custom_call_target="tpu_custom_call" | custom-call | bytes 2678808 | tf_op jit(solution)/shard_map/pallas_call | solution.py:73
  116.0 9.5 %shard_map.102 = (f32[1536,128]{1,0:T(8,128)}, f32[1536,128]{1,0:T(8,128)}, f32[1536,128]{1,0:T(8,128)}, f32[1536,128]{1,0:T(8,128)}, f32[8,128]{1,0:T(8,128)}, ...) custom-call(s32[1,6]{1,0:T(1,128)} %refs_0_.13, s32[1,24]{1,0:T(1,128)} %refs_1_.11, ...), custom_call_target="tpu_custom_call" | custom-call | bytes 13267736 | tf_op jit(solution)/shard_map/pallas_call | solution.py:73
  125.5 6.2 %all-to-all-start.3 = ((f32[32,24,128]{2,1,0:T(8,128)}), f32[32,24,128]{2,1,0:T(8,128)S(1)}, u32[]{:S(2)}, u32[]{:S(2)}) async-start(f32[32,24,128]{2,1,0:T(8,128)} %bitcast.18), calls=%async_computation.3 | async-start | bytes 786432 | tf_op jit(solution)/shard_map/all_to_all | solution.py:395
  131.7 6.5 %shard_map.103 = (f32[256,128]{1,0:T(8,128)}, f32[256,128]{1,0:T(8,128)}, f32[256,128]{1,0:T(8,128)}, f32[256,128]{1,0:T(8,128)}, f32[256,128]{1,0:T(8,128)}, /*...) custom-call(bf16[1536,1536]{1,0:T(8,128)(2,1)} %get-tuple-element.106.schur, ...), custom_call_target="tpu_custom_call" | custom-call | flops 603979776 | bytes 7479296 | tf_op jit(solution)/shard_map/pallas_call | solution.py:73
  151.3 8.0 %collective-permute-done.14.refs_2_.refs_10_ = f32[256,128]{1,0:T(8,128)S(1)} collective-permute-done((f32[256,128]{1,0:T(8,128)}, f32[256,128]{1,0:T(8,128)S(1)}, u32[]{:S(2)}, u32[]{:S(2)}) %collective-permute-start.14) | collective-permute-done | bytes 131104 | tf_op jit(solution)/shard_map/ppermute | solution.py:52
  162.3 7.1 %all-to-all-start.5 = ((f32[32,32,128]{2,1,0:T(8,128)}), f32[32,32,128]{2,1,0:T(8,128)S(1)}, u32[]{:S(2)}, u32[]{:S(2)}) async-start(f32[32,32,128]{2,1,0:T(8,128)} %shard_map.105), calls=%async_computation.5 | async-start | bytes 1048576 | tf_op jit(solution)/shard_map/all_to_all | solution.py:410
  169.5 6.4 %collective-permute-start.15 = (f32[256,128]{1,0:T(8,128)S(1)}, f32[256,128]{1,0:T(8,128)S(1)}, u32[]{:S(2)}, u32[]{:S(2)}) collective-permute-start(f32[256,128]{1,0:T(8,128)S(1)} %copy-done.62), channel_id=1, source_target_pairs={{16,0},{17,1},{18,2},{19,3},{20,4},{21,5},{22,6},{23,7},{24,8},{25... | collective-permute-start | bytes 393224 | tf_op jit(solution)/shard_map/ppermute | solution.py:52
  175.9 4.9 %collective-permute-start.16 = (f32[256,128]{1,0:T(8,128)S(1)}, f32[256,128]{1,0:T(8,128)S(1)}, u32[]{:S(2)}, u32[]{:S(2)}) collective-permute-start(f32[256,128]{1,0:T(8,128)S(1)} %copy-done.58), channel_id=1, source_target_pairs={{0,4},{1,5},{2,6},{3,7},{4,8},{5,9},{6,10},{7,11},{8,12},{9,13},{1... | collective-permute-start | bytes 393224 | tf_op jit(solution)/shard_map/ppermute | solution.py:52
  183.6 8.3 %collective-permute-done.17.refs_14_ = f32[256,128]{1,0:T(8,128)S(1)} collective-permute-done((f32[256,128]{1,0:T(8,128)S(1)}, f32[256,128]{1,0:T(8,128)S(1)}, u32[]{:S(2)}, u32[]{:S(2)}) %collective-permute-start.17) | collective-permute-done | bytes 131104 | tf_op jit(solution)/shard_map/ppermute | solution.py:52
  192.7 10.0 %shard_map.106 = (f32[1536,128]{1,0:T(8,128)}, f32[1536,128]{1,0:T(8,128)}, f32[1536,128]{1,0:T(8,128)}, f32[1536,128]{1,0:T(8,128)}, f32[8,128]{1,0:T(8,128)}, ...) custom-call(s32[1,6]{1,0:T(1,128)} %refs_0_.13, s32[1,24]{1,0:T(1,128)} %refs_1_.11, ...), custom_call_target="tpu_custom_call" | custom-call | bytes 15627032 | tf_op jit(solution)/shard_map/pallas_call | solution.py:73
  202.7 4.8 %all-to-all-start.6 = ((f32[32,24,128]{2,1,0:T(8,128)}), f32[32,24,128]{2,1,0:T(8,128)S(1)}, u32[]{:S(2)}, u32[]{:S(2)}) async-start(f32[32,24,128]{2,1,0:T(8,128)} %bitcast.16), calls=%async_computation.6 | async-start | bytes 786432 | tf_op jit(solution)/shard_map/all_to_all | solution.py:395
  207.5 6.5 %shard_map.107 = (f32[256,128]{1,0:T(8,128)}, f32[256,128]{1,0:T(8,128)}, f32[256,128]{1,0:T(8,128)}, f32[256,128]{1,0:T(8,128)}, f32[256,128]{1,0:T(8,128)}, /*...) custom-call(bf16[1536,1536]{1,0:T(8,128)(2,1)} %get-tuple-element.106.schur, ...), custom_call_target="tpu_custom_call" | custom-call | flops 603979776 | bytes 7479296 | tf_op jit(solution)/shard_map/pallas_call | solution.py:73
  218.0 3.8 all-to-all-start.7
  227.5 8.2 %collective-permute-done.20.refs_2_.refs_10_ = f32[256,128]{1,0:T(8,128)S(1)} collective-permute-done((f32[256,128]{1,0:T(8,128)}, f32[256,128]{1,0:T(8,128)S(1)}, u32[]{:S(2)}, u32[]{:S(2)}) %collective-permute-start.20) | collective-permute-done | bytes 131104 | tf_op jit(solution)/shard_map/ppermute | solution.py:52
  238.8 7.1 %all-to-all-start.8 = ((f32[32,32,128]{2,1,0:T(8,128)}), f32[32,32,128]{2,1,0:T(8,128)S(1)}, u32[]{:S(2)}, u32[]{:S(2)}) async-start(f32[32,32,128]{2,1,0:T(8,128)} %shard_map.109), calls=%async_computation.8 | async-start | bytes 1048576 | tf_op jit(solution)/shard_map/all_to_all | solution.py:410
  245.9 6.3 %collective-permute-start.21 = (f32[256,128]{1,0:T(8,128)S(1)}, f32[256,128]{1,0:T(8,128)S(1)}, u32[]{:S(2)}, u32[]{:S(2)}) collective-permute-start(f32[256,128]{1,0:T(8,128)S(1)} %copy-done.63), channel_id=1, source_target_pairs={{16,0},{17,1},{18,2},{19,3},{20,4},{21,5},{22,6},{23,7},{24,8},{25... | collective-permute-start | bytes 393224 | tf_op jit(solution)/shard_map/ppermute | solution.py:52
  252.2 4.9 %collective-permute-start.22 = (f32[256,128]{1,0:T(8,128)S(1)}, f32[256,128]{1,0:T(8,128)S(1)}, u32[]{:S(2)}, u32[]{:S(2)}) collective-permute-start(f32[256,128]{1,0:T(8,128)S(1)} %copy-done.59), channel_id=1, source_target_pairs={{0,4},{1,5},{2,6},{3,7},{4,8},{5,9},{6,10},{7,11},{8,12},{9,13},{1... | collective-permute-start | bytes 393224 | tf_op jit(solution)/shard_map/ppermute | solution.py:52
  259.9 8.3 %collective-permute-done.23.refs_14_ = f32[256,128]{1,0:T(8,128)S(1)} collective-permute-done((f32[256,128]{1,0:T(8,128)S(1)}, f32[256,128]{1,0:T(8,128)S(1)}, u32[]{:S(2)}, u32[]{:S(2)}) %collective-permute-start.23) | collective-permute-done | bytes 131104 | tf_op jit(solution)/shard_map/ppermute | solution.py:52
  269.0 10.1 %shard_map.110 = (f32[1536,128]{1,0:T(8,128)}, f32[1536,128]{1,0:T(8,128)}, f32[1536,128]{1,0:T(8,128)}, f32[1536,128]{1,0:T(8,128)}, f32[8,128]{1,0:T(8,128)}, ...) custom-call(s32[1,6]{1,0:T(1,128)} %refs_0_.13, s32[1,24]{1,0:T(1,128)} %refs_1_.11, ...), custom_call_target="tpu_custom_call" | custom-call | bytes 15627032 | tf_op jit(solution)/shard_map/pallas_call | solution.py:73
  279.1 4.8 %all-to-all-start.9 = ((f32[32,24,128]{2,1,0:T(8,128)}), f32[32,24,128]{2,1,0:T(8,128)S(1)}, u32[]{:S(2)}, u32[]{:S(2)}) async-start(f32[32,24,128]{2,1,0:T(8,128)} %bitcast.17), calls=%async_computation.9 | async-start | bytes 786432 | tf_op jit(solution)/shard_map/all_to_all | solution.py:395
  283.9 6.5 %shard_map.111 = (f32[256,128]{1,0:T(8,128)}, f32[256,128]{1,0:T(8,128)}, f32[256,128]{1,0:T(8,128)}, f32[256,128]{1,0:T(8,128)}, f32[256,128]{1,0:T(8,128)}, /*...) custom-call(bf16[1536,1536]{1,0:T(8,128)(2,1)} %get-tuple-element.106.schur, ...), custom_call_target="tpu_custom_call" | custom-call | flops 603979776 | bytes 7479296 | tf_op jit(solution)/shard_map/pallas_call | solution.py:73
  303.7 8.2 %collective-permute-done.26.refs_2_.refs_10_ = f32[256,128]{1,0:T(8,128)S(1)} collective-permute-done((f32[256,128]{1,0:T(8,128)}, f32[256,128]{1,0:T(8,128)S(1)}, u32[]{:S(2)}, u32[]{:S(2)}) %collective-permute-start.26) | collective-permute-done | bytes 131104 | tf_op jit(solution)/shard_map/ppermute | solution.py:52
  315.0 7.1 %all-to-all-start.11 = ((f32[32,32,128]{2,1,0:T(8,128)}), f32[32,32,128]{2,1,0:T(8,128)S(1)}, u32[]{:S(2)}, u32[]{:S(2)}) async-start(f32[32,32,128]{2,1,0:T(8,128)} %shard_map.113), calls=%async_computation.11 | async-start | bytes 1048576 | tf_op jit(solution)/shard_map/all_to_all | solution.py:410
  322.1 6.3 %collective-permute-start.27 = (f32[256,128]{1,0:T(8,128)S(1)}, f32[256,128]{1,0:T(8,128)S(1)}, u32[]{:S(2)}, u32[]{:S(2)}) collective-permute-start(f32[256,128]{1,0:T(8,128)S(1)} %copy-done.64), channel_id=1, source_target_pairs={{16,0},{17,1},{18,2},{19,3},{20,4},{21,5},{22,6},{23,7},{24,8},{25... | collective-permute-start | bytes 393224 | tf_op jit(solution)/shard_map/ppermute | solution.py:52
  328.4 4.9 %collective-permute-start.28 = (f32[256,128]{1,0:T(8,128)S(1)}, f32[256,128]{1,0:T(8,128)S(1)}, u32[]{:S(2)}, u32[]{:S(2)}) collective-permute-start(f32[256,128]{1,0:T(8,128)S(1)} %copy-done.60), channel_id=1, source_target_pairs={{0,4},{1,5},{2,6},{3,7},{4,8},{5,9},{6,10},{7,11},{8,12},{9,13},{1... | collective-permute-start | bytes 393224 | tf_op jit(solution)/shard_map/ppermute | solution.py:52
  336.1 8.3 %collective-permute-done.29.refs_14_ = f32[256,128]{1,0:T(8,128)S(1)} collective-permute-done((f32[256,128]{1,0:T(8,128)S(1)}, f32[256,128]{1,0:T(8,128)S(1)}, u32[]{:S(2)}, u32[]{:S(2)}) %collective-permute-start.29) | collective-permute-done | bytes 131104 | tf_op jit(solution)/shard_map/ppermute | solution.py:52
  345.2 10.1 %shard_map.114 = (f32[1536,128]{1,0:T(8,128)}, f32[1536,128]{1,0:T(8,128)}, f32[1536,128]{1,0:T(8,128)}, f32[1536,128]{1,0:T(8,128)}, f32[8,128]{1,0:T(8,128)}, ...) custom-call(s32[1,6]{1,0:T(1,128)} %refs_0_.13, s32[1,24]{1,0:T(1,128)} %refs_1_.11, ...), custom_call_target="tpu_custom_call" | custom-call | bytes 15627032 | tf_op jit(solution)/shard_map/pallas_call | solution.py:73
  355.3 4.8 %all-to-all-start.12 = ((f32[32,24,128]{2,1,0:T(8,128)}), f32[32,24,128]{2,1,0:T(8,128)S(1)}, u32[]{:S(2)}, u32[]{:S(2)}) async-start(f32[32,24,128]{2,1,0:T(8,128)} %bitcast.15), calls=%async_computation.12 | async-start | bytes 786432 | tf_op jit(solution)/shard_map/all_to_all | solution.py:395
  360.1 6.5 %shard_map.115 = (f32[256,128]{1,0:T(8,128)}, f32[256,128]{1,0:T(8,128)}, f32[256,128]{1,0:T(8,128)}, f32[256,128]{1,0:T(8,128)}, f32[256,128]{1,0:T(8,128)}, /*...) custom-call(bf16[1536,1536]{1,0:T(8,128)(2,1)} %get-tuple-element.106.schur, ...), custom_call_target="tpu_custom_call" | custom-call | flops 603979776 | bytes 7479296 | tf_op jit(solution)/shard_map/pallas_call | solution.py:73
  370.6 3.7 all-to-all-start.13
  379.9 8.2 %collective-permute-done.32.refs_2_.refs_10_ = f32[256,128]{1,0:T(8,128)S(1)} collective-permute-done((f32[256,128]{1,0:T(8,128)}, f32[256,128]{1,0:T(8,128)S(1)}, u32[]{:S(2)}, u32[]{:S(2)}) %collective-permute-start.32) | collective-permute-done | bytes 131104 | tf_op jit(solution)/shard_map/ppermute | solution.py:52
  391.2 7.1 %all-to-all-start.14 = ((f32[32,32,128]{2,1,0:T(8,128)}), f32[32,32,128]{2,1,0:T(8,128)S(1)}, u32[]{:S(2)}, u32[]{:S(2)}) async-start(f32[32,32,128]{2,1,0:T(8,128)} %shard_map.117), calls=%async_computation.14 | async-start | bytes 1048576 | tf_op jit(solution)/shard_map/all_to_all | solution.py:410
  398.3 6.3 %collective-permute-start.33 = (f32[256,128]{1,0:T(8,128)S(1)}, f32[256,128]{1,0:T(8,128)S(1)}, u32[]{:S(2)}, u32[]{:S(2)}) collective-permute-start(f32[256,128]{1,0:T(8,128)S(1)} %copy-done.61), channel_id=1, source_target_pairs={{16,0},{17,1},{18,2},{19,3},{20,4},{21,5},{22,6},{23,7},{24,8},{25... | collective-permute-start | bytes 393224 | tf_op jit(solution)/shard_map/ppermute | solution.py:52
  404.6 4.9 %collective-permute-start.34 = (f32[256,128]{1,0:T(8,128)S(1)}, f32[256,128]{1,0:T(8,128)S(1)}, u32[]{:S(2)}, u32[]{:S(2)}) collective-permute-start(f32[256,128]{1,0:T(8,128)S(1)} %copy-done.57), channel_id=1, source_target_pairs={{0,4},{1,5},{2,6},{3,7},{4,8},{5,9},{6,10},{7,11},{8,12},{9,13},{1... | collective-permute-start | bytes 393224 | tf_op jit(solution)/shard_map/ppermute | solution.py:52
  412.3 8.3 %collective-permute-done.35.refs_14_ = f32[256,128]{1,0:T(8,128)S(1)} collective-permute-done((f32[256,128]{1,0:T(8,128)S(1)}, f32[256,128]{1,0:T(8,128)S(1)}, u32[]{:S(2)}, u32[]{:S(2)}) %collective-permute-start.35) | collective-permute-done | bytes 131104 | tf_op jit(solution)/shard_map/ppermute | solution.py:52
  421.4 9.4 %shard_map.118 = (f32[1536,128]{1,0:T(8,128)}, f32[1536,128]{1,0:T(8,128)}) custom-call(s32[1,6]{1,0:T(1,128)} %refs_0_.13, s32[1,24]{1,0:T(1,128)} %refs_1_.11, s32[1,168]{1,0:T(1,128)} %concatenate.3.refs_2_, f32[32,32,128]{2,1,0:T(8,128)} %copy-done.5, bf16[768,768]{1,0:T(8,128)(2,1)} %get-tuple-element.193.refs_4_, ...), custom_call_target="tpu_custom_call" | custom-call | bytes 12331800 | tf_op jit(solution)/shard_map/pallas_call | solution.py:73
  (221 shorter events, 110.3 us)
Async XLA Ops:
  5.9 20.8 %collective-permute-start = (f32[312,128]{1,0:T(8,128)}, f32[312,128]{1,0:T(8,128)S(1)}, u32[]{:S(2)}, u32[]{:S(2)}) collective-permute-start(f32[312,128]{1,0:T(8,128)} %get-tuple-element.97.refs_5_), channel_id=1, source_target_pairs={{1,0},{2,1},{3,2},{5,4},{6,5},{7,6},{9,8},{10,9},{11,10},{13,12},{... | collective-permute-start | bytes 479240 | tf_op jit(solution)/shard_map/ppermute | solution.py:52
  7.2 29.3 %collective-permute-start.1 = (f32[312,128]{1,0:T(8,128)}, f32[312,128]{1,0:T(8,128)S(1)}, u32[]{:S(2)}, u32[]{:S(2)}) collective-permute-start(f32[312,128]{1,0:T(8,128)} %get-tuple-element.98.refs_4_), channel_id=1, source_target_pairs={{0,1},{1,2},{2,3},{4,5},{5,6},{6,7},{8,9},{9,10},{10,11},{12,13},{... | collective-permute-start | bytes 479240 | tf_op jit(solution)/shard_map/ppermute | solution.py:52
  10.3 26.3 %collective-permute-start.2 = (f32[312,128]{1,0:T(8,128)}, f32[312,128]{1,0:T(8,128)S(1)}, u32[]{:S(2)}, u32[]{:S(2)}) collective-permute-start(f32[312,128]{1,0:T(8,128)} %get-tuple-element.99.refs_7_), channel_id=1, source_target_pairs={{4,0},{5,1},{6,2},{7,3},{8,4},{9,5},{10,6},{11,7},{12,8},{13,9},{1... | collective-permute-start | bytes 479240 | tf_op jit(solution)/shard_map/ppermute | solution.py:52
  11.6 25.0 %collective-permute-start.3 = (f32[312,128]{1,0:T(8,128)}, f32[312,128]{1,0:T(8,128)S(1)}, u32[]{:S(2)}, u32[]{:S(2)}) collective-permute-start(f32[312,128]{1,0:T(8,128)} %get-tuple-element.100.refs_6_), channel_id=1, source_target_pairs={{0,4},{1,5},{2,6},{3,7},{4,8},{5,9},{6,10},{7,11},{8,12},{9,13},{1... | collective-permute-start | bytes 479240 | tf_op jit(solution)/shard_map/ppermute | solution.py:52
  17.6 19.0 %collective-permute-start.4 = (f32[312,128]{1,0:T(8,128)}, f32[312,128]{1,0:T(8,128)S(1)}, u32[]{:S(2)}, u32[]{:S(2)}) collective-permute-start(f32[312,128]{1,0:T(8,128)} %get-tuple-element.101.refs_9_), channel_id=1, source_target_pairs={{16,0},{17,1},{18,2},{19,3},{20,4},{21,5},{22,6},{23,7},{24,8},{25... | collective-permute-start | bytes 479240 | tf_op jit(solution)/shard_map/ppermute | solution.py:52
  26.8 14.4 %collective-permute-start.5 = (f32[312,128]{1,0:T(8,128)}, f32[312,128]{1,0:T(8,128)S(1)}, u32[]{:S(2)}, u32[]{:S(2)}) collective-permute-start(f32[312,128]{1,0:T(8,128)} %get-tuple-element.102.refs_8_), channel_id=1, source_target_pairs={{0,16},{1,17},{2,18},{3,19},{4,20},{5,21},{6,22},{7,23},{8,24},{9,... | collective-permute-start | bytes 479240 | tf_op jit(solution)/shard_map/ppermute | solution.py:52
  47.7 31.6 %all-to-all-start = ((f32[32,24,128]{2,1,0:T(8,128)}), f32[32,24,128]{2,1,0:T(8,128)S(1)}, u32[]{:S(2)}, u32[]{:S(2)}) async-start(f32[32,24,128]{2,1,0:T(8,128)} %bitcast.14), calls=%async_computation | async-start | bytes 786432 | tf_op jit(solution)/shard_map/all_to_all | solution.py:395
  61.1 25.5 %collective-permute-start.6 = (f32[256,128]{1,0:T(8,128)}, f32[256,128]{1,0:T(8,128)S(1)}, u32[]{:S(2)}, u32[]{:S(2)}) collective-permute-start(f32[256,128]{1,0:T(8,128)} %get-tuple-element.111), channel_id=1, source_target_pairs={{1,0},{2,1},{3,2},{5,4},{6,5},{7,6},{9,8},{10,9},{11,10},{13,12},{... | collective-permute-start | bytes 393224 | tf_op jit(solution)/shard_map/ppermute | solution.py:52
  62.4 28.9 %collective-permute-start.7 = (f32[256,128]{1,0:T(8,128)}, f32[256,128]{1,0:T(8,128)S(1)}, u32[]{:S(2)}, u32[]{:S(2)}) collective-permute-start(f32[256,128]{1,0:T(8,128)} %get-tuple-element.112), channel_id=1, source_target_pairs={{0,1},{1,2},{2,3},{4,5},{5,6},{6,7},{8,9},{9,10},{10,11},{12,13},{... | collective-permute-start | bytes 393224 | tf_op jit(solution)/shard_map/ppermute | solution.py:52
  65.4 25.9 %collective-permute-start.8 = (f32[256,128]{1,0:T(8,128)}, f32[256,128]{1,0:T(8,128)S(1)}, u32[]{:S(2)}, u32[]{:S(2)}) collective-permute-start(f32[256,128]{1,0:T(8,128)} %get-tuple-element.113), channel_id=1, source_target_pairs={{4,0},{5,1},{6,2},{7,3},{8,4},{9,5},{10,6},{11,7},{12,8},{13,9},{1... | collective-permute-start | bytes 393224 | tf_op jit(solution)/shard_map/ppermute | solution.py:52
  66.7 46.5 %collective-permute-start.9 = (f32[256,128]{1,0:T(8,128)}, f32[256,128]{1,0:T(8,128)S(1)}, u32[]{:S(2)}, u32[]{:S(2)}) collective-permute-start(f32[256,128]{1,0:T(8,128)} %get-tuple-element.118), channel_id=1, source_target_pairs={{16,0},{17,1},{18,2},{19,3},{20,4},{21,5},{22,6},{23,7},{24,8},{25... | collective-permute-start | bytes 393224 | tf_op jit(solution)/shard_map/ppermute | solution.py:52
  72.6 40.7 %collective-permute-start.10 = (f32[256,128]{1,0:T(8,128)}, f32[256,128]{1,0:T(8,128)S(1)}, u32[]{:S(2)}, u32[]{:S(2)}) collective-permute-start(f32[256,128]{1,0:T(8,128)} %get-tuple-element.119), channel_id=1, source_target_pairs={{0,4},{1,5},{2,6},{3,7},{4,8},{5,9},{6,10},{7,11},{8,12},{9,13},{1... | collective-permute-start | bytes 393224 | tf_op jit(solution)/shard_map/ppermute | solution.py:52
  81.8 13.3 %all-to-all-start.1 = ((f32[8,32,128]{2,1,0:T(8,128)}), f32[8,32,128]{2,1,0:T(8,128)S(1)}, u32[]{:S(2)}, u32[]{:S(2)}) async-start(f32[8,32,128]{2,1,0:T(8,128)} %shard_map.99), calls=%async_computation.1 | async-start | bytes 262144 | tf_op jit(solution)/shard_map/all_to_all | solution.py:408
  86.5 26.7 %collective-permute-start.11 = (f32[256,128]{1,0:T(8,128)}, f32[256,128]{1,0:T(8,128)S(1)}, u32[]{:S(2)}, u32[]{:S(2)}) collective-permute-start(f32[256,128]{1,0:T(8,128)} %get-tuple-element.120), channel_id=1, source_target_pairs={{0,16},{1,17},{2,18},{3,19},{4,20},{5,21},{6,22},{7,23},{8,24},{9,... | collective-permute-start | bytes 393224 | tf_op jit(solution)/shard_map/ppermute | solution.py:52
  97.6 17.6 %all-to-all-start.2 = ((f32[32,32,128]{2,1,0:T(8,128)}), f32[32,32,128]{2,1,0:T(8,128)S(1)}, u32[]{:S(2)}, u32[]{:S(2)}) async-start(f32[32,32,128]{2,1,0:T(8,128)} %shard_map.100), calls=%async_computation.2 | async-start | bytes 1048576 | tf_op jit(solution)/shard_map/all_to_all | solution.py:410
  125.5 14.3 %all-to-all-start.3 = ((f32[32,24,128]{2,1,0:T(8,128)}), f32[32,24,128]{2,1,0:T(8,128)S(1)}, u32[]{:S(2)}, u32[]{:S(2)}) async-start(f32[32,24,128]{2,1,0:T(8,128)} %bitcast.18), calls=%async_computation.3 | async-start | bytes 786432 | tf_op jit(solution)/shard_map/all_to_all | solution.py:395
  142.2 17.0 %all-to-all-start.4 = ((f32[8,32,128]{2,1,0:T(8,128)}), f32[8,32,128]{2,1,0:T(8,128)S(1)}, u32[]{:S(2)}, u32[]{:S(2)}) async-start(f32[8,32,128]{2,1,0:T(8,128)} %shard_map.104), calls=%async_computation.4 | async-start | bytes 262144 | tf_op jit(solution)/shard_map/all_to_all | solution.py:408
  145.6 5.6 %collective-permute-start.12 = (f32[256,128]{1,0:T(8,128)}, f32[256,128]{1,0:T(8,128)S(1)}, u32[]{:S(2)}, u32[]{:S(2)}) collective-permute-start(f32[256,128]{1,0:T(8,128)} %get-tuple-element.127), channel_id=1, source_target_pairs={{1,0},{2,1},{3,2},{5,4},{6,5},{7,6},{9,8},{10,9},{11,10},{13,12},{... | collective-permute-start | bytes 393224 | tf_op jit(solution)/shard_map/ppermute | solution.py:52
  149.9 9.3 %collective-permute-start.14 = (f32[256,128]{1,0:T(8,128)}, f32[256,128]{1,0:T(8,128)S(1)}, u32[]{:S(2)}, u32[]{:S(2)}) collective-permute-start(f32[256,128]{1,0:T(8,128)} %get-tuple-element.129), channel_id=1, source_target_pairs={{4,0},{5,1},{6,2},{7,3},{8,4},{9,5},{10,6},{11,7},{12,8},{13,9},{1... | collective-permute-start | bytes 393224 | tf_op jit(solution)/shard_map/ppermute | solution.py:52
  162.3 29.6 %all-to-all-start.5 = ((f32[32,32,128]{2,1,0:T(8,128)}), f32[32,32,128]{2,1,0:T(8,128)S(1)}, u32[]{:S(2)}, u32[]{:S(2)}) async-start(f32[32,32,128]{2,1,0:T(8,128)} %shard_map.105), calls=%async_computation.5 | async-start | bytes 1048576 | tf_op jit(solution)/shard_map/all_to_all | solution.py:410
  169.5 13.3 %collective-permute-start.15 = (f32[256,128]{1,0:T(8,128)S(1)}, f32[256,128]{1,0:T(8,128)S(1)}, u32[]{:S(2)}, u32[]{:S(2)}) collective-permute-start(f32[256,128]{1,0:T(8,128)S(1)} %copy-done.62), channel_id=1, source_target_pairs={{16,0},{17,1},{18,2},{19,3},{20,4},{21,5},{22,6},{23,7},{24,8},{25... | collective-permute-start | bytes 393224 | tf_op jit(solution)/shard_map/ppermute | solution.py:52
  175.9 7.7 %collective-permute-start.16 = (f32[256,128]{1,0:T(8,128)S(1)}, f32[256,128]{1,0:T(8,128)S(1)}, u32[]{:S(2)}, u32[]{:S(2)}) collective-permute-start(f32[256,128]{1,0:T(8,128)S(1)} %copy-done.58), channel_id=1, source_target_pairs={{0,4},{1,5},{2,6},{3,7},{4,8},{5,9},{6,10},{7,11},{8,12},{9,13},{1... | collective-permute-start | bytes 393224 | tf_op jit(solution)/shard_map/ppermute | solution.py:52
  180.8 11.1 %collective-permute-start.17 = (f32[256,128]{1,0:T(8,128)S(1)}, f32[256,128]{1,0:T(8,128)S(1)}, u32[]{:S(2)}, u32[]{:S(2)}) collective-permute-start(f32[256,128]{1,0:T(8,128)S(1)} %copy-done.54), channel_id=1, source_target_pairs={{0,16},{1,17},{2,18},{3,19},{4,20},{5,21},{6,22},{7,23},{8,24},{9,... | collective-permute-start | bytes 393224 | tf_op jit(solution)/shard_map/ppermute | solution.py:52
  202.7 12.9 %all-to-all-start.6 = ((f32[32,24,128]{2,1,0:T(8,128)}), f32[32,24,128]{2,1,0:T(8,128)S(1)}, u32[]{:S(2)}, u32[]{:S(2)}) async-start(f32[32,24,128]{2,1,0:T(8,128)} %bitcast.16), calls=%async_computation.6 | async-start | bytes 786432 | tf_op jit(solution)/shard_map/all_to_all | solution.py:395
  218.0 17.7 %all-to-all-start.7 = ((f32[8,32,128]{2,1,0:T(8,128)}), f32[8,32,128]{2,1,0:T(8,128)S(1)}, u32[]{:S(2)}, u32[]{:S(2)}) async-start(f32[8,32,128]{2,1,0:T(8,128)} %shard_map.108), calls=%async_computation.7 | async-start | bytes 262144 | tf_op jit(solution)/shard_map/all_to_all | solution.py:408
  221.9 5.6 %collective-permute-start.18 = (f32[256,128]{1,0:T(8,128)}, f32[256,128]{1,0:T(8,128)S(1)}, u32[]{:S(2)}, u32[]{:S(2)}) collective-permute-start(f32[256,128]{1,0:T(8,128)} %get-tuple-element.144), channel_id=1, source_target_pairs={{1,0},{2,1},{3,2},{5,4},{6,5},{7,6},{9,8},{10,9},{11,10},{13,12},{... | collective-permute-start | bytes 393224 | tf_op jit(solution)/shard_map/ppermute | solution.py:52
  223.1 4.4 %collective-permute-start.19 = (f32[256,128]{1,0:T(8,128)}, f32[256,128]{1,0:T(8,128)S(1)}, u32[]{:S(2)}, u32[]{:S(2)}) collective-permute-start(f32[256,128]{1,0:T(8,128)} %get-tuple-element.145), channel_id=1, source_target_pairs={{0,1},{1,2},{2,3},{4,5},{5,6},{6,7},{8,9},{9,10},{10,11},{12,13},{... | collective-permute-start | bytes 393224 | tf_op jit(solution)/shard_map/ppermute | solution.py:52
  226.2 9.5 %collective-permute-start.20 = (f32[256,128]{1,0:T(8,128)}, f32[256,128]{1,0:T(8,128)S(1)}, u32[]{:S(2)}, u32[]{:S(2)}) collective-permute-start(f32[256,128]{1,0:T(8,128)} %get-tuple-element.146), channel_id=1, source_target_pairs={{4,0},{5,1},{6,2},{7,3},{8,4},{9,5},{10,6},{11,7},{12,8},{13,9},{1... | collective-permute-start | bytes 393224 | tf_op jit(solution)/shard_map/ppermute | solution.py:52
  238.8 29.4 %all-to-all-start.8 = ((f32[32,32,128]{2,1,0:T(8,128)}), f32[32,32,128]{2,1,0:T(8,128)S(1)}, u32[]{:S(2)}, u32[]{:S(2)}) async-start(f32[32,32,128]{2,1,0:T(8,128)} %shard_map.109), calls=%async_computation.8 | async-start | bytes 1048576 | tf_op jit(solution)/shard_map/all_to_all | solution.py:410
  245.9 13.2 %collective-permute-start.21 = (f32[256,128]{1,0:T(8,128)S(1)}, f32[256,128]{1,0:T(8,128)S(1)}, u32[]{:S(2)}, u32[]{:S(2)}) collective-permute-start(f32[256,128]{1,0:T(8,128)S(1)} %copy-done.63), channel_id=1, source_target_pairs={{16,0},{17,1},{18,2},{19,3},{20,4},{21,5},{22,6},{23,7},{24,8},{25... | collective-permute-start | bytes 393224 | tf_op jit(solution)/shard_map/ppermute | solution.py:52
  252.2 7.7 %collective-permute-start.22 = (f32[256,128]{1,0:T(8,128)S(1)}, f32[256,128]{1,0:T(8,128)S(1)}, u32[]{:S(2)}, u32[]{:S(2)}) collective-permute-start(f32[256,128]{1,0:T(8,128)S(1)} %copy-done.59), channel_id=1, source_target_pairs={{0,4},{1,5},{2,6},{3,7},{4,8},{5,9},{6,10},{7,11},{8,12},{9,13},{1... | collective-permute-start | bytes 393224 | tf_op jit(solution)/shard_map/ppermute | solution.py:52
  257.1 11.0 %collective-permute-start.23 = (f32[256,128]{1,0:T(8,128)S(1)}, f32[256,128]{1,0:T(8,128)S(1)}, u32[]{:S(2)}, u32[]{:S(2)}) collective-permute-start(f32[256,128]{1,0:T(8,128)S(1)} %copy-done.55), channel_id=1, source_target_pairs={{0,16},{1,17},{2,18},{3,19},{4,20},{5,21},{6,22},{7,23},{8,24},{9,... | collective-permute-start | bytes 393224 | tf_op jit(solution)/shard_map/ppermute | solution.py:52
  279.1 12.9 %all-to-all-start.9 = ((f32[32,24,128]{2,1,0:T(8,128)}), f32[32,24,128]{2,1,0:T(8,128)S(1)}, u32[]{:S(2)}, u32[]{:S(2)}) async-start(f32[32,24,128]{2,1,0:T(8,128)} %bitcast.17), calls=%async_computation.9 | async-start | bytes 786432 | tf_op jit(solution)/shard_map/all_to_all | solution.py:395
  294.4 17.6 %all-to-all-start.10 = ((f32[8,32,128]{2,1,0:T(8,128)}), f32[8,32,128]{2,1,0:T(8,128)S(1)}, u32[]{:S(2)}, u32[]{:S(2)}) async-start(f32[8,32,128]{2,1,0:T(8,128)} %shard_map.112), calls=%async_computation.10 | async-start | bytes 262144 | tf_op jit(solution)/shard_map/all_to_all | solution.py:408
  298.1 5.6 %collective-permute-start.24 = (f32[256,128]{1,0:T(8,128)}, f32[256,128]{1,0:T(8,128)S(1)}, u32[]{:S(2)}, u32[]{:S(2)}) collective-permute-start(f32[256,128]{1,0:T(8,128)} %get-tuple-element.161), channel_id=1, source_target_pairs={{1,0},{2,1},{3,2},{5,4},{6,5},{7,6},{9,8},{10,9},{11,10},{13,12},{... | collective-permute-start | bytes 393224 | tf_op jit(solution)/shard_map/ppermute | solution.py:52
  302.4 9.6 %collective-permute-start.26 = (f32[256,128]{1,0:T(8,128)}, f32[256,128]{1,0:T(8,128)S(1)}, u32[]{:S(2)}, u32[]{:S(2)}) collective-permute-start(f32[256,128]{1,0:T(8,128)} %get-tuple-element.163), channel_id=1, source_target_pairs={{4,0},{5,1},{6,2},{7,3},{8,4},{9,5},{10,6},{11,7},{12,8},{13,9},{1... | collective-permute-start | bytes 393224 | tf_op jit(solution)/shard_map/ppermute | solution.py:52
  315.0 29.3 %all-to-all-start.11 = ((f32[32,32,128]{2,1,0:T(8,128)}), f32[32,32,128]{2,1,0:T(8,128)S(1)}, u32[]{:S(2)}, u32[]{:S(2)}) async-start(f32[32,32,128]{2,1,0:T(8,128)} %shard_map.113), calls=%async_computation.11 | async-start | bytes 1048576 | tf_op jit(solution)/shard_map/all_to_all | solution.py:410
  322.1 13.2 %collective-permute-start.27 = (f32[256,128]{1,0:T(8,128)S(1)}, f32[256,128]{1,0:T(8,128)S(1)}, u32[]{:S(2)}, u32[]{:S(2)}) collective-permute-start(f32[256,128]{1,0:T(8,128)S(1)} %copy-done.64), channel_id=1, source_target_pairs={{16,0},{17,1},{18,2},{19,3},{20,4},{21,5},{22,6},{23,7},{24,8},{25... | collective-permute-start | bytes 393224 | tf_op jit(solution)/shard_map/ppermute | solution.py:52
  328.4 7.7 %collective-permute-start.28 = (f32[256,128]{1,0:T(8,128)S(1)}, f32[256,128]{1,0:T(8,128)S(1)}, u32[]{:S(2)}, u32[]{:S(2)}) collective-permute-start(f32[256,128]{1,0:T(8,128)S(1)} %copy-done.60), channel_id=1, source_target_pairs={{0,4},{1,5},{2,6},{3,7},{4,8},{5,9},{6,10},{7,11},{8,12},{9,13},{1... | collective-permute-start | bytes 393224 | tf_op jit(solution)/shard_map/ppermute | solution.py:52
  333.3 11.0 %collective-permute-start.29 = (f32[256,128]{1,0:T(8,128)S(1)}, f32[256,128]{1,0:T(8,128)S(1)}, u32[]{:S(2)}, u32[]{:S(2)}) collective-permute-start(f32[256,128]{1,0:T(8,128)S(1)} %copy-done.56), channel_id=1, source_target_pairs={{0,16},{1,17},{2,18},{3,19},{4,20},{5,21},{6,22},{7,23},{8,24},{9,... | collective-permute-start | bytes 393224 | tf_op jit(solution)/shard_map/ppermute | solution.py:52
  355.3 12.9 %all-to-all-start.12 = ((f32[32,24,128]{2,1,0:T(8,128)}), f32[32,24,128]{2,1,0:T(8,128)S(1)}, u32[]{:S(2)}, u32[]{:S(2)}) async-start(f32[32,24,128]{2,1,0:T(8,128)} %bitcast.15), calls=%async_computation.12 | async-start | bytes 786432 | tf_op jit(solution)/shard_map/all_to_all | solution.py:395
  370.6 17.6 %all-to-all-start.13 = ((f32[8,32,128]{2,1,0:T(8,128)}), f32[8,32,128]{2,1,0:T(8,128)S(1)}, u32[]{:S(2)}, u32[]{:S(2)}) async-start(f32[8,32,128]{2,1,0:T(8,128)} %shard_map.116), calls=%async_computation.13 | async-start | bytes 262144 | tf_op jit(solution)/shard_map/all_to_all | solution.py:408
  374.2 5.6 %collective-permute-start.30 = (f32[256,128]{1,0:T(8,128)}, f32[256,128]{1,0:T(8,128)S(1)}, u32[]{:S(2)}, u32[]{:S(2)}) collective-permute-start(f32[256,128]{1,0:T(8,128)} %get-tuple-element.178), channel_id=1, source_target_pairs={{1,0},{2,1},{3,2},{5,4},{6,5},{7,6},{9,8},{10,9},{11,10},{13,12},{... | collective-permute-start | bytes 393224 | tf_op jit(solution)/shard_map/ppermute | solution.py:52
  378.6 9.6 %collective-permute-start.32 = (f32[256,128]{1,0:T(8,128)}, f32[256,128]{1,0:T(8,128)S(1)}, u32[]{:S(2)}, u32[]{:S(2)}) collective-permute-start(f32[256,128]{1,0:T(8,128)} %get-tuple-element.180), channel_id=1, source_target_pairs={{4,0},{5,1},{6,2},{7,3},{8,4},{9,5},{10,6},{11,7},{12,8},{13,9},{1... | collective-permute-start | bytes 393224 | tf_op jit(solution)/shard_map/ppermute | solution.py:52
  391.2 29.3 %all-to-all-start.14 = ((f32[32,32,128]{2,1,0:T(8,128)}), f32[32,32,128]{2,1,0:T(8,128)S(1)}, u32[]{:S(2)}, u32[]{:S(2)}) async-start(f32[32,32,128]{2,1,0:T(8,128)} %shard_map.117), calls=%async_computation.14 | async-start | bytes 1048576 | tf_op jit(solution)/shard_map/all_to_all | solution.py:410
  398.3 13.1 %collective-permute-start.33 = (f32[256,128]{1,0:T(8,128)S(1)}, f32[256,128]{1,0:T(8,128)S(1)}, u32[]{:S(2)}, u32[]{:S(2)}) collective-permute-start(f32[256,128]{1,0:T(8,128)S(1)} %copy-done.61), channel_id=1, source_target_pairs={{16,0},{17,1},{18,2},{19,3},{20,4},{21,5},{22,6},{23,7},{24,8},{25... | collective-permute-start | bytes 393224 | tf_op jit(solution)/shard_map/ppermute | solution.py:52
  404.6 7.7 %collective-permute-start.34 = (f32[256,128]{1,0:T(8,128)S(1)}, f32[256,128]{1,0:T(8,128)S(1)}, u32[]{:S(2)}, u32[]{:S(2)}) collective-permute-start(f32[256,128]{1,0:T(8,128)S(1)} %copy-done.57), channel_id=1, source_target_pairs={{0,4},{1,5},{2,6},{3,7},{4,8},{5,9},{6,10},{7,11},{8,12},{9,13},{1... | collective-permute-start | bytes 393224 | tf_op jit(solution)/shard_map/ppermute | solution.py:52
  409.5 11.0 %collective-permute-start.35 = (f32[256,128]{1,0:T(8,128)S(1)}, f32[256,128]{1,0:T(8,128)S(1)}, u32[]{:S(2)}, u32[]{:S(2)}) collective-permute-start(f32[256,128]{1,0:T(8,128)S(1)} %copy-done.53), channel_id=1, source_target_pairs={{0,16},{1,17},{2,18},{3,19},{4,20},{5,21},{6,22},{7,23},{8,24},{9,... | collective-permute-start | bytes 393224 | tf_op jit(solution)/shard_map/ppermute | solution.py:52
  (68 other events, 728.0 us)

commit v6 on v5

--- a/solution.py
+++ b/solution.py
@@ -21,7 +21,7 @@
 NEAR = 256
 DOTS = 8
 TURN = (0, 2, 4, 1, 3, 5)
-EARLY = (0, 1, 2)
+EARLY = (0, 1)
 PACKED = FD + 2 * CORNERS + 8
 PLACES = np.arange(NSUB).reshape(4, 8, 8)
 PLANES = PLACES.transpose(1, 0, 2).reshape(8, 32).tolist()

time: 435 us -> 428 us (0.984)
  waiting for transfers between devices: 85.3 us -> 79.2 us
    ppermute x36, waiting for transfers between devices: 73.5 us -> 49.9 us  [swap_faces(): lax.ppermute(blocks[f ^ 1], 'sub', UP[f // 2] if f % 2 else DOWN[f // 2])]
    all_to_all x5, waiting for transfers between devices: 3.83 us -> 21.4 us  [shards(): lines = lax.all_to_all(lines, 'sub', 0, 0, axis_index_groups=LINES)]
    all_to_all x5, starting transfers between devices: 36.5 us -> 31.3 us  [shards(): whole = lax.all_to_all(whole, 'sub', 0, 0, axis_index_groups=PLANES)]
    all_to_all x5, starting transfers between devices: 25.6 us -> 30.1 us  [shards(): lax.all_to_all(spread.reshape(PLANE, ROWS, LOADS), 'sub', 0, 0, axis_inde...]
    unnamed x131 -> x139, local copies, waits for them, and re-layouts: 15.7 us -> 13.1 us
  transfers between devices with their start and end apart: 51 -> 51, of which waited for: 19 -> 23; matrix products, arithmetic and copies ran while one was open for 2% -> 2% of each run, Pallas kernels for 11% -> 11%
where the time goes in v6:
time: 428 us; the launch traced here: 424 us
  starting transfers between devices  201 us (47%)
  Pallas kernels  119 us (28%)
  waiting for transfers between devices  79.2 us (19%)
  local copies, waits for them, and re-layouts  15.5 us (4%)
  other arithmetic  7.17 us (2%)
    ppermute x36, starting transfers between devices, swap_faces(): lax.ppermute(blocks[f ^ 1], 'sub', UP[f // 2] if f % 2 else DOWN[f // 2])  122 us
    pallas_call x24, Pallas kernels, call(): pl.pallas_call(kernel, grid=(steps,), out_shape=[jax.ShapeDtypeStruct(s,...  119 us
    ppermute x36, waiting for transfers between devices, swap_faces(): lax.ppermute(blocks[f ^ 1], 'sub', UP[f // 2] if f % 2 else DOWN[f // 2])  49.9 us
    all_to_all x5, starting transfers between devices, shards(): whole = lax.all_to_all(whole, 'sub', 0, 0, axis_index_groups=PLANES)  31.3 us
    all_to_all x5, starting transfers between devices, shards(): lax.all_to_all(spread.reshape(PLANE, ROWS, LOADS), 'sub', 0, 0, axis_inde...  30.1 us
    all_to_all x5, waiting for transfers between devices, shards(): lines = lax.all_to_all(lines, 'sub', 0, 0, axis_index_groups=LINES)  21.4 us
    all_to_all x5, starting transfers between devices, shards(): lines = lax.all_to_all(lines, 'sub', 0, 0, axis_index_groups=LINES)  17 us
    unnamed x139, local copies, waits for them, and re-layouts  13.1 us
  transfers between devices with their start and end apart: 51, of which 23 were waited for; matrix products, arithmetic and copies ran while one was open for 2% of the time, Pallas kernels for 11%

profile of v6, /device:TPU:24, one launch (start us, length us, event | category | flops | bytes accessed | tf_op | source)
XLA Modules:
  0.0 423.7 jit_solution(5566306420755449366)
XLA Ops:
  11.6 6.1 %collective-permute-start.3 = (f32[312,128]{1,0:T(8,128)}, f32[312,128]{1,0:T(8,128)S(1)}, u32[]{:S(2)}, u32[]{:S(2)}) collective-permute-start(f32[312,128]{1,0:T(8,128)} %get-tuple-element.100.refs_6_), channel_id=1, source_target_pairs={{0,4},{1,5},{2,6},{3,7},{4,8},{5,9},{6,10},{7,11},{8,12},{9,13},{1... | collective-permute-start | bytes 479240 | tf_op jit(solution)/shard_map/ppermute | solution.py:52
  17.6 8.4 %collective-permute-start.4 = (f32[312,128]{1,0:T(8,128)}, f32[312,128]{1,0:T(8,128)S(1)}, u32[]{:S(2)}, u32[]{:S(2)}) collective-permute-start(f32[312,128]{1,0:T(8,128)} %get-tuple-element.101.refs_9_), channel_id=1, source_target_pairs={{16,0},{17,1},{18,2},{19,3},{20,4},{21,5},{22,6},{23,7},{24,8},{25... | collective-permute-start | bytes 479240 | tf_op jit(solution)/shard_map/ppermute | solution.py:52
  29.8 6.7 %shard_map.96 = (bf16[1536,1536]{1,0:T(8,128)(2,1)}, f32[1536,128]{1,0:T(8,128)}) custom-call(bf16[1536,1536]{1,0:T(8,128)(2,1)} %bitcast.23, s32[6,256]{1,0:T(8,128)} %bitcast.21, f32[1536,128]{1,0:T(8,128)} %broadcast_in_dim.14.weights), custom_call_target="tpu_custom_call" | custom-call | flops 2415919104 | bytes 11016192 | tf_op jit(solution)/shard_map/pallas_call | solution.py:73
  36.6 4.5 %collective-permute-done.5.refs_15_.refs_7_ = f32[312,128]{1,0:T(8,128)S(1)} collective-permute-done((f32[312,128]{1,0:T(8,128)}, f32[312,128]{1,0:T(8,128)S(1)}, u32[]{:S(2)}, u32[]{:S(2)}) %collective-permute-start.5) | collective-permute-done | bytes 159776 | tf_op jit(solution)/shard_map/ppermute | solution.py:52
  41.8 5.9 %shard_map.97 = (f32[1536,128]{1,0:T(8,128)}, f32[1536,128]{1,0:T(8,128)}, bf16[1536,128]{1,0:T(8,128)(2,1)}, f32[768,128]{1,0:T(8,128)}, f32[8,128]{1,0:T(8,128)}) custom-call(s32[1,6]{1,0:T(1,128)} %refs_0_.13, s32[1,24]{1,0:T(1,128)} %refs_1_.11, bf16[48,1536]{1,0:T(8,128)(2,1)} %get-tuple-element.103.refs_2_.refs_19_.refs_22_, ...), custom_call_target="tpu_custom_call" | custom-call | bytes 5214328 | tf_op jit(solution)/shard_map/pallas_call | solution.py:73
  47.7 5.1 %all-to-all-start = ((f32[32,24,128]{2,1,0:T(8,128)}), f32[32,24,128]{2,1,0:T(8,128)S(1)}, u32[]{:S(2)}, u32[]{:S(2)}) async-start(f32[32,24,128]{2,1,0:T(8,128)} %bitcast.14), calls=%async_computation | async-start | bytes 786432 | tf_op jit(solution)/shard_map/all_to_all | solution.py:395
  54.5 6.5 %shard_map.98 = (f32[256,128]{1,0:T(8,128)}, f32[256,128]{1,0:T(8,128)}, f32[256,128]{1,0:T(8,128)}, f32[256,128]{1,0:T(8,128)}, f32[256,128]{1,0:T(8,128)}, /*i...) custom-call(bf16[1536,1536]{1,0:T(8,128)(2,1)} %get-tuple-element.106.schur, ...), custom_call_target="tpu_custom_call" | custom-call | flops 603979776 | bytes 7479296 | tf_op jit(solution)/shard_map/pallas_call | solution.py:73
  66.8 5.9 %collective-permute-start.9 = (f32[256,128]{1,0:T(8,128)}, f32[256,128]{1,0:T(8,128)S(1)}, u32[]{:S(2)}, u32[]{:S(2)}) collective-permute-start(f32[256,128]{1,0:T(8,128)} %get-tuple-element.118), channel_id=1, source_target_pairs={{16,0},{17,1},{18,2},{19,3},{20,4},{21,5},{22,6},{23,7},{24,8},{25... | collective-permute-start | bytes 393224 | tf_op jit(solution)/shard_map/ppermute | solution.py:52
  72.7 6.1 %collective-permute-start.10 = (f32[256,128]{1,0:T(8,128)}, f32[256,128]{1,0:T(8,128)S(1)}, u32[]{:S(2)}, u32[]{:S(2)}) collective-permute-start(f32[256,128]{1,0:T(8,128)} %get-tuple-element.119), channel_id=1, source_target_pairs={{0,4},{1,5},{2,6},{3,7},{4,8},{5,9},{6,10},{7,11},{8,12},{9,13},{1... | collective-permute-start | bytes 393224 | tf_op jit(solution)/shard_map/ppermute | solution.py:52
  81.9 3.4 all-to-all-start.1
  86.7 4.7 %collective-permute-start.11 = (f32[256,128]{1,0:T(8,128)}, f32[256,128]{1,0:T(8,128)S(1)}, u32[]{:S(2)}, u32[]{:S(2)}) collective-permute-start(f32[256,128]{1,0:T(8,128)} %get-tuple-element.120), channel_id=1, source_target_pairs={{0,16},{1,17},{2,18},{3,19},{4,20},{5,21},{6,22},{7,23},{8,24},{9,... | collective-permute-start | bytes 393224 | tf_op jit(solution)/shard_map/ppermute | solution.py:52
  91.4 3.8 all-to-all-done.1.parts
  97.7 8.1 %all-to-all-start.2 = ((f32[32,32,128]{2,1,0:T(8,128)}), f32[32,32,128]{2,1,0:T(8,128)S(1)}, u32[]{:S(2)}, u32[]{:S(2)}) async-start(f32[32,32,128]{2,1,0:T(8,128)} %shard_map.100), calls=%async_computation.2 | async-start | bytes 1048576 | tf_op jit(solution)/shard_map/all_to_all | solution.py:410
  108.5 4.8 %shard_map.101 = (bf16[1536,256]{1,0:T(8,128)(2,1)}, bf16[1536,256]{1,0:T(8,128)(2,1)}) custom-call(s32[1,6]{1,0:T(1,128)} %refs_0_.13, f32[24,1536]{1,0:T(8,128)} %get-tuple-element.113.refs_1_, f32[312,128]{1,0:T(8,128)} %copy-done.11, f32[312,128]{1,0:T(8,128)} %copy-done.13, f32[312,128]{1,0:T(8,128)} %copy-done.15, f32[312,128]{1,0:T(8,128)} %copy-done.12, ...), custom_call_target="tpu_custom_call" | custom-call | bytes 2678808 | tf_op jit(solution)/shard_map/pallas_call | solution.py:73
  116.1 9.4 %shard_map.102 = (f32[1536,128]{1,0:T(8,128)}, f32[1536,128]{1,0:T(8,128)}, f32[1536,128]{1,0:T(8,128)}, f32[1536,128]{1,0:T(8,128)}, f32[8,128]{1,0:T(8,128)}, ...) custom-call(s32[1,6]{1,0:T(1,128)} %refs_0_.13, s32[1,24]{1,0:T(1,128)} %refs_1_.11, ...), custom_call_target="tpu_custom_call" | custom-call | bytes 13267736 | tf_op jit(solution)/shard_map/pallas_call | solution.py:73
  125.6 6.2 %all-to-all-start.3 = ((f32[32,24,128]{2,1,0:T(8,128)}), f32[32,24,128]{2,1,0:T(8,128)S(1)}, u32[]{:S(2)}, u32[]{:S(2)}) async-start(f32[32,24,128]{2,1,0:T(8,128)} %bitcast.18), calls=%async_computation.3 | async-start | bytes 786432 | tf_op jit(solution)/shard_map/all_to_all | solution.py:395
  131.7 6.5 %shard_map.103 = (f32[256,128]{1,0:T(8,128)}, f32[256,128]{1,0:T(8,128)}, f32[256,128]{1,0:T(8,128)}, f32[256,128]{1,0:T(8,128)}, f32[256,128]{1,0:T(8,128)}, /*...) custom-call(bf16[1536,1536]{1,0:T(8,128)(2,1)} %get-tuple-element.106.schur, ...), custom_call_target="tpu_custom_call" | custom-call | flops 603979776 | bytes 7479296 | tf_op jit(solution)/shard_map/pallas_call | solution.py:73
  151.1 4.4 %all-to-all-done.4.parts = f32[8,32,128]{2,1,0:T(8,128)S(1)} async-done(((f32[8,32,128]{2,1,0:T(8,128)}), f32[8,32,128]{2,1,0:T(8,128)S(1)}, u32[]{:S(2)}, u32[]{:S(2)}) %all-to-all-start.4) | async-done | bytes 131104 | tf_op jit(solution)/shard_map/all_to_all | solution.py:408
  157.9 5.8 %all-to-all-start.5 = ((f32[32,32,128]{2,1,0:T(8,128)}), f32[32,32,128]{2,1,0:T(8,128)S(1)}, u32[]{:S(2)}, u32[]{:S(2)}) async-start(f32[32,32,128]{2,1,0:T(8,128)} %shard_map.105), calls=%async_computation.5 | async-start | bytes 1048576 | tf_op jit(solution)/shard_map/all_to_all | solution.py:410
  165.1 5.9 %collective-permute-start.15 = (f32[256,128]{1,0:T(8,128)S(1)}, f32[256,128]{1,0:T(8,128)S(1)}, u32[]{:S(2)}, u32[]{:S(2)}) collective-permute-start(f32[256,128]{1,0:T(8,128)S(1)} %copy-done.62), channel_id=1, source_target_pairs={{16,0},{17,1},{18,2},{19,3},{20,4},{21,5},{22,6},{23,7},{24,8},{25... | collective-permute-start | bytes 393224 | tf_op jit(solution)/shard_map/ppermute | solution.py:52
  171.0 6.1 %collective-permute-start.16 = (f32[256,128]{1,0:T(8,128)S(1)}, f32[256,128]{1,0:T(8,128)S(1)}, u32[]{:S(2)}, u32[]{:S(2)}) collective-permute-start(f32[256,128]{1,0:T(8,128)S(1)} %copy-done.58), channel_id=1, source_target_pairs={{0,4},{1,5},{2,6},{3,7},{4,8},{5,9},{6,10},{7,11},{8,12},{9,13},{1... | collective-permute-start | bytes 393224 | tf_op jit(solution)/shard_map/ppermute | solution.py:52
  179.5 9.7 %collective-permute-done.17.refs_14_ = f32[256,128]{1,0:T(8,128)S(1)} collective-permute-done((f32[256,128]{1,0:T(8,128)S(1)}, f32[256,128]{1,0:T(8,128)S(1)}, u32[]{:S(2)}, u32[]{:S(2)}) %collective-permute-start.17) | collective-permute-done | bytes 131104 | tf_op jit(solution)/shard_map/ppermute | solution.py:52
  190.1 10.0 %shard_map.106 = (f32[1536,128]{1,0:T(8,128)}, f32[1536,128]{1,0:T(8,128)}, f32[1536,128]{1,0:T(8,128)}, f32[1536,128]{1,0:T(8,128)}, f32[8,128]{1,0:T(8,128)}, ...) custom-call(s32[1,6]{1,0:T(1,128)} %refs_0_.13, s32[1,24]{1,0:T(1,128)} %refs_1_.11, ...), custom_call_target="tpu_custom_call" | custom-call | bytes 15627032 | tf_op jit(solution)/shard_map/pallas_call | solution.py:73
  200.1 6.3 %all-to-all-start.6 = ((f32[32,24,128]{2,1,0:T(8,128)}), f32[32,24,128]{2,1,0:T(8,128)S(1)}, u32[]{:S(2)}, u32[]{:S(2)}) async-start(f32[32,24,128]{2,1,0:T(8,128)} %bitcast.16), calls=%async_computation.6 | async-start | bytes 786432 | tf_op jit(solution)/shard_map/all_to_all | solution.py:395
  206.4 6.5 %shard_map.107 = (f32[256,128]{1,0:T(8,128)}, f32[256,128]{1,0:T(8,128)}, f32[256,128]{1,0:T(8,128)}, f32[256,128]{1,0:T(8,128)}, f32[256,128]{1,0:T(8,128)}, /*...) custom-call(bf16[1536,1536]{1,0:T(8,128)(2,1)} %get-tuple-element.106.schur, ...), custom_call_target="tpu_custom_call" | custom-call | flops 603979776 | bytes 7479296 | tf_op jit(solution)/shard_map/pallas_call | solution.py:73
  216.9 3.5 all-to-all-start.7
  225.9 4.4 %all-to-all-done.7.parts = f32[8,32,128]{2,1,0:T(8,128)S(1)} async-done(((f32[8,32,128]{2,1,0:T(8,128)}), f32[8,32,128]{2,1,0:T(8,128)S(1)}, u32[]{:S(2)}, u32[]{:S(2)}) %all-to-all-start.7) | async-done | bytes 131104 | tf_op jit(solution)/shard_map/all_to_all | solution.py:408
  232.8 5.8 %all-to-all-start.8 = ((f32[32,32,128]{2,1,0:T(8,128)}), f32[32,32,128]{2,1,0:T(8,128)S(1)}, u32[]{:S(2)}, u32[]{:S(2)}) async-start(f32[32,32,128]{2,1,0:T(8,128)} %shard_map.109), calls=%async_computation.8 | async-start | bytes 1048576 | tf_op jit(solution)/shard_map/all_to_all | solution.py:410
  239.9 5.9 %collective-permute-start.21 = (f32[256,128]{1,0:T(8,128)S(1)}, f32[256,128]{1,0:T(8,128)S(1)}, u32[]{:S(2)}, u32[]{:S(2)}) collective-permute-start(f32[256,128]{1,0:T(8,128)S(1)} %copy-done.63), channel_id=1, source_target_pairs={{16,0},{17,1},{18,2},{19,3},{20,4},{21,5},{22,6},{23,7},{24,8},{25... | collective-permute-start | bytes 393224 | tf_op jit(solution)/shard_map/ppermute | solution.py:52
  245.8 6.1 %collective-permute-start.22 = (f32[256,128]{1,0:T(8,128)S(1)}, f32[256,128]{1,0:T(8,128)S(1)}, u32[]{:S(2)}, u32[]{:S(2)}) collective-permute-start(f32[256,128]{1,0:T(8,128)S(1)} %copy-done.59), channel_id=1, source_target_pairs={{0,4},{1,5},{2,6},{3,7},{4,8},{5,9},{6,10},{7,11},{8,12},{9,13},{1... | collective-permute-start | bytes 393224 | tf_op jit(solution)/shard_map/ppermute | solution.py:52
  254.4 9.7 %collective-permute-done.23.refs_14_ = f32[256,128]{1,0:T(8,128)S(1)} collective-permute-done((f32[256,128]{1,0:T(8,128)S(1)}, f32[256,128]{1,0:T(8,128)S(1)}, u32[]{:S(2)}, u32[]{:S(2)}) %collective-permute-start.23) | collective-permute-done | bytes 131104 | tf_op jit(solution)/shard_map/ppermute | solution.py:52
  264.9 10.0 %shard_map.110 = (f32[1536,128]{1,0:T(8,128)}, f32[1536,128]{1,0:T(8,128)}, f32[1536,128]{1,0:T(8,128)}, f32[1536,128]{1,0:T(8,128)}, f32[8,128]{1,0:T(8,128)}, ...) custom-call(s32[1,6]{1,0:T(1,128)} %refs_0_.13, s32[1,24]{1,0:T(1,128)} %refs_1_.11, ...), custom_call_target="tpu_custom_call" | custom-call | bytes 15627032 | tf_op jit(solution)/shard_map/pallas_call | solution.py:73
  274.9 6.3 %all-to-all-start.9 = ((f32[32,24,128]{2,1,0:T(8,128)}), f32[32,24,128]{2,1,0:T(8,128)S(1)}, u32[]{:S(2)}, u32[]{:S(2)}) async-start(f32[32,24,128]{2,1,0:T(8,128)} %bitcast.17), calls=%async_computation.9 | async-start | bytes 786432 | tf_op jit(solution)/shard_map/all_to_all | solution.py:395
  281.2 6.5 %shard_map.111 = (f32[256,128]{1,0:T(8,128)}, f32[256,128]{1,0:T(8,128)}, f32[256,128]{1,0:T(8,128)}, f32[256,128]{1,0:T(8,128)}, f32[256,128]{1,0:T(8,128)}, /*...) custom-call(bf16[1536,1536]{1,0:T(8,128)(2,1)} %get-tuple-element.106.schur, ...), custom_call_target="tpu_custom_call" | custom-call | flops 603979776 | bytes 7479296 | tf_op jit(solution)/shard_map/pallas_call | solution.py:73
  300.6 4.4 %all-to-all-done.10.parts = f32[8,32,128]{2,1,0:T(8,128)S(1)} async-done(((f32[8,32,128]{2,1,0:T(8,128)}), f32[8,32,128]{2,1,0:T(8,128)S(1)}, u32[]{:S(2)}, u32[]{:S(2)}) %all-to-all-start.10) | async-done | bytes 131104 | tf_op jit(solution)/shard_map/all_to_all | solution.py:408
  307.4 5.8 %all-to-all-start.11 = ((f32[32,32,128]{2,1,0:T(8,128)}), f32[32,32,128]{2,1,0:T(8,128)S(1)}, u32[]{:S(2)}, u32[]{:S(2)}) async-start(f32[32,32,128]{2,1,0:T(8,128)} %shard_map.113), calls=%async_computation.11 | async-start | bytes 1048576 | tf_op jit(solution)/shard_map/all_to_all | solution.py:410
  314.5 5.9 %collective-permute-start.27 = (f32[256,128]{1,0:T(8,128)S(1)}, f32[256,128]{1,0:T(8,128)S(1)}, u32[]{:S(2)}, u32[]{:S(2)}) collective-permute-start(f32[256,128]{1,0:T(8,128)S(1)} %copy-done.64), channel_id=1, source_target_pairs={{16,0},{17,1},{18,2},{19,3},{20,4},{21,5},{22,6},{23,7},{24,8},{25... | collective-permute-start | bytes 393224 | tf_op jit(solution)/shard_map/ppermute | solution.py:52
  320.5 6.1 %collective-permute-start.28 = (f32[256,128]{1,0:T(8,128)S(1)}, f32[256,128]{1,0:T(8,128)S(1)}, u32[]{:S(2)}, u32[]{:S(2)}) collective-permute-start(f32[256,128]{1,0:T(8,128)S(1)} %copy-done.60), channel_id=1, source_target_pairs={{0,4},{1,5},{2,6},{3,7},{4,8},{5,9},{6,10},{7,11},{8,12},{9,13},{1... | collective-permute-start | bytes 393224 | tf_op jit(solution)/shard_map/ppermute | solution.py:52
  329.0 9.7 %collective-permute-done.29.refs_14_ = f32[256,128]{1,0:T(8,128)S(1)} collective-permute-done((f32[256,128]{1,0:T(8,128)S(1)}, f32[256,128]{1,0:T(8,128)S(1)}, u32[]{:S(2)}, u32[]{:S(2)}) %collective-permute-start.29) | collective-permute-done | bytes 131104 | tf_op jit(solution)/shard_map/ppermute | solution.py:52
  339.5 10.1 %shard_map.114 = (f32[1536,128]{1,0:T(8,128)}, f32[1536,128]{1,0:T(8,128)}, f32[1536,128]{1,0:T(8,128)}, f32[1536,128]{1,0:T(8,128)}, f32[8,128]{1,0:T(8,128)}, ...) custom-call(s32[1,6]{1,0:T(1,128)} %refs_0_.13, s32[1,24]{1,0:T(1,128)} %refs_1_.11, ...), custom_call_target="tpu_custom_call" | custom-call | bytes 15627032 | tf_op jit(solution)/shard_map/pallas_call | solution.py:73
  349.6 6.3 %all-to-all-start.12 = ((f32[32,24,128]{2,1,0:T(8,128)}), f32[32,24,128]{2,1,0:T(8,128)S(1)}, u32[]{:S(2)}, u32[]{:S(2)}) async-start(f32[32,24,128]{2,1,0:T(8,128)} %bitcast.15), calls=%async_computation.12 | async-start | bytes 786432 | tf_op jit(solution)/shard_map/all_to_all | solution.py:395
  355.9 6.5 %shard_map.115 = (f32[256,128]{1,0:T(8,128)}, f32[256,128]{1,0:T(8,128)}, f32[256,128]{1,0:T(8,128)}, f32[256,128]{1,0:T(8,128)}, f32[256,128]{1,0:T(8,128)}, /*...) custom-call(bf16[1536,1536]{1,0:T(8,128)(2,1)} %get-tuple-element.106.schur, ...), custom_call_target="tpu_custom_call" | custom-call | flops 603979776 | bytes 7479296 | tf_op jit(solution)/shard_map/pallas_call | solution.py:73
  375.3 4.4 %all-to-all-done.13.parts = f32[8,32,128]{2,1,0:T(8,128)S(1)} async-done(((f32[8,32,128]{2,1,0:T(8,128)}), f32[8,32,128]{2,1,0:T(8,128)S(1)}, u32[]{:S(2)}, u32[]{:S(2)}) %all-to-all-start.13) | async-done | bytes 131104 | tf_op jit(solution)/shard_map/all_to_all | solution.py:408
  382.1 5.8 %all-to-all-start.14 = ((f32[32,32,128]{2,1,0:T(8,128)}), f32[32,32,128]{2,1,0:T(8,128)S(1)}, u32[]{:S(2)}, u32[]{:S(2)}) async-start(f32[32,32,128]{2,1,0:T(8,128)} %shard_map.117), calls=%async_computation.14 | async-start | bytes 1048576 | tf_op jit(solution)/shard_map/all_to_all | solution.py:410
  389.2 5.9 %collective-permute-start.33 = (f32[256,128]{1,0:T(8,128)S(1)}, f32[256,128]{1,0:T(8,128)S(1)}, u32[]{:S(2)}, u32[]{:S(2)}) collective-permute-start(f32[256,128]{1,0:T(8,128)S(1)} %copy-done.61), channel_id=1, source_target_pairs={{16,0},{17,1},{18,2},{19,3},{20,4},{21,5},{22,6},{23,7},{24,8},{25... | collective-permute-start | bytes 393224 | tf_op jit(solution)/shard_map/ppermute | solution.py:52
  395.1 6.1 %collective-permute-start.34 = (f32[256,128]{1,0:T(8,128)S(1)}, f32[256,128]{1,0:T(8,128)S(1)}, u32[]{:S(2)}, u32[]{:S(2)}) collective-permute-start(f32[256,128]{1,0:T(8,128)S(1)} %copy-done.57), channel_id=1, source_target_pairs={{0,4},{1,5},{2,6},{3,7},{4,8},{5,9},{6,10},{7,11},{8,12},{9,13},{1... | collective-permute-start | bytes 393224 | tf_op jit(solution)/shard_map/ppermute | solution.py:52
  403.7 9.7 %collective-permute-done.35.refs_14_ = f32[256,128]{1,0:T(8,128)S(1)} collective-permute-done((f32[256,128]{1,0:T(8,128)S(1)}, f32[256,128]{1,0:T(8,128)S(1)}, u32[]{:S(2)}, u32[]{:S(2)}) %collective-permute-start.35) | collective-permute-done | bytes 131104 | tf_op jit(solution)/shard_map/ppermute | solution.py:52
  414.2 9.4 %shard_map.118 = (f32[1536,128]{1,0:T(8,128)}, f32[1536,128]{1,0:T(8,128)}) custom-call(s32[1,6]{1,0:T(1,128)} %refs_0_.13, s32[1,24]{1,0:T(1,128)} %refs_1_.11, s32[1,168]{1,0:T(1,128)} %concatenate.3.refs_2_, f32[32,32,128]{2,1,0:T(8,128)} %copy-done.5, bf16[768,768]{1,0:T(8,128)(2,1)} %get-tuple-element.193.refs_4_, ...), custom_call_target="tpu_custom_call" | custom-call | bytes 12331800 | tf_op jit(solution)/shard_map/pallas_call | solution.py:73
  (229 shorter events, 110.9 us)
Async XLA Ops:
  5.9 20.8 %collective-permute-start = (f32[312,128]{1,0:T(8,128)}, f32[312,128]{1,0:T(8,128)S(1)}, u32[]{:S(2)}, u32[]{:S(2)}) collective-permute-start(f32[312,128]{1,0:T(8,128)} %get-tuple-element.97.refs_5_), channel_id=1, source_target_pairs={{1,0},{2,1},{3,2},{5,4},{6,5},{7,6},{9,8},{10,9},{11,10},{13,12},{... | collective-permute-start | bytes 479240 | tf_op jit(solution)/shard_map/ppermute | solution.py:52
  7.2 29.3 %collective-permute-start.1 = (f32[312,128]{1,0:T(8,128)}, f32[312,128]{1,0:T(8,128)S(1)}, u32[]{:S(2)}, u32[]{:S(2)}) collective-permute-start(f32[312,128]{1,0:T(8,128)} %get-tuple-element.98.refs_4_), channel_id=1, source_target_pairs={{0,1},{1,2},{2,3},{4,5},{5,6},{6,7},{8,9},{9,10},{10,11},{12,13},{... | collective-permute-start | bytes 479240 | tf_op jit(solution)/shard_map/ppermute | solution.py:52
  10.3 26.3 %collective-permute-start.2 = (f32[312,128]{1,0:T(8,128)}, f32[312,128]{1,0:T(8,128)S(1)}, u32[]{:S(2)}, u32[]{:S(2)}) collective-permute-start(f32[312,128]{1,0:T(8,128)} %get-tuple-element.99.refs_7_), channel_id=1, source_target_pairs={{4,0},{5,1},{6,2},{7,3},{8,4},{9,5},{10,6},{11,7},{12,8},{13,9},{1... | collective-permute-start | bytes 479240 | tf_op jit(solution)/shard_map/ppermute | solution.py:52
  11.6 25.0 %collective-permute-start.3 = (f32[312,128]{1,0:T(8,128)}, f32[312,128]{1,0:T(8,128)S(1)}, u32[]{:S(2)}, u32[]{:S(2)}) collective-permute-start(f32[312,128]{1,0:T(8,128)} %get-tuple-element.100.refs_6_), channel_id=1, source_target_pairs={{0,4},{1,5},{2,6},{3,7},{4,8},{5,9},{6,10},{7,11},{8,12},{9,13},{1... | collective-permute-start | bytes 479240 | tf_op jit(solution)/shard_map/ppermute | solution.py:52
  17.6 19.0 %collective-permute-start.4 = (f32[312,128]{1,0:T(8,128)}, f32[312,128]{1,0:T(8,128)S(1)}, u32[]{:S(2)}, u32[]{:S(2)}) collective-permute-start(f32[312,128]{1,0:T(8,128)} %get-tuple-element.101.refs_9_), channel_id=1, source_target_pairs={{16,0},{17,1},{18,2},{19,3},{20,4},{21,5},{22,6},{23,7},{24,8},{25... | collective-permute-start | bytes 479240 | tf_op jit(solution)/shard_map/ppermute | solution.py:52
  26.8 14.4 %collective-permute-start.5 = (f32[312,128]{1,0:T(8,128)}, f32[312,128]{1,0:T(8,128)S(1)}, u32[]{:S(2)}, u32[]{:S(2)}) collective-permute-start(f32[312,128]{1,0:T(8,128)} %get-tuple-element.102.refs_8_), channel_id=1, source_target_pairs={{0,16},{1,17},{2,18},{3,19},{4,20},{5,21},{6,22},{7,23},{8,24},{9,... | collective-permute-start | bytes 479240 | tf_op jit(solution)/shard_map/ppermute | solution.py:52
  47.7 31.8 %all-to-all-start = ((f32[32,24,128]{2,1,0:T(8,128)}), f32[32,24,128]{2,1,0:T(8,128)S(1)}, u32[]{:S(2)}, u32[]{:S(2)}) async-start(f32[32,24,128]{2,1,0:T(8,128)} %bitcast.14), calls=%async_computation | async-start | bytes 786432 | tf_op jit(solution)/shard_map/all_to_all | solution.py:395
  61.0 25.6 %collective-permute-start.6 = (f32[256,128]{1,0:T(8,128)}, f32[256,128]{1,0:T(8,128)S(1)}, u32[]{:S(2)}, u32[]{:S(2)}) collective-permute-start(f32[256,128]{1,0:T(8,128)} %get-tuple-element.111), channel_id=1, source_target_pairs={{1,0},{2,1},{3,2},{5,4},{6,5},{7,6},{9,8},{10,9},{11,10},{13,12},{... | collective-permute-start | bytes 393224 | tf_op jit(solution)/shard_map/ppermute | solution.py:52
  62.5 28.9 %collective-permute-start.7 = (f32[256,128]{1,0:T(8,128)}, f32[256,128]{1,0:T(8,128)S(1)}, u32[]{:S(2)}, u32[]{:S(2)}) collective-permute-start(f32[256,128]{1,0:T(8,128)} %get-tuple-element.112), channel_id=1, source_target_pairs={{0,1},{1,2},{2,3},{4,5},{5,6},{6,7},{8,9},{9,10},{10,11},{12,13},{... | collective-permute-start | bytes 393224 | tf_op jit(solution)/shard_map/ppermute | solution.py:52
  65.5 47.8 %collective-permute-start.8 = (f32[256,128]{1,0:T(8,128)}, f32[256,128]{1,0:T(8,128)S(1)}, u32[]{:S(2)}, u32[]{:S(2)}) collective-permute-start(f32[256,128]{1,0:T(8,128)} %get-tuple-element.117), channel_id=1, source_target_pairs={{4,0},{5,1},{6,2},{7,3},{8,4},{9,5},{10,6},{11,7},{12,8},{13,9},{1... | collective-permute-start | bytes 393224 | tf_op jit(solution)/shard_map/ppermute | solution.py:52
  66.8 46.5 %collective-permute-start.9 = (f32[256,128]{1,0:T(8,128)}, f32[256,128]{1,0:T(8,128)S(1)}, u32[]{:S(2)}, u32[]{:S(2)}) collective-permute-start(f32[256,128]{1,0:T(8,128)} %get-tuple-element.118), channel_id=1, source_target_pairs={{16,0},{17,1},{18,2},{19,3},{20,4},{21,5},{22,6},{23,7},{24,8},{25... | collective-permute-start | bytes 393224 | tf_op jit(solution)/shard_map/ppermute | solution.py:52
  72.7 40.6 %collective-permute-start.10 = (f32[256,128]{1,0:T(8,128)}, f32[256,128]{1,0:T(8,128)S(1)}, u32[]{:S(2)}, u32[]{:S(2)}) collective-permute-start(f32[256,128]{1,0:T(8,128)} %get-tuple-element.119), channel_id=1, source_target_pairs={{0,4},{1,5},{2,6},{3,7},{4,8},{5,9},{6,10},{7,11},{8,12},{9,13},{1... | collective-permute-start | bytes 393224 | tf_op jit(solution)/shard_map/ppermute | solution.py:52
  81.9 13.3 %all-to-all-start.1 = ((f32[8,32,128]{2,1,0:T(8,128)}), f32[8,32,128]{2,1,0:T(8,128)S(1)}, u32[]{:S(2)}, u32[]{:S(2)}) async-start(f32[8,32,128]{2,1,0:T(8,128)} %shard_map.99), calls=%async_computation.1 | async-start | bytes 262144 | tf_op jit(solution)/shard_map/all_to_all | solution.py:408
  86.7 26.7 %collective-permute-start.11 = (f32[256,128]{1,0:T(8,128)}, f32[256,128]{1,0:T(8,128)S(1)}, u32[]{:S(2)}, u32[]{:S(2)}) collective-permute-start(f32[256,128]{1,0:T(8,128)} %get-tuple-element.120), channel_id=1, source_target_pairs={{0,16},{1,17},{2,18},{3,19},{4,20},{5,21},{6,22},{7,23},{8,24},{9,... | collective-permute-start | bytes 393224 | tf_op jit(solution)/shard_map/ppermute | solution.py:52
  97.7 17.6 %all-to-all-start.2 = ((f32[32,32,128]{2,1,0:T(8,128)}), f32[32,32,128]{2,1,0:T(8,128)S(1)}, u32[]{:S(2)}, u32[]{:S(2)}) async-start(f32[32,32,128]{2,1,0:T(8,128)} %shard_map.100), calls=%async_computation.2 | async-start | bytes 1048576 | tf_op jit(solution)/shard_map/all_to_all | solution.py:410
  125.6 14.3 %all-to-all-start.3 = ((f32[32,24,128]{2,1,0:T(8,128)}), f32[32,24,128]{2,1,0:T(8,128)S(1)}, u32[]{:S(2)}, u32[]{:S(2)}) async-start(f32[32,24,128]{2,1,0:T(8,128)} %bitcast.18), calls=%async_computation.3 | async-start | bytes 786432 | tf_op jit(solution)/shard_map/all_to_all | solution.py:395
  142.2 13.2 %all-to-all-start.4 = ((f32[8,32,128]{2,1,0:T(8,128)}), f32[8,32,128]{2,1,0:T(8,128)S(1)}, u32[]{:S(2)}, u32[]{:S(2)}) async-start(f32[8,32,128]{2,1,0:T(8,128)} %shard_map.104), calls=%async_computation.4 | async-start | bytes 262144 | tf_op jit(solution)/shard_map/all_to_all | solution.py:408
  145.6 4.3 %collective-permute-start.12 = (f32[256,128]{1,0:T(8,128)}, f32[256,128]{1,0:T(8,128)S(1)}, u32[]{:S(2)}, u32[]{:S(2)}) collective-permute-start(f32[256,128]{1,0:T(8,128)} %get-tuple-element.127), channel_id=1, source_target_pairs={{1,0},{2,1},{3,2},{5,4},{6,5},{7,6},{9,8},{10,9},{11,10},{13,12},{... | collective-permute-start | bytes 393224 | tf_op jit(solution)/shard_map/ppermute | solution.py:52
  146.9 4.2 collective-permute-start.13
  157.9 31.3 %all-to-all-start.5 = ((f32[32,32,128]{2,1,0:T(8,128)}), f32[32,32,128]{2,1,0:T(8,128)S(1)}, u32[]{:S(2)}, u32[]{:S(2)}) async-start(f32[32,32,128]{2,1,0:T(8,128)} %shard_map.105), calls=%async_computation.5 | async-start | bytes 1048576 | tf_op jit(solution)/shard_map/all_to_all | solution.py:410
  163.7 15.2 %collective-permute-start.14 = (f32[256,128]{1,0:T(8,128)S(1)}, f32[256,128]{1,0:T(8,128)S(1)}, u32[]{:S(2)}, u32[]{:S(2)}) collective-permute-start(f32[256,128]{1,0:T(8,128)S(1)} %copy-done.66), channel_id=1, source_target_pairs={{4,0},{5,1},{6,2},{7,3},{8,4},{9,5},{10,6},{11,7},{12,8},{13,9},{1... | collective-permute-start | bytes 393224 | tf_op jit(solution)/shard_map/ppermute | solution.py:52
  165.1 14.0 %collective-permute-start.15 = (f32[256,128]{1,0:T(8,128)S(1)}, f32[256,128]{1,0:T(8,128)S(1)}, u32[]{:S(2)}, u32[]{:S(2)}) collective-permute-start(f32[256,128]{1,0:T(8,128)S(1)} %copy-done.62), channel_id=1, source_target_pairs={{16,0},{17,1},{18,2},{19,3},{20,4},{21,5},{22,6},{23,7},{24,8},{25... | collective-permute-start | bytes 393224 | tf_op jit(solution)/shard_map/ppermute | solution.py:52
  171.0 8.6 %collective-permute-start.16 = (f32[256,128]{1,0:T(8,128)S(1)}, f32[256,128]{1,0:T(8,128)S(1)}, u32[]{:S(2)}, u32[]{:S(2)}) collective-permute-start(f32[256,128]{1,0:T(8,128)S(1)} %copy-done.58), channel_id=1, source_target_pairs={{0,4},{1,5},{2,6},{3,7},{4,8},{5,9},{6,10},{7,11},{8,12},{9,13},{1... | collective-permute-start | bytes 393224 | tf_op jit(solution)/shard_map/ppermute | solution.py:52
  177.1 12.2 %collective-permute-start.17 = (f32[256,128]{1,0:T(8,128)S(1)}, f32[256,128]{1,0:T(8,128)S(1)}, u32[]{:S(2)}, u32[]{:S(2)}) collective-permute-start(f32[256,128]{1,0:T(8,128)S(1)} %copy-done.54), channel_id=1, source_target_pairs={{0,16},{1,17},{2,18},{3,19},{4,20},{5,21},{6,22},{7,23},{8,24},{9,... | collective-permute-start | bytes 393224 | tf_op jit(solution)/shard_map/ppermute | solution.py:52
  200.1 14.4 %all-to-all-start.6 = ((f32[32,24,128]{2,1,0:T(8,128)}), f32[32,24,128]{2,1,0:T(8,128)S(1)}, u32[]{:S(2)}, u32[]{:S(2)}) async-start(f32[32,24,128]{2,1,0:T(8,128)} %bitcast.16), calls=%async_computation.6 | async-start | bytes 786432 | tf_op jit(solution)/shard_map/all_to_all | solution.py:395
  216.9 13.5 %all-to-all-start.7 = ((f32[8,32,128]{2,1,0:T(8,128)}), f32[8,32,128]{2,1,0:T(8,128)S(1)}, u32[]{:S(2)}, u32[]{:S(2)}) async-start(f32[8,32,128]{2,1,0:T(8,128)} %shard_map.108), calls=%async_computation.7 | async-start | bytes 262144 | tf_op jit(solution)/shard_map/all_to_all | solution.py:408
  220.4 4.3 %collective-permute-start.18 = (f32[256,128]{1,0:T(8,128)}, f32[256,128]{1,0:T(8,128)S(1)}, u32[]{:S(2)}, u32[]{:S(2)}) collective-permute-start(f32[256,128]{1,0:T(8,128)} %get-tuple-element.144), channel_id=1, source_target_pairs={{1,0},{2,1},{3,2},{5,4},{6,5},{7,6},{9,8},{10,9},{11,10},{13,12},{... | collective-permute-start | bytes 393224 | tf_op jit(solution)/shard_map/ppermute | solution.py:52
  232.8 31.3 %all-to-all-start.8 = ((f32[32,32,128]{2,1,0:T(8,128)}), f32[32,32,128]{2,1,0:T(8,128)S(1)}, u32[]{:S(2)}, u32[]{:S(2)}) async-start(f32[32,32,128]{2,1,0:T(8,128)} %shard_map.109), calls=%async_computation.8 | async-start | bytes 1048576 | tf_op jit(solution)/shard_map/all_to_all | solution.py:410
  238.6 15.2 %collective-permute-start.20 = (f32[256,128]{1,0:T(8,128)S(1)}, f32[256,128]{1,0:T(8,128)S(1)}, u32[]{:S(2)}, u32[]{:S(2)}) collective-permute-start(f32[256,128]{1,0:T(8,128)S(1)} %copy-done.67), channel_id=1, source_target_pairs={{4,0},{5,1},{6,2},{7,3},{8,4},{9,5},{10,6},{11,7},{12,8},{13,9},{1... | collective-permute-start | bytes 393224 | tf_op jit(solution)/shard_map/ppermute | solution.py:52
  239.9 14.0 %collective-permute-start.21 = (f32[256,128]{1,0:T(8,128)S(1)}, f32[256,128]{1,0:T(8,128)S(1)}, u32[]{:S(2)}, u32[]{:S(2)}) collective-permute-start(f32[256,128]{1,0:T(8,128)S(1)} %copy-done.63), channel_id=1, source_target_pairs={{16,0},{17,1},{18,2},{19,3},{20,4},{21,5},{22,6},{23,7},{24,8},{25... | collective-permute-start | bytes 393224 | tf_op jit(solution)/shard_map/ppermute | solution.py:52
  245.8 8.6 %collective-permute-start.22 = (f32[256,128]{1,0:T(8,128)S(1)}, f32[256,128]{1,0:T(8,128)S(1)}, u32[]{:S(2)}, u32[]{:S(2)}) collective-permute-start(f32[256,128]{1,0:T(8,128)S(1)} %copy-done.59), channel_id=1, source_target_pairs={{0,4},{1,5},{2,6},{3,7},{4,8},{5,9},{6,10},{7,11},{8,12},{9,13},{1... | collective-permute-start | bytes 393224 | tf_op jit(solution)/shard_map/ppermute | solution.py:52
  251.9 12.2 %collective-permute-start.23 = (f32[256,128]{1,0:T(8,128)S(1)}, f32[256,128]{1,0:T(8,128)S(1)}, u32[]{:S(2)}, u32[]{:S(2)}) collective-permute-start(f32[256,128]{1,0:T(8,128)S(1)} %copy-done.55), channel_id=1, source_target_pairs={{0,16},{1,17},{2,18},{3,19},{4,20},{5,21},{6,22},{7,23},{8,24},{9,... | collective-permute-start | bytes 393224 | tf_op jit(solution)/shard_map/ppermute | solution.py:52
  274.9 14.4 %all-to-all-start.9 = ((f32[32,24,128]{2,1,0:T(8,128)}), f32[32,24,128]{2,1,0:T(8,128)S(1)}, u32[]{:S(2)}, u32[]{:S(2)}) async-start(f32[32,24,128]{2,1,0:T(8,128)} %bitcast.17), calls=%async_computation.9 | async-start | bytes 786432 | tf_op jit(solution)/shard_map/all_to_all | solution.py:395
  291.7 13.3 %all-to-all-start.10 = ((f32[8,32,128]{2,1,0:T(8,128)}), f32[8,32,128]{2,1,0:T(8,128)S(1)}, u32[]{:S(2)}, u32[]{:S(2)}) async-start(f32[8,32,128]{2,1,0:T(8,128)} %shard_map.112), calls=%async_computation.10 | async-start | bytes 262144 | tf_op jit(solution)/shard_map/all_to_all | solution.py:408
  295.1 4.3 %collective-permute-start.24 = (f32[256,128]{1,0:T(8,128)}, f32[256,128]{1,0:T(8,128)S(1)}, u32[]{:S(2)}, u32[]{:S(2)}) collective-permute-start(f32[256,128]{1,0:T(8,128)} %get-tuple-element.161), channel_id=1, source_target_pairs={{1,0},{2,1},{3,2},{5,4},{6,5},{7,6},{9,8},{10,9},{11,10},{13,12},{... | collective-permute-start | bytes 393224 | tf_op jit(solution)/shard_map/ppermute | solution.py:52
  307.4 31.3 %all-to-all-start.11 = ((f32[32,32,128]{2,1,0:T(8,128)}), f32[32,32,128]{2,1,0:T(8,128)S(1)}, u32[]{:S(2)}, u32[]{:S(2)}) async-start(f32[32,32,128]{2,1,0:T(8,128)} %shard_map.113), calls=%async_computation.11 | async-start | bytes 1048576 | tf_op jit(solution)/shard_map/all_to_all | solution.py:410
  313.2 15.3 %collective-permute-start.26 = (f32[256,128]{1,0:T(8,128)S(1)}, f32[256,128]{1,0:T(8,128)S(1)}, u32[]{:S(2)}, u32[]{:S(2)}) collective-permute-start(f32[256,128]{1,0:T(8,128)S(1)} %copy-done.68), channel_id=1, source_target_pairs={{4,0},{5,1},{6,2},{7,3},{8,4},{9,5},{10,6},{11,7},{12,8},{13,9},{1... | collective-permute-start | bytes 393224 | tf_op jit(solution)/shard_map/ppermute | solution.py:52
  314.5 14.0 %collective-permute-start.27 = (f32[256,128]{1,0:T(8,128)S(1)}, f32[256,128]{1,0:T(8,128)S(1)}, u32[]{:S(2)}, u32[]{:S(2)}) collective-permute-start(f32[256,128]{1,0:T(8,128)S(1)} %copy-done.64), channel_id=1, source_target_pairs={{16,0},{17,1},{18,2},{19,3},{20,4},{21,5},{22,6},{23,7},{24,8},{25... | collective-permute-start | bytes 393224 | tf_op jit(solution)/shard_map/ppermute | solution.py:52
  320.5 8.6 %collective-permute-start.28 = (f32[256,128]{1,0:T(8,128)S(1)}, f32[256,128]{1,0:T(8,128)S(1)}, u32[]{:S(2)}, u32[]{:S(2)}) collective-permute-start(f32[256,128]{1,0:T(8,128)S(1)} %copy-done.60), channel_id=1, source_target_pairs={{0,4},{1,5},{2,6},{3,7},{4,8},{5,9},{6,10},{7,11},{8,12},{9,13},{1... | collective-permute-start | bytes 393224 | tf_op jit(solution)/shard_map/ppermute | solution.py:52
  326.5 12.2 %collective-permute-start.29 = (f32[256,128]{1,0:T(8,128)S(1)}, f32[256,128]{1,0:T(8,128)S(1)}, u32[]{:S(2)}, u32[]{:S(2)}) collective-permute-start(f32[256,128]{1,0:T(8,128)S(1)} %copy-done.56), channel_id=1, source_target_pairs={{0,16},{1,17},{2,18},{3,19},{4,20},{5,21},{6,22},{7,23},{8,24},{9,... | collective-permute-start | bytes 393224 | tf_op jit(solution)/shard_map/ppermute | solution.py:52
  349.6 14.4 %all-to-all-start.12 = ((f32[32,24,128]{2,1,0:T(8,128)}), f32[32,24,128]{2,1,0:T(8,128)S(1)}, u32[]{:S(2)}, u32[]{:S(2)}) async-start(f32[32,24,128]{2,1,0:T(8,128)} %bitcast.15), calls=%async_computation.12 | async-start | bytes 786432 | tf_op jit(solution)/shard_map/all_to_all | solution.py:395
  366.4 13.3 %all-to-all-start.13 = ((f32[8,32,128]{2,1,0:T(8,128)}), f32[8,32,128]{2,1,0:T(8,128)S(1)}, u32[]{:S(2)}, u32[]{:S(2)}) async-start(f32[8,32,128]{2,1,0:T(8,128)} %shard_map.116), calls=%async_computation.13 | async-start | bytes 262144 | tf_op jit(solution)/shard_map/all_to_all | solution.py:408
  369.8 4.3 %collective-permute-start.30 = (f32[256,128]{1,0:T(8,128)}, f32[256,128]{1,0:T(8,128)S(1)}, u32[]{:S(2)}, u32[]{:S(2)}) collective-permute-start(f32[256,128]{1,0:T(8,128)} %get-tuple-element.178), channel_id=1, source_target_pairs={{1,0},{2,1},{3,2},{5,4},{6,5},{7,6},{9,8},{10,9},{11,10},{13,12},{... | collective-permute-start | bytes 393224 | tf_op jit(solution)/shard_map/ppermute | solution.py:52
  382.1 31.3 %all-to-all-start.14 = ((f32[32,32,128]{2,1,0:T(8,128)}), f32[32,32,128]{2,1,0:T(8,128)S(1)}, u32[]{:S(2)}, u32[]{:S(2)}) async-start(f32[32,32,128]{2,1,0:T(8,128)} %shard_map.117), calls=%async_computation.14 | async-start | bytes 1048576 | tf_op jit(solution)/shard_map/all_to_all | solution.py:410
  387.9 15.2 %collective-permute-start.32 = (f32[256,128]{1,0:T(8,128)S(1)}, f32[256,128]{1,0:T(8,128)S(1)}, u32[]{:S(2)}, u32[]{:S(2)}) collective-permute-start(f32[256,128]{1,0:T(8,128)S(1)} %copy-done.65), channel_id=1, source_target_pairs={{4,0},{5,1},{6,2},{7,3},{8,4},{9,5},{10,6},{11,7},{12,8},{13,9},{1... | collective-permute-start | bytes 393224 | tf_op jit(solution)/shard_map/ppermute | solution.py:52
  389.2 13.9 %collective-permute-start.33 = (f32[256,128]{1,0:T(8,128)S(1)}, f32[256,128]{1,0:T(8,128)S(1)}, u32[]{:S(2)}, u32[]{:S(2)}) collective-permute-start(f32[256,128]{1,0:T(8,128)S(1)} %copy-done.61), channel_id=1, source_target_pairs={{16,0},{17,1},{18,2},{19,3},{20,4},{21,5},{22,6},{23,7},{24,8},{25... | collective-permute-start | bytes 393224 | tf_op jit(solution)/shard_map/ppermute | solution.py:52
  395.1 8.6 %collective-permute-start.34 = (f32[256,128]{1,0:T(8,128)S(1)}, f32[256,128]{1,0:T(8,128)S(1)}, u32[]{:S(2)}, u32[]{:S(2)}) collective-permute-start(f32[256,128]{1,0:T(8,128)S(1)} %copy-done.57), channel_id=1, source_target_pairs={{0,4},{1,5},{2,6},{3,7},{4,8},{5,9},{6,10},{7,11},{8,12},{9,13},{1... | collective-permute-start | bytes 393224 | tf_op jit(solution)/shard_map/ppermute | solution.py:52
  401.2 12.2 %collective-permute-start.35 = (f32[256,128]{1,0:T(8,128)S(1)}, f32[256,128]{1,0:T(8,128)S(1)}, u32[]{:S(2)}, u32[]{:S(2)}) collective-permute-start(f32[256,128]{1,0:T(8,128)S(1)} %copy-done.53), channel_id=1, source_target_pairs={{0,16},{1,17},{2,18},{3,19},{4,20},{5,21},{6,22},{7,23},{8,24},{9,... | collective-permute-start | bytes 393224 | tf_op jit(solution)/shard_map/ppermute | solution.py:52
  (72 other events, 794.2 us)
